TPU v7x, 768 devices: a whole 4x8x12 slice. The times are simulated.
768 devices in a mesh: section: 12 (over z), tensor: 16 (over y, core), dp: 4 (over x).
Axes of the slice: x: 4, y: 8, z: 12, core: 2. Of those that a mesh axis runs over, the one named last changes fastest.
Arguments:
- frame_query: bfloat16 [12, 4, 1280, 16], P('section', 'dp', 'tensor'), may hold values from -108 to 108
- frame_key: bfloat16 [12, 4, 1280, 16], P('section', 'dp', 'tensor'), may hold values from -4.5 to 4.5
- frame_value: bfloat16 [12, 4, 1280, 16], P('section', 'dp', 'tensor'), may hold values from -6 to 6
- frame_segment: int32 [12, 4, 16], P('section', 'dp'), may hold values from 0 to 1, never falling along the last dimension, each value on 1 to 12 neighbouring positions
- past_query: bfloat16 [12, 4, 1280, 16], P('section', 'dp', 'tensor'), may hold values from -108 to 108
- past_key: bfloat16 [12, 4, 1280, 16], P('section', 'dp', 'tensor'), may hold values from -4.5 to 4.5
- past_value: bfloat16 [12, 4, 1280, 16], P('section', 'dp', 'tensor'), may hold values from -6 to 6
- past_segment: int32 [12, 4, 16], P('section', 'dp'), may hold values from 0 to 1, never falling along the last dimension, each value on 1 to 12 neighbouring positions
- visual_slot: int32 [4, 192], P('dp'), may hold values from 0 to 191, as said below
- past_slot: int32 [4, 192], P('dp'), may hold values from 0 to 191, as said below
- visual_proj: bfloat16 [1280, 8192], P('tensor'), may hold values from -0.15625 to 0.15625
- layer_weight: bfloat16 [12, 8192, 8192], P('section', 'tensor'), may hold values from -0.0625 to 0.0625
- layer_input: bfloat16 [12, 8192, 768], P('section', 'tensor', 'dp'), may hold values from -6 to 6
- saved_preact: bfloat16 [12, 8192, 768], P('section', 'tensor', 'dp'), may hold values from -8 to 8
- layer_cotangent: bfloat16 [12, 8192, 768], P('section', 'tensor', 'dp'), may hold values from -6 to 6
Outputs:
- forward_out: bfloat16 [12, 8192, 768], P('section', 'tensor', 'dp')
- backward_out: bfloat16 [12, 8192, 768], P('section', 'tensor', 'dp')
- grad_proj: bfloat16 [1280, 8192], P('tensor')
- grad_frames: float32 [3, 12, 4, 1280, 16], P(None, 'section', 'dp', 'tensor')
Inputs may be any that keep to these rules, and one draw needn't show every extreme that they name: `visual_slot`: within one replica the 192 positions are distinct. `past_slot`: within one replica the 192 positions are distinct.
All inputs are finite; a program needn't handle non-finite values.
Results may differ from a plain program's by a relative error of at most 0.02.
Values may be sent and summed in bfloat16 or wider, within the bound.
No kernel may reach another device: no remote copies, remote signals or barrier semaphores. Data moves between devices by JAX's collectives and lax.ppermute only.
A program may use at most 64 MiB of HBM per device.

v0:
```python
import jax
import jax.numpy as jnp
from jax import lax
from jax.sharding import PartitionSpec as P

HEAD_DIM = 80


SCORE_FLOOR = -1e30


def from_behind(value, axis, steps):
    count = lax.axis_size(axis)
    first, last = (max(0, -steps), min(count, count - steps))
    return lax.ppermute(value, axis, [(source, source + steps) for source in range(first, last)])


def attend_parts(query_rows, key_rows, value_rows, segment):
    head_count = query_rows.shape[0] // HEAD_DIM
    row_total = query_rows.shape[1]
    query_heads = query_rows.reshape(head_count, HEAD_DIM, row_total)
    key_heads = key_rows.reshape(head_count, HEAD_DIM, row_total)
    value_heads = value_rows.reshape(head_count, HEAD_DIM, row_total)
    scores = jnp.einsum(
        "hci,hcj->hij", query_heads, key_heads, preferred_element_type=jnp.float32
    ) * HEAD_DIM ** (-0.5)
    same_sample = segment[:, None] == segment[None, :]
    scores = jnp.where(same_sample[None], scores, SCORE_FLOOR)
    row_peak = jnp.max(scores, axis=2, keepdims=True)
    exponent = jnp.exp(scores - row_peak)
    share = exponent / jnp.sum(exponent, axis=2, keepdims=True)
    weights = share.astype(jnp.bfloat16)
    mixed = jnp.einsum("hij,hcj->hci", weights, value_heads, preferred_element_type=jnp.float32)
    return (
        mixed.reshape(head_count * HEAD_DIM, row_total),
        (query_heads, key_heads, value_heads, share, weights),
    )


def attend_grad(saved, out_grad):
    query_heads, key_heads, value_heads, share, weights = saved
    head_count, head_size, row_total = query_heads.shape
    grad_heads = out_grad.reshape(head_count, head_size, row_total)
    weight_grad = jnp.einsum(
        "hci,hcj->hij", grad_heads, value_heads, preferred_element_type=jnp.float32
    )
    weight_grad = lax.optimization_barrier(weight_grad.astype(jnp.bfloat16)).astype(jnp.float32)
    score_grad = (
        share
        * (weight_grad - jnp.sum(weight_grad * share, axis=2, keepdims=True))
        * HEAD_DIM ** (-0.5)
    )
    query_grad = jnp.einsum(
        "hij,hcj->hci", score_grad, key_heads.astype(jnp.float32), precision=lax.Precision.HIGHEST
    )
    key_grad = jnp.einsum(
        "hij,hci->hcj", score_grad, query_heads.astype(jnp.float32), precision=lax.Precision.HIGHEST
    )
    value_grad = jnp.einsum("hij,hci->hcj", weights, grad_heads, preferred_element_type=jnp.float32)
    stacked = jnp.stack([query_grad, key_grad, value_grad])
    return stacked.reshape(3, head_count * head_size, row_total)


def silu_slope(preact):
    sigmoid_value = jax.nn.sigmoid(preact)
    return sigmoid_value * (1.0 + preact * (1.0 - sigmoid_value))


def spread(weight_term, row_count):
    return lax.psum_scatter(
        weight_term(jnp.int32(0), lax.axis_size("tensor") * row_count).astype(jnp.bfloat16),
        "tensor",
        scatter_dimension=0,
        tiled=True,
    ).astype(jnp.float32)


def fold(pieces, combine, initial):
    return combine(initial, lax.all_gather(pieces, "tensor", axis=0, tiled=True), jnp.int32(0))


def section_pass(values, steps):
    return from_behind(values, "section", steps)


def local(
    frame_query,
    frame_key,
    frame_value,
    frame_segment,
    past_query,
    past_key,
    past_value,
    past_segment,
    visual_slot,
    past_slot,
    visual_proj,
    layer_weight,
    layer_input,
    saved_preact,
    layer_cotangent,
):
    section_count = lax.axis_size("section")
    first_flag = lax.axis_index("section") == 0
    model_rows = layer_weight.shape[1]
    head_rows = visual_proj.shape[0]
    model_width = visual_proj.shape[1]
    group_rows = frame_query.shape[3]
    token_count = layer_input.shape[2]
    visual_count = section_count * group_rows
    weight = layer_weight[0]
    current = attend_parts(
        frame_query[0, 0], frame_key[0, 0], frame_value[0, 0], frame_segment[0, 0]
    )[0].astype(jnp.bfloat16)
    past_float, past_saved = attend_parts(
        past_query[0, 0], past_key[0, 0], past_value[0, 0], past_segment[0, 0]
    )
    past_heads = past_float.astype(jnp.bfloat16)
    columns = jnp.arange(token_count, dtype=jnp.int32)
    slot_table = (visual_slot[0][:, None] == columns[None, :]).astype(jnp.bfloat16)
    past_table = (past_slot[0][:, None] == columns[None, :]).astype(jnp.bfloat16)

    def move_rows(rows_block):
        return lax.all_to_all(rows_block, "section", split_axis=1, concat_axis=1, tiled=True)

    def weight_term(first_row, row_count):
        return lax.dot_general(
            visual_proj, current, (((0,), (0,)), ((), ())), preferred_element_type=jnp.float32
        )

    embedded = spread(weight_term, model_rows).astype(jnp.bfloat16)
    padding = jnp.zeros((model_rows, visual_count - group_rows), jnp.bfloat16)
    visual_rows = move_rows(jnp.concatenate([embedded, padding], axis=1))
    placed = jnp.dot(visual_rows, slot_table, preferred_element_type=jnp.float32).astype(
        jnp.bfloat16
    )
    covered = jnp.sum(slot_table, axis=0, dtype=jnp.float32)
    text_rows = layer_input[0]
    inputs = jnp.where(first_flag & (covered[None, :] > 0.5), placed, text_rows)

    def weight_term(first_row, row_count):
        return lax.dot_general(
            weight, inputs, (((0,), (0,)), ((), ())), preferred_element_type=jnp.float32
        )

    preact = spread(weight_term, model_rows)
    hidden = (inputs.astype(jnp.float32) + jax.nn.silu(preact)).astype(jnp.bfloat16)
    forward_out = section_pass(hidden, 1)
    upstream = layer_cotangent[0].astype(jnp.float32)
    pre_grad = (upstream * silu_slope(saved_preact[0].astype(jnp.float32))).astype(jnp.bfloat16)

    def add_rows(running, arrived_piece, first_row):
        return jnp.dot(weight, arrived_piece, preferred_element_type=jnp.float32)

    input_grad = (
        upstream + fold(pre_grad, add_rows, jnp.zeros((model_rows, token_count), jnp.float32))
    ).astype(jnp.bfloat16)
    passed = section_pass(input_grad, -1)
    visual_grad = lax.dot_general(
        input_grad, past_table, (((1,), (1,)), ((), ())), preferred_element_type=jnp.float32
    ).astype(jnp.bfloat16)
    visual_grad = jnp.where(first_flag, visual_grad, jnp.zeros_like(visual_grad))

    def collect(state_pair, arrived_piece, first_row):
        outer_block = lax.dot_general(
            past_heads, arrived_piece, (((1,), (1,)), ((), ())), preferred_element_type=jnp.float32
        )
        head_total = jnp.dot(visual_proj, arrived_piece, preferred_element_type=jnp.float32)
        return (outer_block, head_total)

    returned = move_rows(visual_grad)[:, :group_rows]
    proj_table, head_total = fold(
        returned,
        collect,
        (
            jnp.zeros((head_rows, model_width), jnp.float32),
            jnp.zeros((head_rows, group_rows), jnp.float32),
        ),
    )
    head_grad = head_total.astype(jnp.bfloat16)
    grad_proj = lax.psum(proj_table, ("section", "dp")).astype(jnp.bfloat16)
    frame_grads = attend_grad(past_saved, head_grad)
    backward_out, grad_proj, grad_frames = (passed, grad_proj, frame_grads)
    return (forward_out[None], backward_out[None], grad_proj, grad_frames[:, None, None])


def solution(mesh):
    in_specs = (
        P("section", "dp", "tensor", None),
        P("section", "dp", "tensor", None),
        P("section", "dp", "tensor", None),
        P("section", "dp", None),
        P("section", "dp", "tensor", None),
        P("section", "dp", "tensor", None),
        P("section", "dp", "tensor", None),
        P("section", "dp", None),
        P("dp", None),
        P("dp", None),
        P("tensor", None),
        P("section", "tensor", None),
        P("section", "tensor", "dp"),
        P("section", "tensor", "dp"),
        P("section", "tensor", "dp"),
    )
    out_specs = (
        P("section", "tensor", "dp"),
        P("section", "tensor", "dp"),
        P("tensor", None),
        P(None, "section", "dp", "tensor", None),
    )
    return jax.shard_map(local, mesh=mesh, in_specs=in_specs, out_specs=out_specs, check_vma=False)
```

profile of v0, /device:TPU:64, one launch (start us, length us, event | category | flops | bytes accessed | tf_op | source)
XLA Modules:
  0.0 437.7 jit_solution(13031012490547648563)
XLA Ops:
  7.2 0.9 fusion.72
  8.2 0.3 copy-done
  8.6 1.8 fusion.1
  10.5 1.9 fusion.24
  12.4 66.4 %reduce-scatter.3.cloned.1.call-done = bf16[512,16]{0,1:T(8,128)(2,1)} async-done(((bf16[8192,16]{0,1:T(8,128)(2,1)}), bf16[512,16]{0,1:T(8,128)(2,1)}) %reduce-scatter.3.cloned.1.call-update) | async-done | bytes 16400 | tf_op jit(solution)/shard_map/reduce_scatter | solution.py:70
  78.7 1.4 concatenate.3
  80.1 10.5 %all-to-all-start = ((bf16[512,12,16]{0,2,1:T(8,128)(2,1)}), bf16[512,12,16]{0,2,1:T(8,128)(2,1)S(1)}, u32[]{:S(2)}, u32[]{:S(2)}) async-start(bf16[512,12,16]{0,2,1:T(8,128)(2,1)} %bitcast.6), calls=%async_computation.1 | async-start | bytes 393216 | tf_op jit(solution)/shard_map/all_to_all | solution.py:124
  90.8 11.6 %all-to-all-done = bf16[512,12,16]{0,2,1:T(8,128)(2,1)S(1)} async-done(((bf16[512,12,16]{0,2,1:T(8,128)(2,1)}), bf16[512,12,16]{0,2,1:T(8,128)(2,1)S(1)}, u32[]{:S(2)}, u32[]{:S(2)}) %all-to-all-start) | async-done | bytes 196640 | tf_op jit(solution)/shard_map/all_to_all | solution.py:124
  102.4 0.3 fusion.14
  102.8 7.0 %fusion = bf16[8192,192]{0,1:T(8,128)(2,1)} fusion(bf16[512,192]{0,1:T(8,128)(2,1)S(1)} %fusion.14, bf16[1,512,8192]{2,1,0:T(8,128)(2,1)} %param.26), kind=kOutput, calls=%fused_computation.1 | convolution fusion | flops 1612185600 | bytes 11730944 | tf_op jit(solution)/shard_map/dot_general | solution.py:142
  109.8 17.6 %all-gather.2.cloned.1.call-done = bf16[8192,192]{0,1:T(8,128)(2,1)} async-done(((bf16[512,192]{0,1:T(8,128)(2,1)}), bf16[8192,192]{0,1:T(8,128)(2,1)}) %all-gather.2.cloned.1.call-update) | async-done | bytes 3145744 | tf_op jit(solution)/shard_map/all_gather | solution.py:79
  127.4 7.2 %fusion.11 = bf16[512,192]{0,1:T(8,128)(2,1)S(1)} fusion(bf16[8192,192]{0,1:T(8,128)(2,1)} %all-gather.2.cloned.1.call-done, bf16[1,512,8192]{2,1,0:T(8,128)(2,1)} %param.26, bf16[1,512,192]{1,2,0:T(8,128)(2,1)S(1)} %copy-done.1), kind=kOutput, calls=%fused_computation.11 | convolution fusion | flops 1610907648 | bytes 11927552 | tf_op jit(solution)/shard_map/dot_general | solution.py:153
  134.7 0.9 fusion.15
  135.6 10.5 %all-to-all-start.1 = ((bf16[512,12,16]{0,2,1:T(8,128)(2,1)}), bf16[512,12,16]{0,2,1:T(8,128)(2,1)S(1)}, u32[]{:S(2)}, u32[]{:S(2)}) async-start(bf16[512,12,16]{0,2,1:T(8,128)(2,1)} %bitcast.23), calls=%async_computation.3 | async-start | bytes 393216 | tf_op jit(solution)/shard_map/all_to_all | solution.py:124
  146.2 1.9 collective-permute-start.1
  148.1 0.1 fusion.73
  148.3 10.1 %collective-permute-done.1 = bf16[512,192]{0,1:T(8,128)(2,1)S(1)} collective-permute-done((bf16[512,192]{0,1:T(8,128)(2,1)S(1)}, bf16[512,192]{0,1:T(8,128)(2,1)S(1)}, u32[]{:S(2)}, u32[]{:S(2)}) %collective-permute-start.1) | collective-permute-done | bytes 196640 | tf_op jit(solution)/shard_map/ppermute | solution.py:15
  158.4 1.9 all-to-all-done.1
  160.3 16.8 %all_gather.7 = bf16[8192,16]{0,1:T(8,128)(2,1)S(1)} all-gather(bf16[512,16]{0,1:T(8,128)(2,1)S(1)} %slice.4), channel_id=1, replica_groups=mesh['section'=12,'tensor'=16,'dp'=4] {'tensor'}, dimensions={0}, use_global_device_ids=true | all-gather | bytes 278528 | tf_op jit(solution)/shard_map/all_gather | solution.py:79
  177.1 2.2 fusion.18
  179.3 0.4 convolution_convert_fusion.4
  179.8 0.1 fusion.19
  179.9 0.1 convolution_bitcast_fusion.1
  180.1 0.2 convolution_bitcast_fusion.2
  180.3 236.9 %all-reduce.2 = bf16[80,8192]{1,0:T(8,128)(2,1)} all-reduce(f32[80,8192]{1,0:T(8,128)} %fusion.18), channel_id=1, replica_groups=mesh['section'=12,'tensor'=16,'dp'=4] {'section','dp'}, use_global_device_ids=true, to_apply=%region_7.8 | all-reduce | flops 655360 | bytes 3932160 | tf_op jit(solution)/shard_map/psum | solution.py:181
  417.2 1.1 fusion.30
  418.3 1.9 collective-permute-start
  420.2 0.1 convolution_bitcast_fusion
  420.3 0.6 maximum_bitcast_fusion
  420.9 8.8 %collective-permute-done = bf16[512,192]{0,1:T(8,128)(2,1)S(1)} collective-permute-done((bf16[512,192]{0,1:T(8,128)(2,1)S(1)}, bf16[512,192]{0,1:T(8,128)(2,1)S(1)}, u32[]{:S(2)}, u32[]{:S(2)}) %collective-permute-start) | collective-permute-done | bytes 196640 | tf_op jit(solution)/shard_map/ppermute | solution.py:15
  429.8 0.7 copy.28
  430.5 0.7 copy.29
  (30 shorter events, 0.4 us)
Async XLA Ops:
  7.2 1.4 copy-start
  7.2 83.5 %copy-start.3 = (s32[1,192]{1,0:T(1,128)S(1)}, s32[1,192]{1,0:T(1,128)}, u32[]{:S(2)}) copy-start(s32[1,192]{1,0:T(1,128)} %param.23) | copy-start | bytes 2308
  7.2 95.2 %copy-start.4 = (bf16[1,512,192]{1,2,0:T(8,128)(2,1)S(1)}, bf16[1,512,192]{1,2,0:T(8,128)(2,1)}, u32[]{:S(2)}) copy-start(bf16[1,512,192]{1,2,0:T(8,128)(2,1)} %param.27) | copy-start | bytes 589828
  7.2 71.5 %reduce-scatter.3.cloned.1.call-start = ((), (), s32[]{:S(2)}) async-start(), calls=%async_computation.4 | async-start | bytes 278528 | tf_op jit(solution)/shard_map/reduce_scatter | solution.py:70
  10.4 117.0 %all-gather.2.cloned.1.call-start = ((), (), s32[]{:S(2)}) async-start(), calls=%async_computation.6 | async-start | bytes 3342336 | tf_op jit(solution)/shard_map/all_gather | solution.py:79
  80.1 22.3 %all-to-all-start = ((bf16[512,12,16]{0,2,1:T(8,128)(2,1)}), bf16[512,12,16]{0,2,1:T(8,128)(2,1)S(1)}, u32[]{:S(2)}, u32[]{:S(2)}) async-start(bf16[512,12,16]{0,2,1:T(8,128)(2,1)} %bitcast.6), calls=%async_computation.1 | async-start | bytes 393216 | tf_op jit(solution)/shard_map/all_to_all | solution.py:124
  90.7 326.6 %reduce-scatter.5.cloned.1.call-start = ((), (), s32[]{:S(2)}) async-start(), calls=%async_computation.5 | async-start | bytes 3342336 | tf_op jit(solution)/shard_map/reduce_scatter | solution.py:70
  109.7 17.7 %copy-start.1 = (bf16[1,512,192]{1,2,0:T(8,128)(2,1)S(1)}, bf16[1,512,192]{1,2,0:T(8,128)(2,1)}, u32[]{:S(2)}) copy-start(bf16[1,512,192]{1,2,0:T(8,128)(2,1)} %param.29) | copy-start | bytes 589828
  109.8 24.9 %copy-start.7 = (s32[1,192]{1,0:T(1,128)S(1)}, s32[1,192]{1,0:T(1,128)}, u32[]{:S(2)}) copy-start(s32[1,192]{1,0:T(1,128)} %param.24) | copy-start | bytes 2308
  109.8 38.3 %copy-start.5 = (bf16[1,1,80,16]{2,3,1,0:T(8,128)(2,1)S(1)}, bf16[1,1,80,16]{2,3,1,0:T(8,128)(2,1)}, u32[]{:S(2)}) copy-start(bf16[1,1,80,16]{2,3,1,0:T(8,128)(2,1)} %param.19) | copy-start | bytes 7684
  109.8 38.3 %copy-start.6 = (bf16[1,1,80,16]{2,3,1,0:T(8,128)(2,1)S(1)}, bf16[1,1,80,16]{2,3,1,0:T(8,128)(2,1)}, u32[]{:S(2)}) copy-start(bf16[1,1,80,16]{2,3,1,0:T(8,128)(2,1)} %param.20) | copy-start | bytes 7684
  109.8 38.3 %copy-start.8 = (s32[1,1,16]{2,1,0:T(1,128)S(1)}, s32[1,1,16]{2,1,0:T(1,128)}, u32[]{:S(2)}) copy-start(s32[1,1,16]{2,1,0:T(1,128)} %param.22) | copy-start | bytes 196
  109.8 67.3 %copy-start.2 = (bf16[1,1,80,16]{2,3,1,0:T(8,128)(2,1)S(1)}, bf16[1,1,80,16]{2,3,1,0:T(8,128)(2,1)}, u32[]{:S(2)}) copy-start(bf16[1,1,80,16]{2,3,1,0:T(8,128)(2,1)} %param.21) | copy-start | bytes 7684
  135.6 24.6 %all-to-all-start.1 = ((bf16[512,12,16]{0,2,1:T(8,128)(2,1)}), bf16[512,12,16]{0,2,1:T(8,128)(2,1)S(1)}, u32[]{:S(2)}, u32[]{:S(2)}) async-start(bf16[512,12,16]{0,2,1:T(8,128)(2,1)} %bitcast.23), calls=%async_computation.3 | async-start | bytes 393216 | tf_op jit(solution)/shard_map/all_to_all | solution.py:124
  146.2 12.2 %collective-permute-start.1 = (bf16[512,192]{0,1:T(8,128)(2,1)S(1)}, bf16[512,192]{0,1:T(8,128)(2,1)S(1)}, u32[]{:S(2)}, u32[]{:S(2)}) collective-permute-start(bf16[512,192]{0,1:T(8,128)(2,1)S(1)} %fusion.11), channel_id=1, source_target_pairs={{64,0},{128,64},{192,128},{256,192},{320,256},{384,320},{448,384},... | collective-permute-start | bytes 589832 | tf_op jit(solution)/shard_map/ppermute | solution.py:15
  418.3 11.5 %collective-permute-start = (bf16[512,192]{0,1:T(8,128)(2,1)S(1)}, bf16[512,192]{0,1:T(8,128)(2,1)S(1)}, u32[]{:S(2)}, u32[]{:S(2)}) collective-permute-start(bf16[512,192]{0,1:T(8,128)(2,1)S(1)} %fusion.30), channel_id=1, source_target_pairs={{0,64},{64,128},{128,192},{192,256},{256,320},{320,384},{384,448},... | collective-permute-start | bytes 589832 | tf_op jit(solution)/shard_map/ppermute | solution.py:15
Sparse Core Ops, SparseCore 0:
  11.7 66.9 reduce-scatter.2
  82.0 45.3 all-gather.1
  130.9 65.8 reduce-scatter.4
where the time goes:
time: 438 us
  blocking collectives  254 us (58%)
  waiting for transfers between devices  116 us (26%)
  starting transfers between devices  25 us (6%)
  matrix products  21.6 us (5%)
  between operations  13.9 us (3%)
    psum x1, blocking collectives, local(): grad_proj = lax.psum(proj_table, ('section', 'dp')).astype(jnp.bfloat16)  237 us
    reduce_scatter x2, waiting for transfers between devices, spread(): lax.psum_scatter(weight_term(jnp.int32(0), lax.axis_size('tensor') * row_...  66.4 us
    all_to_all x2, starting transfers between devices, move_rows(): lax.all_to_all(rows_block, 'section', split_axis=1, concat_axis=1, tiled=...  21 us
    ppermute x2, waiting for transfers between devices, from_behind(): lax.ppermute(value, axis, [(source, source + steps) for source in range(f...  18.9 us
    all_gather x1, waiting for transfers between devices, fold(): lax.all_gather(pieces, 'tensor', axis=0, tiled=True)  17.6 us
    all_gather x1, blocking collectives, fold(): lax.all_gather(pieces, 'tensor', axis=0, tiled=True)  16.8 us
    all_to_all x2, waiting for transfers between devices, move_rows(): lax.all_to_all(rows_block, 'section', split_axis=1, concat_axis=1, tiled=...  13.5 us
  transfers between devices with their start and end apart: 7, of which 6 were waited for; matrix products, arithmetic and copies ran while one was open for 5% of the time, Pallas kernels for 0%

commit v1 on v0

v1 whole, which is shorter than its diff:
```python
import functools

import jax
import jax.numpy as jnp
from jax import lax
from jax.experimental import pallas as pl
from jax.experimental.pallas import tpu as pltpu
from jax.sharding import PartitionSpec as P

HEAD_DIM = 80


SCORE_FLOOR = -1e30


def attend_parts(query_rows, key_rows, value_rows, segment):
    scores = lax.dot_general(
        query_rows, key_rows, (((0,), (0,)), ((), ())), preferred_element_type=jnp.float32
    ) * HEAD_DIM ** (-0.5)
    same_sample = segment[:, None] == segment[None, :]
    scores = jnp.where(same_sample, scores, SCORE_FLOOR)
    row_peak = jnp.max(scores, axis=1, keepdims=True)
    exponent = jnp.exp(scores - row_peak)
    share = exponent / jnp.sum(exponent, axis=1, keepdims=True)
    weights = share.astype(jnp.bfloat16)
    mixed = lax.dot_general(
        weights, value_rows, (((1,), (1,)), ((), ())), preferred_element_type=jnp.float32
    )
    return mixed.astype(jnp.bfloat16), (query_rows, key_rows, value_rows, share, weights)


def attend_grad(saved, out_grad):
    query_rows, key_rows, value_rows, share, weights = saved
    weight_grad = jnp.dot(out_grad, value_rows, preferred_element_type=jnp.float32)
    score_grad = (
        share
        * (weight_grad - jnp.sum(weight_grad * share, axis=1, keepdims=True))
        * HEAD_DIM ** (-0.5)
    )
    query_grad = lax.dot_general(
        key_rows.astype(jnp.float32),
        score_grad,
        (((1,), (1,)), ((), ())),
        precision=lax.Precision.HIGHEST,
    )
    key_grad = jnp.dot(
        query_rows.astype(jnp.float32), score_grad, precision=lax.Precision.HIGHEST
    )
    value_grad = lax.dot_general(
        out_grad, weights, (((0,), (0,)), ((), ())), preferred_element_type=jnp.float32
    )
    return jnp.stack([query_grad, key_grad, value_grad])


def silu_slope(preact):
    sigmoid_value = jax.nn.sigmoid(preact)
    return sigmoid_value * (1.0 + preact * (1.0 - sigmoid_value))


def shift(value, axis, steps):
    count = lax.axis_size(axis)
    first, last = (max(0, -steps), min(count, count - steps))
    return lax.ppermute(value, axis, [(source, source + steps) for source in range(first, last)])


def rotate(value, axis, steps):
    count = lax.axis_size(axis)
    return lax.ppermute(value, axis, [(i, (i + steps) % count) for i in range(count)])


BLOCK = 4


def to_relays(value):
    count = lax.axis_size("section")
    own = lax.axis_index("section")
    base = jnp.where(own == 0, value, jnp.zeros_like(value))
    arrived = [lax.ppermute(value, "section", [(0, relay)]) for relay in range(BLOCK, count, BLOCK)]
    for piece in arrived:
        base = base + piece
    return base


def block_place(position, relay, count):
    return (relay + position - 1) % count


def spread_columns(base):
    sections, tensors, replicas = (lax.axis_size(axis) for axis in ("section", "tensor", "dp"))
    own = lax.axis_index("dp")
    width = base.shape[1] // replicas
    per_block = tensors // BLOCK

    def device(section, tensor, replica):
        return (section * tensors + tensor) * replicas + replica

    total = None
    for step in range(replicas):
        pairs = [
            (
                device(relay, per_block * position + j, replica),
                device(
                    block_place(position, relay, sections),
                    replicas * j + step,
                    (replica + step) % replicas,
                ),
            )
            for relay in range(0, sections, BLOCK)
            for position in range(BLOCK)
            for j in range(per_block)
            for replica in range(replicas)
        ]
        part = lax.dynamic_slice_in_dim(
            base, lax.rem(own + step, replicas) * width, width, axis=1
        )
        piece = lax.ppermute(part, ("section", "tensor", "dp"), pairs)
        total = piece if total is None else total + piece
    return total


def own_tokens(base, group_rows):
    count = lax.axis_size("section")
    own = lax.axis_index("section")

    def rows_of(section):
        return lax.dynamic_slice_in_dim(base, section * group_rows, group_rows, axis=0)

    total = jnp.where(own % BLOCK == 0, rows_of(own), 0)
    for position in range(BLOCK):
        if position != 1:
            pairs = [
                (relay, block_place(position, relay, count)) for relay in range(0, count, BLOCK)
            ]
            target = lax.rem(own + position - 1 + count, count)
            total = total + lax.ppermute(rows_of(target), "section", pairs)
    return total


def place_kernel(replicas, per_block, own_ref, *refs):
    pieces, out_ref = refs[:-1], refs[-1]
    position, replica = own_ref[0], own_ref[1]
    width = pieces[0].shape[3]
    for step in range(replicas):
        source = lax.rem(replica - step + replicas, replicas)
        for back in range(BLOCK):
            place = lax.rem(position - back + BLOCK, BLOCK)
            for j in range(per_block):
                column = ((place * per_block + j) * replicas + source) * width
                out_ref[:, pl.ds(pl.multiple_of(column, width), width)] = pieces[step][back, j]


def place_columns(own, pieces):
    replicas = len(pieces)
    block, per_block, rows, width = pieces[0].shape
    return pl.pallas_call(
        functools.partial(place_kernel, replicas, per_block),
        out_shape=jax.ShapeDtypeStruct((rows, replicas * block * per_block * width), jnp.bfloat16),
        in_specs=[pl.BlockSpec(memory_space=pltpu.SMEM)]
        + [pl.BlockSpec(memory_space=pltpu.VMEM)] * replicas,
        out_specs=pl.BlockSpec(memory_space=pltpu.VMEM),
        compiler_params=pltpu.CompilerParams(vmem_limit_bytes=16 * 1024 * 1024),
    )(own, *pieces)


def local(
    frame_query,
    frame_key,
    frame_value,
    frame_segment,
    past_query,
    past_key,
    past_value,
    past_segment,
    visual_slot,
    past_slot,
    visual_proj,
    layer_weight,
    layer_input,
    saved_preact,
    layer_cotangent,
):
    section_count = lax.axis_size("section")
    tensor_count = lax.axis_size("tensor")
    replica_count = lax.axis_size("dp")
    own_section = lax.axis_index("section")
    first_flag = own_section == 0
    model_rows = layer_weight.shape[1]
    head_rows = visual_proj.shape[0]
    group_rows = frame_query.shape[3]
    token_count = layer_input.shape[2]
    visual_count = section_count * group_rows
    weight = layer_weight[0]

    upstream = layer_cotangent[0].T.astype(jnp.float32)
    pre_grad = (upstream * silu_slope(saved_preact[0].T.astype(jnp.float32))).astype(jnp.bfloat16)
    pre_full = lax.all_gather(pre_grad, "tensor", axis=1, tiled=True)

    current, _ = attend_parts(
        frame_query[0, 0], frame_key[0, 0], frame_value[0, 0], frame_segment[0, 0]
    )
    past_heads, past_saved = attend_parts(
        past_query[0, 0], past_key[0, 0], past_value[0, 0], past_segment[0, 0]
    )
    columns = jnp.arange(token_count, dtype=jnp.int32)
    slot_table = (visual_slot[0][:, None] == columns[None, :]).astype(jnp.bfloat16)
    past_table = (past_slot[0][:, None] == columns[None, :]).astype(jnp.bfloat16)

    past_all = [past_heads] + [rotate(past_heads, "dp", step) for step in range(1, replica_count)]

    terms = jnp.dot(current, visual_proj, preferred_element_type=jnp.float32).astype(jnp.bfloat16)
    terms = lax.all_to_all(
        terms.reshape(group_rows, tensor_count, model_rows), "tensor", 1, 1, tiled=True
    )
    embedded = jnp.sum(terms.astype(jnp.float32), axis=1).astype(jnp.bfloat16)
    spare = jnp.zeros((group_rows, -(head_rows * replica_count) % 128), jnp.bfloat16)
    parcel = lax.all_gather(
        jnp.concatenate([embedded, *past_all, spare], axis=1), "section", axis=0, tiled=True
    )
    visual_rows = parcel[:, :model_rows]
    past_rows = jnp.concatenate(
        [
            parcel[:, model_rows + step * head_rows : model_rows + (step + 1) * head_rows]
            for step in range(replica_count)
        ],
        axis=0,
    )
    placed = lax.dot_general(
        slot_table, visual_rows, (((0,), (0,)), ((), ())), preferred_element_type=jnp.float32
    ).astype(jnp.bfloat16)
    covered = jnp.sum(slot_table, axis=0, dtype=jnp.float32)
    inputs = jnp.where(first_flag & (covered[:, None] > 0.5), placed, layer_input[0].T)

    input_grad = (
        upstream
        + lax.dot_general(
            pre_full, weight, (((1,), (1,)), ((), ())), preferred_element_type=jnp.float32
        )
    ).astype(jnp.bfloat16)
    visual_grad = jnp.dot(past_table, input_grad, preferred_element_type=jnp.float32).astype(
        jnp.bfloat16
    )

    inputs, visual_grad = lax.optimization_barrier((inputs, visual_grad))
    products = jnp.dot(inputs, weight, preferred_element_type=jnp.float32).astype(jnp.bfloat16)
    preact = lax.psum_scatter(products, "tensor", scatter_dimension=1, tiled=True).astype(
        jnp.float32
    )
    hidden = (inputs.astype(jnp.float32) + jax.nn.silu(preact)).astype(jnp.bfloat16)
    forward_out = shift(hidden, "section", 1)

    backward_out = shift(input_grad, "section", -1)
    base = to_relays(visual_grad)
    piece = spread_columns(base)
    own_grad = own_tokens(base, group_rows)
    gathered = lax.all_gather(piece, "tensor", axis=0)
    per_block = tensor_count // BLOCK
    gathered = gathered.reshape(per_block, replica_count * visual_count, model_rows // replica_count)
    own_columns = jnp.stack(
        [
            lax.dot_general(
                past_rows, gathered[j], (((0,), (0,)), ((), ())), preferred_element_type=jnp.float32
            ).astype(jnp.bfloat16)
            for j in range(per_block)
        ]
    )
    in_block = jnp.stack(
        [own_columns]
        + [
            rotate(own_columns, "section", step if step <= BLOCK // 2 else step - BLOCK)
            for step in range(1, BLOCK)
        ]
    )
    in_block, own_grad = lax.optimization_barrier((in_block, own_grad))
    pieces = [in_block] + [rotate(in_block, "dp", step) for step in range(1, replica_count)]
    position = jnp.stack([lax.rem(own_section + 1, BLOCK), lax.axis_index("dp")]).astype(jnp.int32)
    grad_proj = place_columns(position, pieces)

    own_full = lax.all_gather(own_grad, "tensor", axis=1, tiled=True)
    head_grad = lax.dot_general(
        own_full, visual_proj, (((1,), (1,)), ((), ())), preferred_element_type=jnp.float32
    ).astype(jnp.bfloat16)
    frame_grads = attend_grad(past_saved, head_grad)
    return (forward_out.T[None], backward_out.T[None], grad_proj, frame_grads[:, None, None])


def solution(mesh):
    in_specs = (
        P("section", "dp", "tensor", None),
        P("section", "dp", "tensor", None),
        P("section", "dp", "tensor", None),
        P("section", "dp", None),
        P("section", "dp", "tensor", None),
        P("section", "dp", "tensor", None),
        P("section", "dp", "tensor", None),
        P("section", "dp", None),
        P("dp", None),
        P("dp", None),
        P("tensor", None),
        P("section", "tensor", None),
        P("section", "tensor", "dp"),
        P("section", "tensor", "dp"),
        P("section", "tensor", "dp"),
    )
    out_specs = (
        P("section", "tensor", "dp"),
        P("section", "tensor", "dp"),
        P("tensor", None),
        P(None, "section", "dp", "tensor", None),
    )
    return jax.shard_map(local, mesh=mesh, in_specs=in_specs, out_specs=out_specs, check_vma=False)
```

time: 438 us -> 188 us (0.43)
  the two profiles are of different devices: /device:TPU:64 before, /device:TPU:1 now
where the time goes in v1:
time: 188 us; the launch traced here: 187 us
  starting transfers between devices  65.5 us (35%)
  blocking collectives  61.2 us (33%)
  matrix products  18.9 us (10%)
  waiting for transfers between devices  18.6 us (10%)
  between operations  14.6 us (8%)
  other arithmetic  4.15 us (2%)
  local copies, waits for them, and re-layouts  2.41 us (1%)
  Pallas kernels  1.98 us (1%)
    ppermute x9, starting transfers between devices, rotate(): lax.ppermute(value, axis, [(i, (i + steps) % count) for i in range(count)])  27.3 us
    all_gather x1, blocking collectives, local(): lax.all_gather(jnp.concatenate([embedded, *past_all, spare], axis=1), 'se...  25.8 us
    all_gather x1, blocking collectives, local(): gathered = lax.all_gather(piece, 'tensor', axis=0)  19.5 us
    all_gather x1, blocking collectives, local(): own_full = lax.all_gather(own_grad, 'tensor', axis=1, tiled=True)  16 us
    all_to_all x1, starting transfers between devices, local(): lax.all_to_all(terms.reshape(group_rows, tensor_count, model_rows), 'tens...  13.8 us
    ppermute x2, starting transfers between devices, to_relays(): lax.ppermute(value, 'section', [(0, relay)])  9.8 us
    dot_general x1, matrix products, local(): lax.dot_general(pre_full, weight, (((1,), (1,)), ((), ())), preferred_ele...  7.24 us
    dot_general x1, matrix products, local(): jnp.dot(inputs, weight, preferred_element_type=jnp.float32)  6.85 us
  transfers between devices with their start and end apart: 23, of which 8 were waited for; matrix products, arithmetic and copies ran while one was open for 4% of the time, Pallas kernels for 1%

profile of v1, /device:TPU:1, one launch (start us, length us, event | category | flops | bytes accessed | tf_op | source)
XLA Modules:
  0.0 187.3 jit_solution(8335878918511120858)
XLA Ops:
  7.3 2.0 %fusion.28 = bf16[192,512]{1,0:T(8,128)(2,1)} fusion(bf16[1,512,192]{1,2,0:T(8,128)(2,1)} %param.28, bf16[1,512,192]{1,2,0:T(8,128)(2,1)} %param.29), kind=kLoop, calls=%fused_computation.43 | loop fusion | flops 1081344 | bytes 589824 | tf_op jit(solution)/shard_map/convert_element_type | solution.py:195
  12.1 13.8 %all-to-all-start = ((bf16[16,16,512]{2,0,1:T(8,128)(2,1)}), bf16[16,16,512]{2,0,1:T(8,128)(2,1)S(1)}, u32[]{:S(2)}, u32[]{:S(2)}) async-start(bf16[16,16,512]{2,0,1:T(8,128)(2,1)} %bitcast.133), calls=%async_computation | async-start | bytes 524288 | tf_op jit(solution)/shard_map/all_to_all | solution.py:211
  26.4 1.9 %collective-permute-start = (bf16[16,80]{1,0:T(8,128)(2,1)S(1)}, bf16[16,80]{1,0:T(8,128)(2,1)S(1)}, u32[]{:S(2)}, u32[]{:S(2)}) collective-permute-start(bf16[16,80]{1,0:T(8,128)(2,1)S(1)} %convolution_convert_fusion.9), channel_id=1, source_target_pairs={{0,1},{1,2},{2,3},{3,0},{4,5},{5,6},{6,7},{7,4},{8,9},{9,10},{10,1... | collective-permute-start | bytes 7688 | tf_op jit(solution)/shard_map/ppermute | solution.py:68
  28.3 1.9 %collective-permute-start.1 = (bf16[16,80]{1,0:T(8,128)(2,1)S(1)}, bf16[16,80]{1,0:T(8,128)(2,1)S(1)}, u32[]{:S(2)}, u32[]{:S(2)}) collective-permute-start(bf16[16,80]{1,0:T(8,128)(2,1)S(1)} %convolution_convert_fusion.9), channel_id=1, source_target_pairs={{0,2},{1,3},{2,0},{3,1},{4,6},{5,7},{6,4},{7,5},{8,10},{9,11},{10,... | collective-permute-start | bytes 7688 | tf_op jit(solution)/shard_map/ppermute | solution.py:68
  30.3 4.6 %collective-permute-start.2 = (bf16[16,80]{1,0:T(8,128)(2,1)S(1)}, bf16[16,80]{1,0:T(8,128)(2,1)S(1)}, u32[]{:S(2)}, u32[]{:S(2)}) collective-permute-start(bf16[16,80]{1,0:T(8,128)(2,1)S(1)} %convolution_convert_fusion.9), channel_id=1, source_target_pairs={{0,3},{1,0},{2,1},{3,2},{4,7},{5,4},{6,5},{7,6},{8,11},{9,8},{10,9... | collective-permute-start | bytes 7688 | tf_op jit(solution)/shard_map/ppermute | solution.py:68
  35.0 2.9 %all-to-all-done = bf16[16,16,512]{2,0,1:T(8,128)(2,1)S(1)} async-done(((bf16[16,16,512]{2,0,1:T(8,128)(2,1)}), bf16[16,16,512]{2,0,1:T(8,128)(2,1)S(1)}, u32[]{:S(2)}, u32[]{:S(2)}) %all-to-all-start) | async-done | bytes 262176 | tf_op jit(solution)/shard_map/all_to_all | solution.py:211
  38.0 25.8 %all_gather.15 = bf16[192,896]{1,0:T(8,128)(2,1)S(1)} all-gather(bf16[16,896]{1,0:T(8,128)(2,1)S(1)} %concatenate.6), channel_id=1, replica_groups=mesh['section'=12,'tensor'=16,'dp'=4] {'section'}, dimensions={0}, use_global_device_ids=true | all-gather | bytes 372736 | tf_op jit(solution)/shard_map/all_gather | solution.py:216
  65.4 7.2 %fusion.6 = bf16[192,512]{1,0:T(8,128)(2,1)S(1)} fusion(bf16[192,8192]{1,0:T(8,128)(2,1)} %all-gather.3.cloned.1.call-done, bf16[1,512,8192]{2,1,0:T(8,128)(2,1)} %param.26, bf16[1,512,192]{1,2,0:T(8,128)(2,1)S(1)} %copy-done.1), kind=kOutput, calls=%fused_computation.8 | convolution fusion | flops 1610907648 | bytes 11927552 | tf_op jit(solution)/shard_map/dot_general | solution.py:235
  72.9 6.9 %convolution_convert_fusion = bf16[192,8192]{1,0:T(8,128)(2,1)} fusion(bf16[192,512]{1,0:T(8,128)(2,1)S(1)} %fusion.9, bf16[1,512,8192]{2,1,0:T(8,128)(2,1)} %param.26), kind=kOutput, calls=%fused_computation | convolution fusion | flops 1612185600 | bytes 11730944 | tf_op jit(solution)/shard_map/dot_general | solution.py:244
  79.9 8.5 %collective-permute-start.6 = (bf16[192,512]{1,0:T(8,128)(2,1)S(1)}, bf16[192,512]{1,0:T(8,128)(2,1)S(1)}, u32[]{:S(2)}, u32[]{:S(2)}) collective-permute-start(bf16[192,512]{1,0:T(8,128)(2,1)S(1)} %convolution_convert_fusion.2), channel_id=1, source_target_pairs={{0,512},{1,513},{2,514},{3,515},{4,516},{5,517},{6,518},{7,519},{8... | collective-permute-start | bytes 589832 | tf_op jit(solution)/shard_map/ppermute | solution.py:78
  88.4 1.3 collective-permute-start.5
  89.8 1.3 collective-permute-start.4
  91.1 1.3 collective-permute-done.6
  93.8 1.5 collective-permute-start.10
  95.4 1.4 collective-permute-start.9
  96.8 1.3 collective-permute-start.7
  98.1 1.9 %collective-permute-start.8 = (bf16[192,128]{1,0:T(8,128)(2,1)S(1)}, bf16[192,128]{1,0:T(8,128)(2,1)S(1)}, u32[]{:S(2)}, u32[]{:S(2)}) collective-permute-start(bf16[192,128]{1,0:T(8,128)(2,1)S(1)} %get-tuple-element.31), channel_id=1, source_target_pairs={{0,709},{1,710},{2,711},{3,708},{4,725},{5,726},{6,727},{7,724},{8... | collective-permute-start | bytes 147464 | tf_op jit(solution)/shard_map/ppermute | solution.py:116
  101.3 1.3 collective-permute-start.15
  104.0 4.9 %collective-permute-done.8 = bf16[192,128]{1,0:T(8,128)(2,1)S(1)} collective-permute-done((bf16[192,128]{1,0:T(8,128)(2,1)S(1)}, bf16[192,128]{1,0:T(8,128)(2,1)S(1)}, u32[]{:S(2)}, u32[]{:S(2)}) %collective-permute-start.8) | collective-permute-done | bytes 49184 | tf_op jit(solution)/shard_map/ppermute | solution.py:116
  108.9 19.5 %all-gather = bf16[3072,128]{1,0:T(8,128)(2,1)S(1)} all-gather(bf16[192,128]{1,0:T(8,128)(2,1)S(1)} %add_add_fusion.1), channel_id=2, replica_groups=mesh['section'=12,'tensor'=16,'dp'=4] {'tensor'}, dimensions={0}, use_global_device_ids=true | all-gather | bytes 835584 | tf_op jit(solution)/shard_map/all_gather | solution.py:255
  129.3 1.9 %collective-permute-start.13 = (bf16[4,80,128]{2,1,0:T(8,128)(2,1)S(1)}, bf16[4,80,128]{2,1,0:T(8,128)(2,1)S(1)}, u32[]{:S(2)}, u32[]{:S(2)}) collective-permute-start(bf16[4,80,128]{2,1,0:T(8,128)(2,1)S(1)} %get-tuple-element.36), channel_id=1, source_target_pairs={{0,704},{64,0},{128,64},{192,128},{256,192},{320,256},{384,320},{4... | collective-permute-start | bytes 245768 | tf_op jit(solution)/shard_map/ppermute | solution.py:68
  131.3 3.4 %collective-permute-start.12 = (bf16[4,80,128]{2,1,0:T(8,128)(2,1)S(1)}, bf16[4,80,128]{2,1,0:T(8,128)(2,1)S(1)}, u32[]{:S(2)}, u32[]{:S(2)}) collective-permute-start(bf16[4,80,128]{2,1,0:T(8,128)(2,1)S(1)} %get-tuple-element.36), channel_id=1, source_target_pairs={{0,128},{64,192},{128,256},{192,320},{256,384},{320,448},{384,512}... | collective-permute-start | bytes 245768 | tf_op jit(solution)/shard_map/ppermute | solution.py:68
  134.7 2.6 %collective-permute-start.11 = (bf16[4,80,128]{2,1,0:T(8,128)(2,1)S(1)}, bf16[4,80,128]{2,1,0:T(8,128)(2,1)S(1)}, u32[]{:S(2)}, u32[]{:S(2)}) collective-permute-start(bf16[4,80,128]{2,1,0:T(8,128)(2,1)S(1)} %get-tuple-element.36), channel_id=1, source_target_pairs={{0,64},{64,128},{128,192},{192,256},{256,320},{320,384},{384,448},... | collective-permute-start | bytes 245768 | tf_op jit(solution)/shard_map/ppermute | solution.py:68
  137.4 1.7 collective-permute-done.12
  139.1 3.8 %collective-permute-done.11 = bf16[4,80,128]{2,1,0:T(8,128)(2,1)S(1)} collective-permute-done((bf16[4,80,128]{2,1,0:T(8,128)(2,1)S(1)}, bf16[4,80,128]{2,1,0:T(8,128)(2,1)S(1)}, u32[]{:S(2)}, u32[]{:S(2)}) %collective-permute-start.11) | collective-permute-done | bytes 81952 | tf_op jit(solution)/shard_map/ppermute | solution.py:68
  143.0 3.9 %collective-permute-start.17 = (bf16[4,4,80,128]{3,2,1,0:T(8,128)(2,1)S(1)}, bf16[4,4,80,128]{3,2,1,0:T(8,128)(2,1)S(1)}, u32[]{:S(2)}, u32[]{:S(2)}) collective-permute-start(bf16[4,4,80,128]{3,2,1,0:T(8,128)(2,1)S(1)} %pad_maximum_fusion.refs_0_), channel_id=1, source_target_pairs={{0,1},{1,2},{2,3},{3,0},{4,5},{5,6},{6,7},{7,4},{8,9},{9,10},{10,1... | collective-permute-start | bytes 983048 | tf_op jit(solution)/shard_map/ppermute | solution.py:68
  146.9 3.8 %collective-permute-start.18 = (bf16[4,4,80,128]{3,2,1,0:T(8,128)(2,1)S(1)}, bf16[4,4,80,128]{3,2,1,0:T(8,128)(2,1)S(1)}, u32[]{:S(2)}, u32[]{:S(2)}) collective-permute-start(bf16[4,4,80,128]{3,2,1,0:T(8,128)(2,1)S(1)} %pad_maximum_fusion.refs_0_), channel_id=1, source_target_pairs={{0,2},{1,3},{2,0},{3,1},{4,6},{5,7},{6,4},{7,5},{8,10},{9,11},{10,... | collective-permute-start | bytes 983048 | tf_op jit(solution)/shard_map/ppermute | solution.py:68
  150.6 3.2 %collective-permute-start.19 = (bf16[4,4,80,128]{3,2,1,0:T(8,128)(2,1)S(1)}, bf16[4,4,80,128]{3,2,1,0:T(8,128)(2,1)S(1)}, u32[]{:S(2)}, u32[]{:S(2)}) collective-permute-start(bf16[4,4,80,128]{3,2,1,0:T(8,128)(2,1)S(1)} %pad_maximum_fusion.refs_0_), channel_id=1, source_target_pairs={{0,3},{1,0},{2,1},{3,2},{4,7},{5,4},{6,5},{7,6},{8,11},{9,8},{10,9... | collective-permute-start | bytes 983048 | tf_op jit(solution)/shard_map/ppermute | solution.py:68
  153.9 16.0 %all_gather.19 = bf16[16,8192]{1,0:T(8,128)(2,1)S(1)} all-gather(bf16[16,512]{1,0:T(8,128)(2,1)S(1)} %add_add_fusion.2), channel_id=1, replica_groups=mesh['section'=12,'tensor'=16,'dp'=4] {'tensor'}, dimensions={1}, use_global_device_ids=true | all-gather | bytes 278528 | tf_op jit(solution)/shard_map/all_gather | solution.py:278
  171.8 3.1 %collective-permute-start.3 = (bf16[192,512]{1,0:T(8,128)(2,1)S(1)}, bf16[192,512]{1,0:T(8,128)(2,1)S(1)}, u32[]{:S(2)}, u32[]{:S(2)}) collective-permute-start(bf16[192,512]{1,0:T(8,128)(2,1)S(1)} %fusion.29), channel_id=1, source_target_pairs={{0,64},{64,128},{128,192},{192,256},{256,320},{320,384},{384,448},... | collective-permute-start | bytes 589832 | tf_op jit(solution)/shard_map/ppermute | solution.py:63
  175.8 2.0 %shard_map.174 = bf16[80,8192]{1,0:T(8,128)(2,1)} custom-call(s32[2]{0:T(128)S(1)} %pad_add_fusion.own_ref, bf16[4,4,80,128]{3,2,1,0:T(8,128)(2,1)S(1)} %pad_maximum_fusion.refs_0_, bf16[4,4,80,128]{3,2,1,0:T(8,128)(2,1)S(1)} %collective-permute-done.17.refs_1_, bf16[4,4,80,128]{3,2,1,0:T(8,128)(2,1)S(1)} %collective-permute-done.18.refs_2_, ...), custom_call_target="tpu_custom_call" | custom-call | tf_op jit(solution)/shard_map/pallas_call | solution.py:155
  177.7 1.4 collective-permute-done.3
  (77 shorter events, 14.6 us)
Async XLA Ops:
  7.2 3.1 %copy-start = (bf16[80,8192]{1,0:T(8,128)(2,1)S(1)}, bf16[80,8192]{1,0:T(8,128)(2,1)}, u32[]{:S(2)}) copy-start(bf16[80,8192]{1,0:T(8,128)(2,1)} %param.25) | copy-start | bytes 3932164
  7.2 58.2 %copy-start.1 = (bf16[1,512,192]{1,2,0:T(8,128)(2,1)S(1)}, bf16[1,512,192]{1,2,0:T(8,128)(2,1)}, u32[]{:S(2)}) copy-start(bf16[1,512,192]{1,2,0:T(8,128)(2,1)} %param.29) | copy-start | bytes 589828
  7.2 18.8 %copy-start.7 = (bf16[1,1,80,16]{2,3,1,0:T(8,128)(2,1)S(1)}, bf16[1,1,80,16]{2,3,1,0:T(8,128)(2,1)}, u32[]{:S(2)}) copy-start(bf16[1,1,80,16]{2,3,1,0:T(8,128)(2,1)} %param.20) | copy-start | bytes 7684
  7.2 18.8 %copy-start.6 = (bf16[1,1,80,16]{2,3,1,0:T(8,128)(2,1)S(1)}, bf16[1,1,80,16]{2,3,1,0:T(8,128)(2,1)}, u32[]{:S(2)}) copy-start(bf16[1,1,80,16]{2,3,1,0:T(8,128)(2,1)} %param.19) | copy-start | bytes 7684
  7.2 18.8 %copy-start.8 = (s32[1,1,16]{2,1,0:T(1,128)S(1)}, s32[1,1,16]{2,1,0:T(1,128)}, u32[]{:S(2)}) copy-start(s32[1,1,16]{2,1,0:T(1,128)} %param.22) | copy-start | bytes 196
  7.2 19.0 %copy-start.5 = (bf16[1,1,80,16]{2,3,1,0:T(8,128)(2,1)S(1)}, bf16[1,1,80,16]{2,3,1,0:T(8,128)(2,1)}, u32[]{:S(2)}) copy-start(bf16[1,1,80,16]{2,3,1,0:T(8,128)(2,1)} %param.21) | copy-start | bytes 7684
  7.2 27.6 %copy-start.3 = (s32[1,192]{1,0:T(1,128)S(1)}, s32[1,192]{1,0:T(1,128)}, u32[]{:S(2)}) copy-start(s32[1,192]{1,0:T(1,128)} %param.23) | copy-start | bytes 2308
  7.2 56.6 %copy-start.4 = (bf16[1,512,192]{1,2,0:T(8,128)(2,1)S(1)}, bf16[1,512,192]{1,2,0:T(8,128)(2,1)}, u32[]{:S(2)}) copy-start(bf16[1,512,192]{1,2,0:T(8,128)(2,1)} %param.27) | copy-start | bytes 589828
  7.3 58.1 %all-gather.3.cloned.1.call-start = ((), (), s32[]{:S(2)}) async-start(), calls=%async_computation.2 | async-start | bytes 3342336 | tf_op jit(solution)/shard_map/all_gather | solution.py:196
  12.1 25.7 %all-to-all-start = ((bf16[16,16,512]{2,0,1:T(8,128)(2,1)}), bf16[16,16,512]{2,0,1:T(8,128)(2,1)S(1)}, u32[]{:S(2)}, u32[]{:S(2)}) async-start(bf16[16,16,512]{2,0,1:T(8,128)(2,1)} %bitcast.133), calls=%async_computation | async-start | bytes 524288 | tf_op jit(solution)/shard_map/all_to_all | solution.py:211
  26.0 144.8 %reduce-scatter.2.cloned.1.call-start = ((), (), s32[]{:S(2)}) async-start(), calls=%async_computation.3 | async-start | bytes 3342336 | tf_op jit(solution)/shard_map/reduce_scatter | solution.py:245
  26.4 11.5 %collective-permute-start = (bf16[16,80]{1,0:T(8,128)(2,1)S(1)}, bf16[16,80]{1,0:T(8,128)(2,1)S(1)}, u32[]{:S(2)}, u32[]{:S(2)}) collective-permute-start(bf16[16,80]{1,0:T(8,128)(2,1)S(1)} %convolution_convert_fusion.9), channel_id=1, source_target_pairs={{0,1},{1,2},{2,3},{3,0},{4,5},{5,6},{6,7},{7,4},{8,9},{9,10},{10,1... | collective-permute-start | bytes 7688 | tf_op jit(solution)/shard_map/ppermute | solution.py:68
  28.3 9.6 %collective-permute-start.1 = (bf16[16,80]{1,0:T(8,128)(2,1)S(1)}, bf16[16,80]{1,0:T(8,128)(2,1)S(1)}, u32[]{:S(2)}, u32[]{:S(2)}) collective-permute-start(bf16[16,80]{1,0:T(8,128)(2,1)S(1)} %convolution_convert_fusion.9), channel_id=1, source_target_pairs={{0,2},{1,3},{2,0},{3,1},{4,6},{5,7},{6,4},{7,5},{8,10},{9,11},{10,... | collective-permute-start | bytes 7688 | tf_op jit(solution)/shard_map/ppermute | solution.py:68
  30.3 7.6 %collective-permute-start.2 = (bf16[16,80]{1,0:T(8,128)(2,1)S(1)}, bf16[16,80]{1,0:T(8,128)(2,1)S(1)}, u32[]{:S(2)}, u32[]{:S(2)}) collective-permute-start(bf16[16,80]{1,0:T(8,128)(2,1)S(1)} %convolution_convert_fusion.9), channel_id=1, source_target_pairs={{0,3},{1,0},{2,1},{3,2},{4,7},{5,4},{6,5},{7,6},{8,11},{9,8},{10,9... | collective-permute-start | bytes 7688 | tf_op jit(solution)/shard_map/ppermute | solution.py:68
  64.1 8.5 %copy-start.2 = (s32[1,192]{1,0:T(1,128)S(1)}, s32[1,192]{1,0:T(1,128)}, u32[]{:S(2)}) copy-start(s32[1,192]{1,0:T(1,128)} %param.24) | copy-start | bytes 2308
  79.9 12.6 %collective-permute-start.6 = (bf16[192,512]{1,0:T(8,128)(2,1)S(1)}, bf16[192,512]{1,0:T(8,128)(2,1)S(1)}, u32[]{:S(2)}, u32[]{:S(2)}) collective-permute-start(bf16[192,512]{1,0:T(8,128)(2,1)S(1)} %convolution_convert_fusion.2), channel_id=1, source_target_pairs={{0,512},{1,513},{2,514},{3,515},{4,516},{5,517},{6,518},{7,519},{8... | collective-permute-start | bytes 589832 | tf_op jit(solution)/shard_map/ppermute | solution.py:78
  88.4 5.3 %collective-permute-start.5 = (bf16[192,512]{1,0:T(8,128)(2,1)S(1)}, bf16[192,512]{1,0:T(8,128)(2,1)S(1)}, u32[]{:S(2)}, u32[]{:S(2)}) collective-permute-start(bf16[192,512]{1,0:T(8,128)(2,1)S(1)} %convolution_convert_fusion.2), channel_id=1, source_target_pairs={{0,256},{1,257},{2,258},{3,259},{4,260},{5,261},{6,262},{7,263},{8... | collective-permute-start | bytes 589832 | tf_op jit(solution)/shard_map/ppermute | solution.py:78
  89.8 10.2 %collective-permute-start.4 = (bf16[192,512]{1,0:T(8,128)(2,1)S(1)}, bf16[192,512]{1,0:T(8,128)(2,1)S(1)}, u32[]{:S(2)}, u32[]{:S(2)}) collective-permute-start(bf16[192,512]{1,0:T(8,128)(2,1)S(1)} %fusion.6), channel_id=1, source_target_pairs={{64,0},{128,64},{192,128},{256,192},{320,256},{384,320},{448,384},... | collective-permute-start | bytes 589832 | tf_op jit(solution)/shard_map/ppermute | solution.py:63
  93.8 7.5 %collective-permute-start.10 = (bf16[192,128]{1,0:T(8,128)(2,1)S(1)}, bf16[192,128]{1,0:T(8,128)(2,1)S(1)}, u32[]{:S(2)}, u32[]{:S(2)}) collective-permute-start(bf16[192,128]{1,0:T(8,128)(2,1)S(1)} %get-tuple-element.32), channel_id=1, source_target_pairs={{0,719},{1,716},{2,717},{3,718},{4,735},{5,732},{6,733},{7,734},{8... | collective-permute-start | bytes 147464 | tf_op jit(solution)/shard_map/ppermute | solution.py:116
  95.4 7.3 %collective-permute-start.9 = (bf16[192,128]{1,0:T(8,128)(2,1)S(1)}, bf16[192,128]{1,0:T(8,128)(2,1)S(1)}, u32[]{:S(2)}, u32[]{:S(2)}) collective-permute-start(bf16[192,128]{1,0:T(8,128)(2,1)S(1)} %get-tuple-element.33), channel_id=1, source_target_pairs={{0,714},{1,715},{2,712},{3,713},{4,730},{5,731},{6,728},{7,729},{8... | collective-permute-start | bytes 147464 | tf_op jit(solution)/shard_map/ppermute | solution.py:116
  96.8 7.2 %collective-permute-start.7 = (bf16[192,128]{1,0:T(8,128)(2,1)S(1)}, bf16[192,128]{1,0:T(8,128)(2,1)S(1)}, u32[]{:S(2)}, u32[]{:S(2)}) collective-permute-start(bf16[192,128]{1,0:T(8,128)(2,1)S(1)} %get-tuple-element.34), channel_id=1, source_target_pairs={{0,704},{1,705},{2,706},{3,707},{4,720},{5,721},{6,722},{7,723},{8... | collective-permute-start | bytes 147464 | tf_op jit(solution)/shard_map/ppermute | solution.py:116
  98.1 10.8 %collective-permute-start.8 = (bf16[192,128]{1,0:T(8,128)(2,1)S(1)}, bf16[192,128]{1,0:T(8,128)(2,1)S(1)}, u32[]{:S(2)}, u32[]{:S(2)}) collective-permute-start(bf16[192,128]{1,0:T(8,128)(2,1)S(1)} %get-tuple-element.31), channel_id=1, source_target_pairs={{0,709},{1,710},{2,711},{3,708},{4,725},{5,726},{6,727},{7,724},{8... | collective-permute-start | bytes 147464 | tf_op jit(solution)/shard_map/ppermute | solution.py:116
  100.0 34.7 %collective-permute-start.16 = (bf16[16,512]{1,0:T(8,128)(2,1)S(1)}, bf16[16,512]{1,0:T(8,128)(2,1)S(1)}, u32[]{:S(2)}, u32[]{:S(2)}) collective-permute-start(bf16[16,512]{1,0:T(8,128)(2,1)S(1)} %get-tuple-element.29), channel_id=1, source_target_pairs={{0,128},{256,384},{512,640},{1,129},{257,385},{513,641},{2,130},{2... | collective-permute-start | bytes 49160 | tf_op jit(solution)/shard_map/ppermute | solution.py:135
  101.3 36.0 %collective-permute-start.15 = (bf16[16,512]{1,0:T(8,128)(2,1)S(1)}, bf16[16,512]{1,0:T(8,128)(2,1)S(1)}, u32[]{:S(2)}, u32[]{:S(2)}) collective-permute-start(bf16[16,512]{1,0:T(8,128)(2,1)S(1)} %get-tuple-element.30), channel_id=1, source_target_pairs={{0,64},{256,320},{512,576},{1,65},{257,321},{513,577},{2,66},{258,... | collective-permute-start | bytes 49160 | tf_op jit(solution)/shard_map/ppermute | solution.py:135
  102.6 34.7 %collective-permute-start.14 = (bf16[16,512]{1,0:T(8,128)(2,1)S(1)}, bf16[16,512]{1,0:T(8,128)(2,1)S(1)}, u32[]{:S(2)}, u32[]{:S(2)}) collective-permute-start(bf16[16,512]{1,0:T(8,128)(2,1)S(1)} %get-tuple-element.28), channel_id=1, source_target_pairs={{0,704},{256,192},{512,448},{1,705},{257,193},{513,449},{2,706},{2... | collective-permute-start | bytes 49160 | tf_op jit(solution)/shard_map/ppermute | solution.py:135
  129.3 8.1 %collective-permute-start.13 = (bf16[4,80,128]{2,1,0:T(8,128)(2,1)S(1)}, bf16[4,80,128]{2,1,0:T(8,128)(2,1)S(1)}, u32[]{:S(2)}, u32[]{:S(2)}) collective-permute-start(bf16[4,80,128]{2,1,0:T(8,128)(2,1)S(1)} %get-tuple-element.36), channel_id=1, source_target_pairs={{0,704},{64,0},{128,64},{192,128},{256,192},{320,256},{384,320},{4... | collective-permute-start | bytes 245768 | tf_op jit(solution)/shard_map/ppermute | solution.py:68
  131.3 7.9 %collective-permute-start.12 = (bf16[4,80,128]{2,1,0:T(8,128)(2,1)S(1)}, bf16[4,80,128]{2,1,0:T(8,128)(2,1)S(1)}, u32[]{:S(2)}, u32[]{:S(2)}) collective-permute-start(bf16[4,80,128]{2,1,0:T(8,128)(2,1)S(1)} %get-tuple-element.36), channel_id=1, source_target_pairs={{0,128},{64,192},{128,256},{192,320},{256,384},{320,448},{384,512}... | collective-permute-start | bytes 245768 | tf_op jit(solution)/shard_map/ppermute | solution.py:68
  134.7 8.2 %collective-permute-start.11 = (bf16[4,80,128]{2,1,0:T(8,128)(2,1)S(1)}, bf16[4,80,128]{2,1,0:T(8,128)(2,1)S(1)}, u32[]{:S(2)}, u32[]{:S(2)}) collective-permute-start(bf16[4,80,128]{2,1,0:T(8,128)(2,1)S(1)} %get-tuple-element.36), channel_id=1, source_target_pairs={{0,64},{64,128},{128,192},{192,256},{256,320},{320,384},{384,448},... | collective-permute-start | bytes 245768 | tf_op jit(solution)/shard_map/ppermute | solution.py:68
  143.0 32.8 %collective-permute-start.17 = (bf16[4,4,80,128]{3,2,1,0:T(8,128)(2,1)S(1)}, bf16[4,4,80,128]{3,2,1,0:T(8,128)(2,1)S(1)}, u32[]{:S(2)}, u32[]{:S(2)}) collective-permute-start(bf16[4,4,80,128]{3,2,1,0:T(8,128)(2,1)S(1)} %pad_maximum_fusion.refs_0_), channel_id=1, source_target_pairs={{0,1},{1,2},{2,3},{3,0},{4,5},{5,6},{6,7},{7,4},{8,9},{9,10},{10,1... | collective-permute-start | bytes 983048 | tf_op jit(solution)/shard_map/ppermute | solution.py:68
  146.9 28.9 %collective-permute-start.18 = (bf16[4,4,80,128]{3,2,1,0:T(8,128)(2,1)S(1)}, bf16[4,4,80,128]{3,2,1,0:T(8,128)(2,1)S(1)}, u32[]{:S(2)}, u32[]{:S(2)}) collective-permute-start(bf16[4,4,80,128]{3,2,1,0:T(8,128)(2,1)S(1)} %pad_maximum_fusion.refs_0_), channel_id=1, source_target_pairs={{0,2},{1,3},{2,0},{3,1},{4,6},{5,7},{6,4},{7,5},{8,10},{9,11},{10,... | collective-permute-start | bytes 983048 | tf_op jit(solution)/shard_map/ppermute | solution.py:68
  150.6 25.1 %collective-permute-start.19 = (bf16[4,4,80,128]{3,2,1,0:T(8,128)(2,1)S(1)}, bf16[4,4,80,128]{3,2,1,0:T(8,128)(2,1)S(1)}, u32[]{:S(2)}, u32[]{:S(2)}) collective-permute-start(bf16[4,4,80,128]{3,2,1,0:T(8,128)(2,1)S(1)} %pad_maximum_fusion.refs_0_), channel_id=1, source_target_pairs={{0,3},{1,0},{2,1},{3,2},{4,7},{5,4},{6,5},{7,6},{8,11},{9,8},{10,9... | collective-permute-start | bytes 983048 | tf_op jit(solution)/shard_map/ppermute | solution.py:68
  171.8 7.3 %collective-permute-start.3 = (bf16[192,512]{1,0:T(8,128)(2,1)S(1)}, bf16[192,512]{1,0:T(8,128)(2,1)S(1)}, u32[]{:S(2)}, u32[]{:S(2)}) collective-permute-start(bf16[192,512]{1,0:T(8,128)(2,1)S(1)} %fusion.29), channel_id=1, source_target_pairs={{0,64},{64,128},{128,192},{192,256},{256,320},{320,384},{384,448},... | collective-permute-start | bytes 589832 | tf_op jit(solution)/shard_map/ppermute | solution.py:63
Sparse Core Ops, SparseCore 0:
  11.1 54.2 all-gather.2
  79.9 64.7 reduce-scatter.1

commit v2 on v1

--- a/solution.py
+++ b/solution.py
@@ -118,48 +118,85 @@
     return total
 
 
-def own_tokens(base, group_rows):
-    count = lax.axis_size("section")
-    own = lax.axis_index("section")
-
-    def rows_of(section):
-        return lax.dynamic_slice_in_dim(base, section * group_rows, group_rows, axis=0)
-
-    total = jnp.where(own % BLOCK == 0, rows_of(own), 0)
-    for position in range(BLOCK):
-        if position != 1:
-            pairs = [
-                (relay, block_place(position, relay, count)) for relay in range(0, count, BLOCK)
-            ]
-            target = lax.rem(own + position - 1 + count, count)
-            total = total + lax.ppermute(rows_of(target), "section", pairs)
-    return total
-
-
-def place_kernel(replicas, per_block, own_ref, *refs):
+def place_kernel(shape, own_ref, *refs):
+    per_block, rows, width = shape
     pieces, out_ref = refs[:-1], refs[-1]
     position, replica = own_ref[0], own_ref[1]
-    width = pieces[0].shape[3]
+    replicas = len(pieces)
     for step in range(replicas):
         source = lax.rem(replica - step + replicas, replicas)
         for back in range(BLOCK):
             place = lax.rem(position - back + BLOCK, BLOCK)
             for j in range(per_block):
+                first = (back * per_block + j) * rows
                 column = ((place * per_block + j) * replicas + source) * width
-                out_ref[:, pl.ds(pl.multiple_of(column, width), width)] = pieces[step][back, j]
-
-
-def place_columns(own, pieces):
+                out_ref[:, pl.ds(pl.multiple_of(column, width), width)] = pieces[step][
+                    first : first + rows, :
+                ]
+
+
+def place_columns(own, pieces, shape):
     replicas = len(pieces)
-    block, per_block, rows, width = pieces[0].shape
+    per_block, rows, width = shape
     return pl.pallas_call(
-        functools.partial(place_kernel, replicas, per_block),
-        out_shape=jax.ShapeDtypeStruct((rows, replicas * block * per_block * width), jnp.bfloat16),
+        functools.partial(place_kernel, shape),
+        out_shape=jax.ShapeDtypeStruct((rows, replicas * BLOCK * per_block * width), jnp.bfloat16),
         in_specs=[pl.BlockSpec(memory_space=pltpu.SMEM)]
         + [pl.BlockSpec(memory_space=pltpu.VMEM)] * replicas,
         out_specs=pl.BlockSpec(memory_space=pltpu.VMEM),
         compiler_params=pltpu.CompilerParams(vmem_limit_bytes=16 * 1024 * 1024),
     )(own, *pieces)
+
+
+def section_kernel(cotangent_ref, inputs_ref, weight_ref, upstream_ref, product_ref, grad_ref, total):
+    step = pl.program_id(0)
+
+    @pl.when(step == 0)
+    def _():
+        total[...] = upstream_ref[...].astype(jnp.float32)
+
+    total[...] += lax.dot_general(
+        cotangent_ref[...],
+        weight_ref[...],
+        (((1,), (1,)), ((), ())),
+        preferred_element_type=jnp.float32,
+    )
+    product_ref[...] = jnp.dot(
+        inputs_ref[...], weight_ref[...], preferred_element_type=jnp.float32
+    ).astype(jnp.bfloat16)
+
+    @pl.when(step == pl.num_programs(0) - 1)
+    def _():
+        grad_ref[...] = total[...].astype(jnp.bfloat16)
+
+
+def section_products(cotangent, inputs, weight, upstream):
+    tokens, rows = inputs.shape
+    width = weight.shape[1]
+    tile = 2048
+    whole = pl.BlockSpec((tokens, rows), lambda n: (0, 0))
+    return pl.pallas_call(
+        section_kernel,
+        grid=(width // tile,),
+        in_specs=[
+            pl.BlockSpec((tokens, tile), lambda n: (0, n)),
+            whole,
+            pl.BlockSpec((rows, tile), lambda n: (0, n)),
+            whole,
+        ],
+        out_specs=[pl.BlockSpec((tokens, tile), lambda n: (0, n)), whole],
+        out_shape=[
+            jax.ShapeDtypeStruct((tokens, width), jnp.bfloat16),
+            jax.ShapeDtypeStruct((tokens, rows), jnp.bfloat16),
+        ],
+        scratch_shapes=[pltpu.VMEM((tokens, rows), jnp.float32)],
+        compiler_params=pltpu.CompilerParams(vmem_limit_bytes=56 * 1024 * 1024),
+        cost_estimate=pl.CostEstimate(
+            flops=4 * tokens * rows * width,
+            bytes_accessed=2 * (rows * width + 2 * tokens * width),
+            transcendentals=0,
+        ),
+    )(cotangent, inputs, weight, upstream)
 
 
 def local(
@@ -205,80 +242,92 @@
     slot_table = (visual_slot[0][:, None] == columns[None, :]).astype(jnp.bfloat16)
     past_table = (past_slot[0][:, None] == columns[None, :]).astype(jnp.bfloat16)
 
-    past_all = [past_heads] + [rotate(past_heads, "dp", step) for step in range(1, replica_count)]
-
     terms = jnp.dot(current, visual_proj, preferred_element_type=jnp.float32).astype(jnp.bfloat16)
     terms = lax.all_to_all(
         terms.reshape(group_rows, tensor_count, model_rows), "tensor", 1, 1, tiled=True
     )
     embedded = jnp.sum(terms.astype(jnp.float32), axis=1).astype(jnp.bfloat16)
-    spare = jnp.zeros((group_rows, -(head_rows * replica_count) % 128), jnp.bfloat16)
+    spare = jnp.zeros((group_rows, -head_rows % 128), jnp.bfloat16)
     parcel = lax.all_gather(
-        jnp.concatenate([embedded, *past_all, spare], axis=1), "section", axis=0, tiled=True
+        jnp.concatenate([embedded, past_heads, spare], axis=1), "section", axis=0, tiled=True
     )
     visual_rows = parcel[:, :model_rows]
-    past_rows = jnp.concatenate(
-        [
-            parcel[:, model_rows + step * head_rows : model_rows + (step + 1) * head_rows]
-            for step in range(replica_count)
-        ],
-        axis=0,
-    )
+    past_rows = parcel[:, model_rows : model_rows + head_rows]
     placed = lax.dot_general(
         slot_table, visual_rows, (((0,), (0,)), ((), ())), preferred_element_type=jnp.float32
     ).astype(jnp.bfloat16)
     covered = jnp.sum(slot_table, axis=0, dtype=jnp.float32)
     inputs = jnp.where(first_flag & (covered[:, None] > 0.5), placed, layer_input[0].T)
 
-    input_grad = (
-        upstream
-        + lax.dot_general(
-            pre_full, weight, (((1,), (1,)), ((), ())), preferred_element_type=jnp.float32
-        )
-    ).astype(jnp.bfloat16)
+    products, input_grad = section_products(pre_full, inputs, weight, layer_cotangent[0].T)
+    preact = lax.psum_scatter(products, "tensor", scatter_dimension=1, tiled=True).astype(
+        jnp.float32
+    )
+    hidden = (inputs.astype(jnp.float32) + jax.nn.silu(preact)).astype(jnp.bfloat16)
+    forward_out = shift(hidden, "section", 1)
+    backward_out = shift(input_grad, "section", -1)
+
     visual_grad = jnp.dot(past_table, input_grad, preferred_element_type=jnp.float32).astype(
         jnp.bfloat16
     )
-
-    inputs, visual_grad = lax.optimization_barrier((inputs, visual_grad))
-    products = jnp.dot(inputs, weight, preferred_element_type=jnp.float32).astype(jnp.bfloat16)
-    preact = lax.psum_scatter(products, "tensor", scatter_dimension=1, tiled=True).astype(
-        jnp.float32
-    )
-    hidden = (inputs.astype(jnp.float32) + jax.nn.silu(preact)).astype(jnp.bfloat16)
-    forward_out = shift(hidden, "section", 1)
-
-    backward_out = shift(input_grad, "section", -1)
     base = to_relays(visual_grad)
-    piece = spread_columns(base)
-    own_grad = own_tokens(base, group_rows)
-    gathered = lax.all_gather(piece, "tensor", axis=0)
+    gathered = lax.all_gather(spread_columns(base), "tensor", axis=0)
+    past_rows = jnp.concatenate(
+        [past_rows] + [rotate(past_rows, "dp", step) for step in range(1, replica_count)], axis=0
+    )
     per_block = tensor_count // BLOCK
-    gathered = gathered.reshape(per_block, replica_count * visual_count, model_rows // replica_count)
-    own_columns = jnp.stack(
-        [
+    part_width = model_rows // replica_count
+    position, replica = lax.rem(own_section + 1, BLOCK), lax.axis_index("dp")
+    gathered = gathered.reshape(per_block, replica_count * visual_count, part_width)
+    own_columns, head_part = [], 0.0
+    for j in range(per_block):
+        own_columns.append(
             lax.dot_general(
                 past_rows, gathered[j], (((0,), (0,)), ((), ())), preferred_element_type=jnp.float32
             ).astype(jnp.bfloat16)
-            for j in range(per_block)
-        ]
-    )
-    in_block = jnp.stack(
-        [own_columns]
-        + [
-            rotate(own_columns, "section", step if step <= BLOCK // 2 else step - BLOCK)
-            for step in range(1, BLOCK)
-        ]
-    )
-    in_block, own_grad = lax.optimization_barrier((in_block, own_grad))
-    pieces = [in_block] + [rotate(in_block, "dp", step) for step in range(1, replica_count)]
-    position = jnp.stack([lax.rem(own_section + 1, BLOCK), lax.axis_index("dp")]).astype(jnp.int32)
-    grad_proj = place_columns(position, pieces)
-
-    own_full = lax.all_gather(own_grad, "tensor", axis=1, tiled=True)
-    head_grad = lax.dot_general(
-        own_full, visual_proj, (((1,), (1,)), ((), ())), preferred_element_type=jnp.float32
-    ).astype(jnp.bfloat16)
+        )
+        proj_part = lax.dynamic_slice_in_dim(
+            visual_proj,
+            (position * per_block + j) * model_rows + replica * part_width,
+            part_width,
+            axis=1,
+        )
+        proj_part = jnp.pad(proj_part, ((0, part_width - head_rows), (0, 0)))
+        head_part = head_part + lax.dot_general(
+            gathered[j], proj_part, (((1,), (1,)), ((), ())), preferred_element_type=jnp.float32
+        )
+    own_columns = jnp.concatenate(own_columns, axis=0)
+    head_part = head_part.astype(jnp.bfloat16).reshape(
+        replica_count, section_count, group_rows, part_width
+    )
+
+    def head_of(section):
+        return lax.dynamic_index_in_dim(head_part, section, axis=1, keepdims=False).reshape(
+            replica_count * group_rows, part_width
+        )
+
+    column_rows = own_columns.shape[0]
+    in_block, head_sum = [own_columns], head_of(own_section).astype(jnp.float32)
+    for step in range(1, BLOCK):
+        hops = step if step <= BLOCK // 2 else step - BLOCK
+        target = lax.rem(own_section + hops + section_count, section_count)
+        arrived = rotate(
+            jnp.concatenate([own_columns, head_of(target)], axis=0), "section", hops
+        )
+        in_block.append(arrived[:column_rows])
+        head_sum = head_sum + arrived[column_rows:].astype(jnp.float32)
+
+    bundle = jnp.concatenate(in_block + [head_sum.astype(jnp.bfloat16)], axis=0)
+    pieces, head_grad = [bundle], head_sum[:group_rows]
+    for step in range(1, replica_count):
+        arrived = rotate(bundle, "dp", step)
+        first = BLOCK * column_rows + (replica_count - step) * group_rows
+        head_grad = head_grad + arrived[first : first + group_rows].astype(jnp.float32)
+        pieces.append(arrived)
+    head_grad = head_grad[:, :head_rows].astype(jnp.bfloat16)
+    grad_proj = place_columns(
+        jnp.stack([position, replica]).astype(jnp.int32), pieces, (per_block, head_rows, part_width)
+    )
     frame_grads = attend_grad(past_saved, head_grad)
     return (forward_out.T[None], backward_out.T[None], grad_proj, frame_grads[:, None, None])
 

time: 188 us -> 191 us (1.016)
  waiting for transfers between devices: 18.6 us -> 41 us
  blocking collectives: 61.2 us -> 48.6 us
  matrix products: 18.9 us -> 6.54 us
  Pallas kernels: 1.98 us -> 11 us
  starting transfers between devices: 65.5 us -> 60.2 us
    dot_general x3 -> x4, matrix products: 14.5 us -> 0.77 us  [local(): lax.dot_general(gathered[j], proj_part, (((1,), (1,)), ((), ())), preferr...]
    all_gather x3 -> x2, blocking collectives: 61.2 us -> 48.6 us  [the longest x1 24.7 us: local(): lax.all_gather(jnp.concatenate([embedded, past_heads, spare], axis=1), 's...]
    ppermute x9, waiting for transfers between devices: 5.52 us -> 16.4 us  [rotate(): lax.ppermute(value, axis, [(i, (i + steps) % count) for i in range(count)])]
    pallas_call x1 -> x2, Pallas kernels: 1.98 us -> 11 us  [the longest x1 8.98 us: section_products(): pl.pallas_call(section_kernel, grid=(width // tile,), in_specs=[pl.BlockS...]
    all_to_all x1, waiting for transfers between devices: 2.85 us -> 11.2 us  [local(): lax.all_to_all(terms.reshape(group_rows, tensor_count, model_rows), 'tens...]
    ppermute x2, waiting for transfers between devices: 1.39 us -> 8.2 us  [shift(): lax.ppermute(value, axis, [(source, source + steps) for source in range(f...]
    ppermute x4, waiting for transfers between devices: 4.95 us -> 0.01 us  [spread_columns(): piece = lax.ppermute(part, ('section', 'tensor', 'dp'), pairs)]
    ppermute x3 -> x0, starting transfers between devices: 3.87 us -> none  [own_tokens(): total = total + lax.ppermute(rows_of(target), 'section', pairs)]
  transfers between devices with their start and end apart: 23 -> 20, of which waited for: 8 -> 10; matrix products, arithmetic and copies ran while one was open for 4% -> 5% of each run, Pallas kernels for 1% -> 1%
where the time goes in v2:
time: 191 us; the launch traced here: 190 us
  starting transfers between devices  60.2 us (32%)
  blocking collectives  48.6 us (25%)
  waiting for transfers between devices  41 us (21%)
  between operations  14.6 us (8%)
  Pallas kernels  11 us (6%)
  matrix products  6.54 us (3%)
  local copies, waits for them, and re-layouts  4.09 us (2%)
  other arithmetic  3.93 us (2%)
    ppermute x9, starting transfers between devices, rotate(): lax.ppermute(value, axis, [(i, (i + steps) % count) for i in range(count)])  26.6 us
    all_gather x1, blocking collectives, local(): lax.all_gather(jnp.concatenate([embedded, past_heads, spare], axis=1), 's...  24.7 us
    all_gather x1, blocking collectives, local(): gathered = lax.all_gather(spread_columns(base), 'tensor', axis=0)  23.9 us
    ppermute x9, waiting for transfers between devices, rotate(): lax.ppermute(value, axis, [(i, (i + steps) % count) for i in range(count)])  16.4 us
    all_to_all x1, starting transfers between devices, local(): lax.all_to_all(terms.reshape(group_rows, tensor_count, model_rows), 'tens...  13.8 us
    all_to_all x1, waiting for transfers between devices, local(): lax.all_to_all(terms.reshape(group_rows, tensor_count, model_rows), 'tens...  11.2 us
    ppermute x2, starting transfers between devices, to_relays(): lax.ppermute(value, 'section', [(0, relay)])  9.76 us
    pallas_call x1, Pallas kernels, section_products(): pl.pallas_call(section_kernel, grid=(width // tile,), in_specs=[pl.BlockS...  8.98 us
  transfers between devices with their start and end apart: 20, of which 10 were waited for; matrix products, arithmetic and copies ran while one was open for 5% of the time, Pallas kernels for 1%

profile of v2, /device:TPU:1, one launch (start us, length us, event | category | flops | bytes accessed | tf_op | source)
XLA Modules:
  0.0 189.8 jit_solution(15856371785336932166)
XLA Ops:
  7.2 1.9 fusion.18
  10.1 1.8 convolution_convert_fusion
  12.6 13.8 %all-to-all-start = ((bf16[16,16,512]{2,0,1:T(8,128)(2,1)}), bf16[16,16,512]{2,0,1:T(8,128)(2,1)S(1)}, u32[]{:S(2)}, u32[]{:S(2)}) async-start(bf16[16,16,512]{2,0,1:T(8,128)(2,1)} %bitcast.117), calls=%async_computation | async-start | bytes 524288 | tf_op jit(solution)/shard_map/all_to_all | solution.py:246
  27.1 11.2 %all-to-all-done = bf16[16,16,512]{2,0,1:T(8,128)(2,1)S(1)} async-done(((bf16[16,16,512]{2,0,1:T(8,128)(2,1)}), bf16[16,16,512]{2,0,1:T(8,128)(2,1)S(1)}, u32[]{:S(2)}, u32[]{:S(2)}) %all-to-all-start) | async-done | bytes 262176 | tf_op jit(solution)/shard_map/all_to_all | solution.py:246
  38.4 24.7 %all_gather.12 = bf16[192,640]{1,0:T(8,128)(2,1)S(1)} all-gather(bf16[16,640]{1,0:T(8,128)(2,1)S(1)} %maximum_maximum_fusion), channel_id=1, replica_groups=mesh['section'=12,'tensor'=16,'dp'=4] {'section'}, dimensions={0}, use_global_device_ids=true | all-gather | bytes 266240 | tf_op jit(solution)/shard_map/all_gather | solution.py:251
  65.3 9.0 %shard_map.174 = (bf16[192,8192]{1,0:T(8,128)(2,1)}, bf16[192,512]{1,0:T(8,128)(2,1)}) custom-call(bf16[192,8192]{1,0:T(8,128)(2,1)} %all-gather.3.cloned.1.call-done.cotangent_ref, bf16[192,512]{1,0:T(8,128)(2,1)} %fusion.3.inputs_ref, bf16[512,8192]{1,0:T(8,128)(2,1)} %bitcast.118, bf16[192,512]{1,0:T(8,128)(2,1)} %bitcast.120), custom_call_target="tpu_custom_call" | custom-call | flops 3221225472 | bytes 14680064 | tf_op jit(solution)/shard_map/pallas_call | solution.py:178
  75.5 8.5 %collective-permute-start.6 = (bf16[192,512]{1,0:T(8,128)(2,1)S(1)}, bf16[192,512]{1,0:T(8,128)(2,1)S(1)}, u32[]{:S(2)}, u32[]{:S(2)}) collective-permute-start(bf16[192,512]{1,0:T(8,128)(2,1)S(1)} %convolution_convert_fusion.1), channel_id=1, source_target_pairs={{0,512},{1,513},{2,514},{3,515},{4,516},{5,517},{6,518},{7,519},{8... | collective-permute-start | bytes 589832 | tf_op jit(solution)/shard_map/ppermute | solution.py:78
  83.9 1.3 collective-permute-start.5
  85.3 2.6 %collective-permute-done.6 = bf16[192,512]{1,0:T(8,128)(2,1)S(1)} collective-permute-done((bf16[192,512]{1,0:T(8,128)(2,1)S(1)}, bf16[192,512]{1,0:T(8,128)(2,1)S(1)}, u32[]{:S(2)}, u32[]{:S(2)}) %collective-permute-start.6) | collective-permute-done | bytes 196640 | tf_op jit(solution)/shard_map/ppermute | solution.py:78
  87.9 1.3 collective-permute-done.5
  89.3 1.3 collective-permute-start.10
  90.6 1.3 collective-permute-start.9
  91.9 1.3 collective-permute-start.7
  93.2 1.9 %collective-permute-start.8 = (bf16[192,128]{1,0:T(8,128)(2,1)S(1)}, bf16[192,128]{1,0:T(8,128)(2,1)S(1)}, u32[]{:S(2)}, u32[]{:S(2)}) collective-permute-start(bf16[192,128]{1,0:T(8,128)(2,1)S(1)} %get-tuple-element.28), channel_id=1, source_target_pairs={{0,709},{1,710},{2,711},{3,708},{4,725},{5,726},{6,727},{7,724},{8... | collective-permute-start | bytes 147464 | tf_op jit(solution)/shard_map/ppermute | solution.py:116
  96.0 4.4 %collective-permute-start.4 = (bf16[192,80]{1,0:T(8,128)(2,1)S(1)}, bf16[192,80]{1,0:T(8,128)(2,1)S(1)}, u32[]{:S(2)}, u32[]{:S(2)}) collective-permute-start(bf16[192,80]{1,0:T(8,128)(2,1)S(1)} %slice.82), channel_id=1, source_target_pairs={{0,3},{1,0},{2,1},{3,2},{4,7},{5,4},{6,5},{7,6},{8,11},{9,8},{10,9... | collective-permute-start | bytes 92168 | tf_op jit(solution)/shard_map/ppermute | solution.py:68
  100.4 2.5 %collective-permute-start.3 = (bf16[192,80]{1,0:T(8,128)(2,1)S(1)}, bf16[192,80]{1,0:T(8,128)(2,1)S(1)}, u32[]{:S(2)}, u32[]{:S(2)}) collective-permute-start(bf16[192,80]{1,0:T(8,128)(2,1)S(1)} %slice.82), channel_id=1, source_target_pairs={{0,2},{1,3},{2,0},{3,1},{4,6},{5,7},{6,4},{7,5},{8,10},{9,11},{10,... | collective-permute-start | bytes 92168 | tf_op jit(solution)/shard_map/ppermute | solution.py:68
  102.8 2.5 %collective-permute-start.2 = (bf16[192,80]{1,0:T(8,128)(2,1)S(1)}, bf16[192,80]{1,0:T(8,128)(2,1)S(1)}, u32[]{:S(2)}, u32[]{:S(2)}) collective-permute-start(bf16[192,80]{1,0:T(8,128)(2,1)S(1)} %slice.82), channel_id=1, source_target_pairs={{0,1},{1,2},{2,3},{3,0},{4,5},{5,6},{6,7},{7,4},{8,9},{9,10},{10,1... | collective-permute-start | bytes 92168 | tf_op jit(solution)/shard_map/ppermute | solution.py:68
  105.4 23.9 %all-gather = bf16[3072,128]{1,0:T(8,128)(2,1)S(1)} all-gather(bf16[192,128]{1,0:T(8,128)(2,1)S(1)} %add_add_fusion.1), channel_id=2, replica_groups=mesh['section'=12,'tensor'=16,'dp'=4] {'tensor'}, dimensions={0}, use_global_device_ids=true | all-gather | bytes 835584 | tf_op jit(solution)/shard_map/all_gather | solution.py:274
  131.1 1.9 %collective-permute-start.11 = (bf16[384,128]{1,0:T(8,128)(2,1)S(1)}, bf16[384,128]{1,0:T(8,128)(2,1)S(1)}, u32[]{:S(2)}, u32[]{:S(2)}) collective-permute-start(bf16[384,128]{1,0:T(8,128)(2,1)S(1)} %constant_dynamic-update-slice_fusion), channel_id=1, source_target_pairs={{0,64},{64,128},{128,192},{192,256},{256,320},{320,384},{384,448},... | collective-permute-start | bytes 294920 | tf_op jit(solution)/shard_map/ppermute | solution.py:68
  133.0 1.9 %collective-permute-start.12 = (bf16[384,128]{1,0:T(8,128)(2,1)S(1)}, bf16[384,128]{1,0:T(8,128)(2,1)S(1)}, u32[]{:S(2)}, u32[]{:S(2)}) collective-permute-start(bf16[384,128]{1,0:T(8,128)(2,1)S(1)} %constant_dynamic-update-slice_fusion.5), channel_id=1, source_target_pairs={{0,128},{64,192},{128,256},{192,320},{256,384},{320,448},{384,512}... | collective-permute-start | bytes 294920 | tf_op jit(solution)/shard_map/ppermute | solution.py:68
  134.9 4.6 %collective-permute-start.13 = (bf16[384,128]{1,0:T(8,128)(2,1)S(1)}, bf16[384,128]{1,0:T(8,128)(2,1)S(1)}, u32[]{:S(2)}, u32[]{:S(2)}) collective-permute-start(bf16[384,128]{1,0:T(8,128)(2,1)S(1)} %constant_dynamic-update-slice_fusion.10), channel_id=1, source_target_pairs={{0,704},{64,0},{128,64},{192,128},{256,192},{320,256},{384,320},{4... | collective-permute-start | bytes 294920 | tf_op jit(solution)/shard_map/ppermute | solution.py:68
  139.6 1.8 collective-permute-done.12
  141.4 5.0 %collective-permute-done.13 = bf16[384,128]{1,0:T(8,128)(2,1)S(1)} collective-permute-done((bf16[384,128]{1,0:T(8,128)(2,1)S(1)}, bf16[384,128]{1,0:T(8,128)(2,1)S(1)}, u32[]{:S(2)}, u32[]{:S(2)}) %collective-permute-start.13) | collective-permute-done | bytes 98336 | tf_op jit(solution)/shard_map/ppermute | solution.py:68
  146.4 4.5 %collective-permute-start.16 = (bf16[1344,128]{1,0:T(8,128)(2,1)S(1)}, bf16[1344,128]{1,0:T(8,128)(2,1)S(1)}, u32[]{:S(2)}, u32[]{:S(2)}) collective-permute-start(bf16[1344,128]{1,0:T(8,128)(2,1)S(1)} %get-tuple-element.44.refs_0_), channel_id=1, source_target_pairs={{0,3},{1,0},{2,1},{3,2},{4,7},{5,4},{6,5},{7,6},{8,11},{9,8},{10,9... | collective-permute-start | bytes 1032200 | tf_op jit(solution)/shard_map/ppermute | solution.py:68
  150.9 2.5 %collective-permute-start.15 = (bf16[1344,128]{1,0:T(8,128)(2,1)S(1)}, bf16[1344,128]{1,0:T(8,128)(2,1)S(1)}, u32[]{:S(2)}, u32[]{:S(2)}) collective-permute-start(bf16[1344,128]{1,0:T(8,128)(2,1)S(1)} %get-tuple-element.44.refs_0_), channel_id=1, source_target_pairs={{0,2},{1,3},{2,0},{3,1},{4,6},{5,7},{6,4},{7,5},{8,10},{9,11},{10,... | collective-permute-start | bytes 1032200 | tf_op jit(solution)/shard_map/ppermute | solution.py:68
  153.4 1.9 %collective-permute-start.14 = (bf16[1344,128]{1,0:T(8,128)(2,1)S(1)}, bf16[1344,128]{1,0:T(8,128)(2,1)S(1)}, u32[]{:S(2)}, u32[]{:S(2)}) collective-permute-start(bf16[1344,128]{1,0:T(8,128)(2,1)S(1)} %get-tuple-element.44.refs_0_), channel_id=1, source_target_pairs={{0,1},{1,2},{2,3},{3,0},{4,5},{5,6},{6,7},{7,4},{8,9},{9,10},{10,1... | collective-permute-start | bytes 1032200 | tf_op jit(solution)/shard_map/ppermute | solution.py:68
  155.3 1.3 collective-permute-start.1
  156.7 5.3 %collective-permute-done.1 = bf16[192,512]{1,0:T(8,128)(2,1)S(1)} collective-permute-done((bf16[192,512]{1,0:T(8,128)(2,1)S(1)}, bf16[192,512]{1,0:T(8,128)(2,1)S(1)}, u32[]{:S(2)}, u32[]{:S(2)}) %collective-permute-start.1) | collective-permute-done | bytes 196640 | tf_op jit(solution)/shard_map/ppermute | solution.py:63
  162.3 9.3 %collective-permute-done.14.refs_1_ = bf16[1344,128]{1,0:T(8,128)(2,1)S(1)} collective-permute-done((bf16[1344,128]{1,0:T(8,128)(2,1)S(1)}, bf16[1344,128]{1,0:T(8,128)(2,1)S(1)}, u32[]{:S(2)}, u32[]{:S(2)}) %collective-permute-start.14) | collective-permute-done | bytes 344096 | tf_op jit(solution)/shard_map/ppermute | solution.py:68
  171.7 2.0 %shard_map.175 = bf16[80,8192]{1,0:T(8,128)(2,1)} custom-call(s32[2]{0:T(128)S(1)} %pad_add_fusion.own_ref, bf16[1344,128]{1,0:T(8,128)(2,1)S(1)} %get-tuple-element.44.refs_0_, bf16[1344,128]{1,0:T(8,128)(2,1)S(1)} %collective-permute-done.14.refs_1_, bf16[1344,128]{1,0:T(8,128)(2,1)S(1)} %collective-permute-done.15.refs_2_, ...), custom_call_target="tpu_custom_call" | custom-call | tf_op jit(solution)/shard_map/pallas_call | solution.py:141
  175.2 2.8 %collective-permute-start = (bf16[192,512]{1,0:T(8,128)(2,1)S(1)}, bf16[192,512]{1,0:T(8,128)(2,1)S(1)}, u32[]{:S(2)}, u32[]{:S(2)}) collective-permute-start(bf16[192,512]{1,0:T(8,128)(2,1)S(1)} %fusion.19), channel_id=1, source_target_pairs={{0,64},{64,128},{128,192},{192,256},{256,320},{320,384},{384,448},... | collective-permute-start | bytes 589832 | tf_op jit(solution)/shard_map/ppermute | solution.py:63
  178.7 2.9 %collective-permute-done = bf16[192,512]{1,0:T(8,128)(2,1)S(1)} collective-permute-done((bf16[192,512]{1,0:T(8,128)(2,1)S(1)}, bf16[192,512]{1,0:T(8,128)(2,1)S(1)}, u32[]{:S(2)}, u32[]{:S(2)}) %collective-permute-start) | collective-permute-done | bytes 196640 | tf_op jit(solution)/shard_map/ppermute | solution.py:63
  (87 shorter events, 12.5 us)
Async XLA Ops:
  7.2 2.9 %copy-start = (bf16[1,1,80,16]{2,3,1,0:T(8,128)(2,1)S(1)}, bf16[1,1,80,16]{2,3,1,0:T(8,128)(2,1)}, u32[]{:S(2)}) copy-start(bf16[1,1,80,16]{2,3,1,0:T(8,128)(2,1)} %param.17) | copy-start | bytes 7684
  7.2 58.1 %all-gather.3.cloned.1.call-start = ((), (), s32[]{:S(2)}) async-start(), calls=%async_computation.2 | async-start | bytes 3342336 | tf_op jit(solution)/shard_map/all_gather | solution.py:233
  10.0 16.5 %copy-start.4 = (s32[1,192]{1,0:T(1,128)S(1)}, s32[1,192]{1,0:T(1,128)}, u32[]{:S(2)}) copy-start(s32[1,192]{1,0:T(1,128)} %param.23) | copy-start | bytes 2308
  10.0 16.6 %copy-start.7 = (bf16[1,1,80,16]{2,3,1,0:T(8,128)(2,1)S(1)}, bf16[1,1,80,16]{2,3,1,0:T(8,128)(2,1)}, u32[]{:S(2)}) copy-start(bf16[1,1,80,16]{2,3,1,0:T(8,128)(2,1)} %param.19) | copy-start | bytes 7684
  10.0 16.6 %copy-start.8 = (bf16[1,1,80,16]{2,3,1,0:T(8,128)(2,1)S(1)}, bf16[1,1,80,16]{2,3,1,0:T(8,128)(2,1)}, u32[]{:S(2)}) copy-start(bf16[1,1,80,16]{2,3,1,0:T(8,128)(2,1)} %param.20) | copy-start | bytes 7684
  10.1 16.6 %copy-start.9 = (s32[1,1,16]{2,1,0:T(1,128)S(1)}, s32[1,1,16]{2,1,0:T(1,128)}, u32[]{:S(2)}) copy-start(s32[1,1,16]{2,1,0:T(1,128)} %param.22) | copy-start | bytes 196
  10.1 16.9 %copy-start.6 = (bf16[1,1,80,16]{2,3,1,0:T(8,128)(2,1)S(1)}, bf16[1,1,80,16]{2,3,1,0:T(8,128)(2,1)}, u32[]{:S(2)}) copy-start(bf16[1,1,80,16]{2,3,1,0:T(8,128)(2,1)} %param.21) | copy-start | bytes 7684
  10.1 53.0 %copy-start.5 = (bf16[1,512,192]{1,2,0:T(8,128)(2,1)S(1)}, bf16[1,512,192]{1,2,0:T(8,128)(2,1)}, u32[]{:S(2)}) copy-start(bf16[1,512,192]{1,2,0:T(8,128)(2,1)} %param.27) | copy-start | bytes 589828
  12.6 25.7 %all-to-all-start = ((bf16[16,16,512]{2,0,1:T(8,128)(2,1)}), bf16[16,16,512]{2,0,1:T(8,128)(2,1)S(1)}, u32[]{:S(2)}, u32[]{:S(2)}) async-start(bf16[16,16,512]{2,0,1:T(8,128)(2,1)} %bitcast.117), calls=%async_computation | async-start | bytes 524288 | tf_op jit(solution)/shard_map/all_to_all | solution.py:246
  26.5 147.6 %reduce-scatter.2.cloned.1.call-start = ((), (), s32[]{:S(2)}) async-start(), calls=%async_computation.3 | async-start | bytes 3342336 | tf_op jit(solution)/shard_map/reduce_scatter | solution.py:263
  74.3 0.9 copy-start.2
  74.3 0.9 copy-start.3
  75.5 12.5 %collective-permute-start.6 = (bf16[192,512]{1,0:T(8,128)(2,1)S(1)}, bf16[192,512]{1,0:T(8,128)(2,1)S(1)}, u32[]{:S(2)}, u32[]{:S(2)}) collective-permute-start(bf16[192,512]{1,0:T(8,128)(2,1)S(1)} %convolution_convert_fusion.1), channel_id=1, source_target_pairs={{0,512},{1,513},{2,514},{3,515},{4,516},{5,517},{6,518},{7,519},{8... | collective-permute-start | bytes 589832 | tf_op jit(solution)/shard_map/ppermute | solution.py:78
  83.9 5.3 %collective-permute-start.5 = (bf16[192,512]{1,0:T(8,128)(2,1)S(1)}, bf16[192,512]{1,0:T(8,128)(2,1)S(1)}, u32[]{:S(2)}, u32[]{:S(2)}) collective-permute-start(bf16[192,512]{1,0:T(8,128)(2,1)S(1)} %convolution_convert_fusion.1), channel_id=1, source_target_pairs={{0,256},{1,257},{2,258},{3,259},{4,260},{5,261},{6,262},{7,263},{8... | collective-permute-start | bytes 589832 | tf_op jit(solution)/shard_map/ppermute | solution.py:78
  89.3 11.0 %collective-permute-start.10 = (bf16[192,128]{1,0:T(8,128)(2,1)S(1)}, bf16[192,128]{1,0:T(8,128)(2,1)S(1)}, u32[]{:S(2)}, u32[]{:S(2)}) collective-permute-start(bf16[192,128]{1,0:T(8,128)(2,1)S(1)} %get-tuple-element.29), channel_id=1, source_target_pairs={{0,719},{1,716},{2,717},{3,718},{4,735},{5,732},{6,733},{7,734},{8... | collective-permute-start | bytes 147464 | tf_op jit(solution)/shard_map/ppermute | solution.py:116
  90.6 12.2 %collective-permute-start.9 = (bf16[192,128]{1,0:T(8,128)(2,1)S(1)}, bf16[192,128]{1,0:T(8,128)(2,1)S(1)}, u32[]{:S(2)}, u32[]{:S(2)}) collective-permute-start(bf16[192,128]{1,0:T(8,128)(2,1)S(1)} %get-tuple-element.30), channel_id=1, source_target_pairs={{0,714},{1,715},{2,712},{3,713},{4,730},{5,731},{6,728},{7,729},{8... | collective-permute-start | bytes 147464 | tf_op jit(solution)/shard_map/ppermute | solution.py:116
  91.9 13.4 %collective-permute-start.7 = (bf16[192,128]{1,0:T(8,128)(2,1)S(1)}, bf16[192,128]{1,0:T(8,128)(2,1)S(1)}, u32[]{:S(2)}, u32[]{:S(2)}) collective-permute-start(bf16[192,128]{1,0:T(8,128)(2,1)S(1)} %get-tuple-element.31), channel_id=1, source_target_pairs={{0,704},{1,705},{2,706},{3,707},{4,720},{5,721},{6,722},{7,723},{8... | collective-permute-start | bytes 147464 | tf_op jit(solution)/shard_map/ppermute | solution.py:116
  93.2 12.1 %collective-permute-start.8 = (bf16[192,128]{1,0:T(8,128)(2,1)S(1)}, bf16[192,128]{1,0:T(8,128)(2,1)S(1)}, u32[]{:S(2)}, u32[]{:S(2)}) collective-permute-start(bf16[192,128]{1,0:T(8,128)(2,1)S(1)} %get-tuple-element.28), channel_id=1, source_target_pairs={{0,709},{1,710},{2,711},{3,708},{4,725},{5,726},{6,727},{7,724},{8... | collective-permute-start | bytes 147464 | tf_op jit(solution)/shard_map/ppermute | solution.py:116
  96.0 33.2 %collective-permute-start.4 = (bf16[192,80]{1,0:T(8,128)(2,1)S(1)}, bf16[192,80]{1,0:T(8,128)(2,1)S(1)}, u32[]{:S(2)}, u32[]{:S(2)}) collective-permute-start(bf16[192,80]{1,0:T(8,128)(2,1)S(1)} %slice.82), channel_id=1, source_target_pairs={{0,3},{1,0},{2,1},{3,2},{4,7},{5,4},{6,5},{7,6},{8,11},{9,8},{10,9... | collective-permute-start | bytes 92168 | tf_op jit(solution)/shard_map/ppermute | solution.py:68
  100.4 28.9 %collective-permute-start.3 = (bf16[192,80]{1,0:T(8,128)(2,1)S(1)}, bf16[192,80]{1,0:T(8,128)(2,1)S(1)}, u32[]{:S(2)}, u32[]{:S(2)}) collective-permute-start(bf16[192,80]{1,0:T(8,128)(2,1)S(1)} %slice.82), channel_id=1, source_target_pairs={{0,2},{1,3},{2,0},{3,1},{4,6},{5,7},{6,4},{7,5},{8,10},{9,11},{10,... | collective-permute-start | bytes 92168 | tf_op jit(solution)/shard_map/ppermute | solution.py:68
  102.8 26.4 %collective-permute-start.2 = (bf16[192,80]{1,0:T(8,128)(2,1)S(1)}, bf16[192,80]{1,0:T(8,128)(2,1)S(1)}, u32[]{:S(2)}, u32[]{:S(2)}) collective-permute-start(bf16[192,80]{1,0:T(8,128)(2,1)S(1)} %slice.82), channel_id=1, source_target_pairs={{0,1},{1,2},{2,3},{3,0},{4,5},{5,6},{6,7},{7,4},{8,9},{9,10},{10,1... | collective-permute-start | bytes 92168 | tf_op jit(solution)/shard_map/ppermute | solution.py:68
  131.1 8.5 %collective-permute-start.11 = (bf16[384,128]{1,0:T(8,128)(2,1)S(1)}, bf16[384,128]{1,0:T(8,128)(2,1)S(1)}, u32[]{:S(2)}, u32[]{:S(2)}) collective-permute-start(bf16[384,128]{1,0:T(8,128)(2,1)S(1)} %constant_dynamic-update-slice_fusion), channel_id=1, source_target_pairs={{0,64},{64,128},{128,192},{192,256},{256,320},{320,384},{384,448},... | collective-permute-start | bytes 294920 | tf_op jit(solution)/shard_map/ppermute | solution.py:68
  133.0 8.3 %collective-permute-start.12 = (bf16[384,128]{1,0:T(8,128)(2,1)S(1)}, bf16[384,128]{1,0:T(8,128)(2,1)S(1)}, u32[]{:S(2)}, u32[]{:S(2)}) collective-permute-start(bf16[384,128]{1,0:T(8,128)(2,1)S(1)} %constant_dynamic-update-slice_fusion.5), channel_id=1, source_target_pairs={{0,128},{64,192},{128,256},{192,320},{256,384},{320,448},{384,512}... | collective-permute-start | bytes 294920 | tf_op jit(solution)/shard_map/ppermute | solution.py:68
  134.9 11.4 %collective-permute-start.13 = (bf16[384,128]{1,0:T(8,128)(2,1)S(1)}, bf16[384,128]{1,0:T(8,128)(2,1)S(1)}, u32[]{:S(2)}, u32[]{:S(2)}) collective-permute-start(bf16[384,128]{1,0:T(8,128)(2,1)S(1)} %constant_dynamic-update-slice_fusion.10), channel_id=1, source_target_pairs={{0,704},{64,0},{128,64},{192,128},{256,192},{320,256},{384,320},{4... | collective-permute-start | bytes 294920 | tf_op jit(solution)/shard_map/ppermute | solution.py:68
  146.4 15.6 %collective-permute-start.16 = (bf16[1344,128]{1,0:T(8,128)(2,1)S(1)}, bf16[1344,128]{1,0:T(8,128)(2,1)S(1)}, u32[]{:S(2)}, u32[]{:S(2)}) collective-permute-start(bf16[1344,128]{1,0:T(8,128)(2,1)S(1)} %get-tuple-element.44.refs_0_), channel_id=1, source_target_pairs={{0,3},{1,0},{2,1},{3,2},{4,7},{5,4},{6,5},{7,6},{8,11},{9,8},{10,9... | collective-permute-start | bytes 1032200 | tf_op jit(solution)/shard_map/ppermute | solution.py:68
  150.9 11.4 %collective-permute-start.15 = (bf16[1344,128]{1,0:T(8,128)(2,1)S(1)}, bf16[1344,128]{1,0:T(8,128)(2,1)S(1)}, u32[]{:S(2)}, u32[]{:S(2)}) collective-permute-start(bf16[1344,128]{1,0:T(8,128)(2,1)S(1)} %get-tuple-element.44.refs_0_), channel_id=1, source_target_pairs={{0,2},{1,3},{2,0},{3,1},{4,6},{5,7},{6,4},{7,5},{8,10},{9,11},{10,... | collective-permute-start | bytes 1032200 | tf_op jit(solution)/shard_map/ppermute | solution.py:68
  153.4 18.3 %collective-permute-start.14 = (bf16[1344,128]{1,0:T(8,128)(2,1)S(1)}, bf16[1344,128]{1,0:T(8,128)(2,1)S(1)}, u32[]{:S(2)}, u32[]{:S(2)}) collective-permute-start(bf16[1344,128]{1,0:T(8,128)(2,1)S(1)} %get-tuple-element.44.refs_0_), channel_id=1, source_target_pairs={{0,1},{1,2},{2,3},{3,0},{4,5},{5,6},{6,7},{7,4},{8,9},{9,10},{10,1... | collective-permute-start | bytes 1032200 | tf_op jit(solution)/shard_map/ppermute | solution.py:68
  155.3 6.7 %collective-permute-start.1 = (bf16[192,512]{1,0:T(8,128)(2,1)S(1)}, bf16[192,512]{1,0:T(8,128)(2,1)S(1)}, u32[]{:S(2)}, u32[]{:S(2)}) collective-permute-start(bf16[192,512]{1,0:T(8,128)(2,1)S(1)} %copy-done.2), channel_id=1, source_target_pairs={{64,0},{128,64},{192,128},{256,192},{320,256},{384,320},{448,384},... | collective-permute-start | bytes 589832 | tf_op jit(solution)/shard_map/ppermute | solution.py:63
  171.7 2.5 %copy-start.1 = (bf16[192,512]{1,0:T(8,128)(2,1)S(1)}, bf16[192,512]{1,0:T(8,128)(2,1)}, u32[]{:S(2)}) copy-start(bf16[192,512]{1,0:T(8,128)(2,1)} %fusion.3.inputs_ref) | copy-start | bytes 589828
  175.2 6.4 %collective-permute-start = (bf16[192,512]{1,0:T(8,128)(2,1)S(1)}, bf16[192,512]{1,0:T(8,128)(2,1)S(1)}, u32[]{:S(2)}, u32[]{:S(2)}) collective-permute-start(bf16[192,512]{1,0:T(8,128)(2,1)S(1)} %fusion.19), channel_id=1, source_target_pairs={{0,64},{64,128},{128,192},{192,256},{256,320},{320,384},{384,448},... | collective-permute-start | bytes 589832 | tf_op jit(solution)/shard_map/ppermute | solution.py:63
Sparse Core Ops, SparseCore 0:
  11.0 54.2 all-gather.2
  74.4 64.3 reduce-scatter.1

commit v3 on v2

--- a/solution.py
+++ b/solution.py
@@ -118,37 +118,49 @@
     return total
 
 
-def place_kernel(shape, own_ref, *refs):
+def place_kernel(shape, own_ref, own, before, upper, lower, after, out_ref):
     per_block, rows, width = shape
-    pieces, out_ref = refs[:-1], refs[-1]
     position, replica = own_ref[0], own_ref[1]
-    replicas = len(pieces)
-    for step in range(replicas):
-        source = lax.rem(replica - step + replicas, replicas)
+    cut = upper.shape[0]
+    for step in range(4):
+        source = lax.rem(replica + 4 - step, 4)
         for back in range(BLOCK):
             place = lax.rem(position - back + BLOCK, BLOCK)
             for j in range(per_block):
                 first = (back * per_block + j) * rows
-                column = ((place * per_block + j) * replicas + source) * width
-                out_ref[:, pl.ds(pl.multiple_of(column, width), width)] = pieces[step][
+                if step == 2:
+                    piece, first = (upper, first) if first < cut else (lower, first - cut)
+                else:
+                    piece = {0: own, 1: before, 3: after}[step]
+                column = ((place * per_block + j) * 4 + source) * width
+                out_ref[:, pl.ds(pl.multiple_of(column, width), width)] = piece[
                     first : first + rows, :
                 ]
 
 
 def place_columns(own, pieces, shape):
-    replicas = len(pieces)
     per_block, rows, width = shape
     return pl.pallas_call(
         functools.partial(place_kernel, shape),
-        out_shape=jax.ShapeDtypeStruct((rows, replicas * BLOCK * per_block * width), jnp.bfloat16),
+        out_shape=jax.ShapeDtypeStruct((rows, 4 * BLOCK * per_block * width), jnp.bfloat16),
         in_specs=[pl.BlockSpec(memory_space=pltpu.SMEM)]
-        + [pl.BlockSpec(memory_space=pltpu.VMEM)] * replicas,
+        + [pl.BlockSpec(memory_space=pltpu.VMEM)] * len(pieces),
         out_specs=pl.BlockSpec(memory_space=pltpu.VMEM),
         compiler_params=pltpu.CompilerParams(vmem_limit_bytes=16 * 1024 * 1024),
     )(own, *pieces)
 
 
-def section_kernel(cotangent_ref, inputs_ref, weight_ref, upstream_ref, product_ref, grad_ref, total):
+def section_kernel(
+    cotangent_ref,
+    inputs_ref,
+    weight_ref,
+    upstream_ref,
+    table_ref,
+    product_ref,
+    grad_ref,
+    picked_ref,
+    total,
+):
     step = pl.program_id(0)
 
     @pl.when(step == 0)
@@ -167,10 +179,14 @@
 
     @pl.when(step == pl.num_programs(0) - 1)
     def _():
-        grad_ref[...] = total[...].astype(jnp.bfloat16)
-
-
-def section_products(cotangent, inputs, weight, upstream):
+        grad = total[...].astype(jnp.bfloat16)
+        grad_ref[...] = grad
+        picked_ref[...] = jnp.dot(
+            table_ref[...], grad, preferred_element_type=jnp.float32
+        ).astype(jnp.bfloat16)
+
+
+def section_products(cotangent, inputs, weight, upstream, table):
     tokens, rows = inputs.shape
     width = weight.shape[1]
     tile = 2048
@@ -183,11 +199,17 @@
             whole,
             pl.BlockSpec((rows, tile), lambda n: (0, n)),
             whole,
+            pl.BlockSpec(table.shape, lambda n: (0, 0)),
         ],
-        out_specs=[pl.BlockSpec((tokens, tile), lambda n: (0, n)), whole],
+        out_specs=[
+            pl.BlockSpec((tokens, tile), lambda n: (0, n)),
+            whole,
+            pl.BlockSpec((table.shape[0], rows), lambda n: (0, 0)),
+        ],
         out_shape=[
             jax.ShapeDtypeStruct((tokens, width), jnp.bfloat16),
             jax.ShapeDtypeStruct((tokens, rows), jnp.bfloat16),
+            jax.ShapeDtypeStruct((table.shape[0], rows), jnp.bfloat16),
         ],
         scratch_shapes=[pltpu.VMEM((tokens, rows), jnp.float32)],
         compiler_params=pltpu.CompilerParams(vmem_limit_bytes=56 * 1024 * 1024),
@@ -196,7 +218,7 @@
             bytes_accessed=2 * (rows * width + 2 * tokens * width),
             transcendentals=0,
         ),
-    )(cotangent, inputs, weight, upstream)
+    )(cotangent, inputs, weight, upstream, table)
 
 
 def local(
@@ -242,39 +264,43 @@
     slot_table = (visual_slot[0][:, None] == columns[None, :]).astype(jnp.bfloat16)
     past_table = (past_slot[0][:, None] == columns[None, :]).astype(jnp.bfloat16)
 
+    past_all = [past_heads] + [rotate(past_heads, "dp", step) for step in range(1, replica_count)]
+
     terms = jnp.dot(current, visual_proj, preferred_element_type=jnp.float32).astype(jnp.bfloat16)
     terms = lax.all_to_all(
         terms.reshape(group_rows, tensor_count, model_rows), "tensor", 1, 1, tiled=True
     )
     embedded = jnp.sum(terms.astype(jnp.float32), axis=1).astype(jnp.bfloat16)
-    spare = jnp.zeros((group_rows, -head_rows % 128), jnp.bfloat16)
+    spare = jnp.zeros((group_rows, -(head_rows * replica_count) % 128), jnp.bfloat16)
     parcel = lax.all_gather(
-        jnp.concatenate([embedded, past_heads, spare], axis=1), "section", axis=0, tiled=True
+        jnp.concatenate([embedded, *past_all, spare], axis=1), "section", axis=0, tiled=True
     )
     visual_rows = parcel[:, :model_rows]
-    past_rows = parcel[:, model_rows : model_rows + head_rows]
+    past_rows = jnp.concatenate(
+        [
+            parcel[:, model_rows + step * head_rows : model_rows + (step + 1) * head_rows]
+            for step in range(replica_count)
+        ],
+        axis=0,
+    )
     placed = lax.dot_general(
         slot_table, visual_rows, (((0,), (0,)), ((), ())), preferred_element_type=jnp.float32
     ).astype(jnp.bfloat16)
     covered = jnp.sum(slot_table, axis=0, dtype=jnp.float32)
     inputs = jnp.where(first_flag & (covered[:, None] > 0.5), placed, layer_input[0].T)
 
-    products, input_grad = section_products(pre_full, inputs, weight, layer_cotangent[0].T)
+    products, input_grad, visual_grad = section_products(
+        pre_full, inputs, weight, layer_cotangent[0].T, past_table
+    )
     preact = lax.psum_scatter(products, "tensor", scatter_dimension=1, tiled=True).astype(
         jnp.float32
     )
     hidden = (inputs.astype(jnp.float32) + jax.nn.silu(preact)).astype(jnp.bfloat16)
-    forward_out = shift(hidden, "section", 1)
     backward_out = shift(input_grad, "section", -1)
 
-    visual_grad = jnp.dot(past_table, input_grad, preferred_element_type=jnp.float32).astype(
-        jnp.bfloat16
-    )
     base = to_relays(visual_grad)
-    gathered = lax.all_gather(spread_columns(base), "tensor", axis=0)
-    past_rows = jnp.concatenate(
-        [past_rows] + [rotate(past_rows, "dp", step) for step in range(1, replica_count)], axis=0
-    )
+    piece, backward_out = lax.optimization_barrier((spread_columns(base), backward_out))
+    gathered = lax.all_gather(piece, "tensor", axis=0)
     per_block = tensor_count // BLOCK
     part_width = model_rows // replica_count
     position, replica = lax.rem(own_section + 1, BLOCK), lax.axis_index("dp")
@@ -318,15 +344,23 @@
         head_sum = head_sum + arrived[column_rows:].astype(jnp.float32)
 
     bundle = jnp.concatenate(in_block + [head_sum.astype(jnp.bfloat16)], axis=0)
-    pieces, head_grad = [bundle], head_sum[:group_rows]
+    before, after, hidden = lax.optimization_barrier(
+        (rotate(bundle, "dp", 1), rotate(bundle, "dp", -1), hidden)
+    )
+    forward_out = shift(hidden, "section", 1)
+    cut = BLOCK * column_rows // 2
+    upper, lower = rotate(before[:cut], "dp", 1), rotate(after[cut:], "dp", -1)
+    halves = [(bundle[:cut], bundle[cut:]), (before[:cut], before[cut:]), (upper, lower)]
+    halves.append((after[:cut], after[cut:]))
+    head_grad = head_sum[:group_rows]
     for step in range(1, replica_count):
-        arrived = rotate(bundle, "dp", step)
-        first = BLOCK * column_rows + (replica_count - step) * group_rows
-        head_grad = head_grad + arrived[first : first + group_rows].astype(jnp.float32)
-        pieces.append(arrived)
+        first = BLOCK * column_rows + (replica_count - step) * group_rows - cut
+        head_grad = head_grad + halves[step][1][first : first + group_rows].astype(jnp.float32)
     head_grad = head_grad[:, :head_rows].astype(jnp.bfloat16)
     grad_proj = place_columns(
-        jnp.stack([position, replica]).astype(jnp.int32), pieces, (per_block, head_rows, part_width)
+        jnp.stack([position, replica]).astype(jnp.int32),
+        (bundle, before, upper, lower, after),
+        (per_block, head_rows, part_width),
     )
     frame_grads = attend_grad(past_saved, head_grad)
     return (forward_out.T[None], backward_out.T[None], grad_proj, frame_grads[:, None, None])

time: 191 us -> 191 us (level)
  waiting for transfers between devices: 41 us -> 33.3 us
  blocking collectives: 48.6 us -> 53.3 us
    ppermute x2, waiting for transfers between devices: 8.2 us -> 1.25 us  [shift(): lax.ppermute(value, axis, [(source, source + steps) for source in range(f...]
    ppermute x9 -> x10, starting transfers between devices: 26.6 us -> 33.5 us  [rotate(): lax.ppermute(value, axis, [(i, (i + steps) % count) for i in range(count)])]
    all_gather x2, blocking collectives: 48.6 us -> 53.3 us  [the longest x1 27.7 us: local(): gathered = lax.all_gather(piece, 'tensor', axis=0)]
    ppermute x4, waiting for transfers between devices: 0.01 us -> 4.24 us  [spread_columns(): piece = lax.ppermute(part, ('section', 'tensor', 'dp'), pairs)]
    ppermute x2, starting transfers between devices: 9.76 us -> 5.6 us  [to_relays(): lax.ppermute(value, 'section', [(0, relay)])]
    ppermute x9 -> x10, waiting for transfers between devices: 16.4 us -> 12.5 us  [rotate(): lax.ppermute(value, axis, [(i, (i + steps) % count) for i in range(count)])]
    all_to_all x1, starting transfers between devices: 13.8 us -> 11.4 us  [local(): lax.all_to_all(terms.reshape(group_rows, tensor_count, model_rows), 'tens...]
    all_to_all x1, waiting for transfers between devices: 11.2 us -> 13.5 us  [local(): lax.all_to_all(terms.reshape(group_rows, tensor_count, model_rows), 'tens...]
  transfers between devices with their start and end apart: 20 -> 21, of which waited for: 10 -> 9; matrix products, arithmetic and copies ran while one was open for 5% -> 7% of each run, Pallas kernels for 1% -> 1%
where the time goes in v3:
time: 191 us; the launch traced here: 189 us
  starting transfers between devices  60 us (31%)
  blocking collectives  53.3 us (28%)
  waiting for transfers between devices  33.3 us (17%)
  between operations  14.7 us (8%)
  Pallas kernels  11.3 us (6%)
  matrix products  7.67 us (4%)
  other arithmetic  4.65 us (2%)
  local copies, waits for them, and re-layouts  4.23 us (2%)
    ppermute x10, starting transfers between devices, rotate(): lax.ppermute(value, axis, [(i, (i + steps) % count) for i in range(count)])  33.5 us
    all_gather x1, blocking collectives, local(): gathered = lax.all_gather(piece, 'tensor', axis=0)  27.7 us
    all_gather x1, blocking collectives, local(): lax.all_gather(jnp.concatenate([embedded, *past_all, spare], axis=1), 'se...  25.6 us
    all_to_all x1, waiting for transfers between devices, local(): lax.all_to_all(terms.reshape(group_rows, tensor_count, model_rows), 'tens...  13.5 us
    ppermute x10, waiting for transfers between devices, rotate(): lax.ppermute(value, axis, [(i, (i + steps) % count) for i in range(count)])  12.5 us
    all_to_all x1, starting transfers between devices, local(): lax.all_to_all(terms.reshape(group_rows, tensor_count, model_rows), 'tens...  11.4 us
    pallas_call x1, Pallas kernels, section_products(): pl.pallas_call(section_kernel, grid=(width // tile,), in_specs=[pl.BlockS...  9.29 us
    ppermute x4, starting transfers between devices, spread_columns(): piece = lax.ppermute(part, ('section', 'tensor', 'dp'), pairs)  5.8 us
  transfers between devices with their start and end apart: 21, of which 9 were waited for; matrix products, arithmetic and copies ran while one was open for 7% of the time, Pallas kernels for 1%

profile of v3, /device:TPU:1, one launch (start us, length us, event | category | flops | bytes accessed | tf_op | source)
XLA Modules:
  0.0 189.0 jit_solution(6168937912055340688)
XLA Ops:
  7.2 1.9 fusion.16
  10.9 5.2 %collective-permute-start.2 = (bf16[16,80]{1,0:T(8,128)(2,1)S(1)}, bf16[16,80]{1,0:T(8,128)(2,1)S(1)}, u32[]{:S(2)}, u32[]{:S(2)}) collective-permute-start(bf16[16,80]{1,0:T(8,128)(2,1)S(1)} %convolution_convert_fusion.6), channel_id=1, source_target_pairs={{0,3},{1,0},{2,1},{3,2},{4,7},{5,4},{6,5},{7,6},{8,11},{9,8},{10,9... | collective-permute-start | bytes 7688 | tf_op jit(solution)/shard_map/ppermute | solution.py:68
  16.1 2.4 %collective-permute-start.1 = (bf16[16,80]{1,0:T(8,128)(2,1)S(1)}, bf16[16,80]{1,0:T(8,128)(2,1)S(1)}, u32[]{:S(2)}, u32[]{:S(2)}) collective-permute-start(bf16[16,80]{1,0:T(8,128)(2,1)S(1)} %convolution_convert_fusion.6), channel_id=1, source_target_pairs={{0,2},{1,3},{2,0},{3,1},{4,6},{5,7},{6,4},{7,5},{8,10},{9,11},{10,... | collective-permute-start | bytes 7688 | tf_op jit(solution)/shard_map/ppermute | solution.py:68
  18.5 2.5 %collective-permute-start = (bf16[16,80]{1,0:T(8,128)(2,1)S(1)}, bf16[16,80]{1,0:T(8,128)(2,1)S(1)}, u32[]{:S(2)}, u32[]{:S(2)}) collective-permute-start(bf16[16,80]{1,0:T(8,128)(2,1)S(1)} %convolution_convert_fusion.6), channel_id=1, source_target_pairs={{0,1},{1,2},{2,3},{3,0},{4,5},{5,6},{6,7},{7,4},{8,9},{9,10},{10,1... | collective-permute-start | bytes 7688 | tf_op jit(solution)/shard_map/ppermute | solution.py:68
  22.0 1.8 convolution_convert_fusion
  24.5 11.4 %all-to-all-start = ((bf16[16,16,512]{2,0,1:T(8,128)(2,1)}), bf16[16,16,512]{2,0,1:T(8,128)(2,1)S(1)}, u32[]{:S(2)}, u32[]{:S(2)}) async-start(bf16[16,16,512]{2,0,1:T(8,128)(2,1)} %bitcast.116), calls=%async_computation | async-start | bytes 524288 | tf_op jit(solution)/shard_map/all_to_all | solution.py:270
  36.9 13.5 %all-to-all-done = bf16[16,16,512]{2,0,1:T(8,128)(2,1)S(1)} async-done(((bf16[16,16,512]{2,0,1:T(8,128)(2,1)}), bf16[16,16,512]{2,0,1:T(8,128)(2,1)S(1)}, u32[]{:S(2)}, u32[]{:S(2)}) %all-to-all-start) | async-done | bytes 262176 | tf_op jit(solution)/shard_map/all_to_all | solution.py:270
  50.6 25.6 %all_gather.12 = bf16[192,896]{1,0:T(8,128)(2,1)S(1)} all-gather(bf16[16,896]{1,0:T(8,128)(2,1)S(1)} %concatenate.23), channel_id=1, replica_groups=mesh['section'=12,'tensor'=16,'dp'=4] {'section'}, dimensions={0}, use_global_device_ids=true | all-gather | bytes 372736 | tf_op jit(solution)/shard_map/all_gather | solution.py:275
  77.2 9.3 %shard_map.174 = (bf16[192,8192]{1,0:T(8,128)(2,1)}, bf16[192,512]{1,0:T(8,128)(2,1)}, bf16[192,512]{1,0:T(8,128)(2,1)}) custom-call(bf16[192,8192]{1,0:T(8,128)(2,1)} %all-gather.3.cloned.1.call-done.cotangent_ref, bf16[192,512]{1,0:T(8,128)(2,1)} %fusion.1.inputs_ref, bf16[512,8192]{1,0:T(8,128)(2,1)} %bitcast.117, bf16[192,512]{1,0:T(8,128)(2,1)} %bitcast.119, ...), custom_call_target="tpu_custom_call" | custom-call | flops 3221225472 | bytes 14680064 | tf_op jit(solution)/shard_map/pallas_call | solution.py:194
  87.4 4.3 %collective-permute-start.4 = (bf16[192,512]{1,0:T(8,128)(2,1)S(1)}, bf16[192,512]{1,0:T(8,128)(2,1)S(1)}, u32[]{:S(2)}, u32[]{:S(2)}) collective-permute-start(bf16[192,512]{1,0:T(8,128)(2,1)S(1)} %copy-done.2), channel_id=1, source_target_pairs={{0,512},{1,513},{2,514},{3,515},{4,516},{5,517},{6,518},{7,519},{8... | collective-permute-start | bytes 589832 | tf_op jit(solution)/shard_map/ppermute | solution.py:78
  91.7 1.3 collective-permute-start.3
  94.3 1.3 collective-permute-done.3
  95.7 1.9 %collective-permute-start.6 = (bf16[192,128]{1,0:T(8,128)(2,1)S(1)}, bf16[192,128]{1,0:T(8,128)(2,1)S(1)}, u32[]{:S(2)}, u32[]{:S(2)}) collective-permute-start(bf16[192,128]{1,0:T(8,128)(2,1)S(1)} %get-tuple-element.44), channel_id=1, source_target_pairs={{0,709},{1,710},{2,711},{3,708},{4,725},{5,726},{6,727},{7,724},{8... | collective-permute-start | bytes 147464 | tf_op jit(solution)/shard_map/ppermute | solution.py:116
  97.7 1.3 collective-permute-start.8
  99.0 1.3 collective-permute-start.7
  100.3 1.3 collective-permute-start.5
  101.7 1.3 collective-permute-start.9
  103.0 4.2 %collective-permute-done.6 = bf16[192,128]{1,0:T(8,128)(2,1)S(1)} collective-permute-done((bf16[192,128]{1,0:T(8,128)(2,1)S(1)}, bf16[192,128]{1,0:T(8,128)(2,1)S(1)}, u32[]{:S(2)}, u32[]{:S(2)}) %collective-permute-start.6) | collective-permute-done | bytes 49184 | tf_op jit(solution)/shard_map/ppermute | solution.py:116
  107.3 1.2 collective-permute-done.9
  108.5 27.7 %all-gather = bf16[3072,128]{1,0:T(8,128)(2,1)S(1)} all-gather(bf16[192,128]{1,0:T(8,128)(2,1)S(1)} %add_add_fusion.1), channel_id=2, replica_groups=mesh['section'=12,'tensor'=16,'dp'=4] {'tensor'}, dimensions={0}, use_global_device_ids=true | all-gather | bytes 835584 | tf_op jit(solution)/shard_map/all_gather | solution.py:303
  138.0 1.9 %collective-permute-start.11 = (bf16[384,128]{1,0:T(8,128)(2,1)S(1)}, bf16[384,128]{1,0:T(8,128)(2,1)S(1)}, u32[]{:S(2)}, u32[]{:S(2)}) collective-permute-start(bf16[384,128]{1,0:T(8,128)(2,1)S(1)} %constant_dynamic-update-slice_fusion.5), channel_id=1, source_target_pairs={{0,128},{64,192},{128,256},{192,320},{256,384},{320,448},{384,512}... | collective-permute-start | bytes 294920 | tf_op jit(solution)/shard_map/ppermute | solution.py:68
  140.0 7.8 %collective-permute-start.10 = (bf16[384,128]{1,0:T(8,128)(2,1)S(1)}, bf16[384,128]{1,0:T(8,128)(2,1)S(1)}, u32[]{:S(2)}, u32[]{:S(2)}) collective-permute-start(bf16[384,128]{1,0:T(8,128)(2,1)S(1)} %constant_dynamic-update-slice_fusion), channel_id=1, source_target_pairs={{0,64},{64,128},{128,192},{192,256},{256,320},{320,384},{384,448},... | collective-permute-start | bytes 294920 | tf_op jit(solution)/shard_map/ppermute | solution.py:68
  147.8 1.9 %collective-permute-start.12 = (bf16[384,128]{1,0:T(8,128)(2,1)S(1)}, bf16[384,128]{1,0:T(8,128)(2,1)S(1)}, u32[]{:S(2)}, u32[]{:S(2)}) collective-permute-start(bf16[384,128]{1,0:T(8,128)(2,1)S(1)} %constant_dynamic-update-slice_fusion.10), channel_id=1, source_target_pairs={{0,704},{64,0},{128,64},{192,128},{256,192},{320,256},{384,320},{4... | collective-permute-start | bytes 294920 | tf_op jit(solution)/shard_map/ppermute | solution.py:68
  149.8 3.4 %collective-permute-done.12 = bf16[384,128]{1,0:T(8,128)(2,1)S(1)} collective-permute-done((bf16[384,128]{1,0:T(8,128)(2,1)S(1)}, bf16[384,128]{1,0:T(8,128)(2,1)S(1)}, u32[]{:S(2)}, u32[]{:S(2)}) %collective-permute-start.12) | collective-permute-done | bytes 98336 | tf_op jit(solution)/shard_map/ppermute | solution.py:68
  153.2 4.4 %collective-permute-start.14 = (bf16[1344,128]{1,0:T(8,128)(2,1)S(1)}, bf16[1344,128]{1,0:T(8,128)(2,1)S(1)}, u32[]{:S(2)}, u32[]{:S(2)}) collective-permute-start(bf16[1344,128]{1,0:T(8,128)(2,1)S(1)} %get-tuple-element.60.own), channel_id=1, source_target_pairs={{0,3},{1,0},{2,1},{3,2},{4,7},{5,4},{6,5},{7,6},{8,11},{9,8},{10,9... | collective-permute-start | bytes 1032200 | tf_op jit(solution)/shard_map/ppermute | solution.py:68
  157.7 1.9 %collective-permute-start.13 = (bf16[1344,128]{1,0:T(8,128)(2,1)S(1)}, bf16[1344,128]{1,0:T(8,128)(2,1)S(1)}, u32[]{:S(2)}, u32[]{:S(2)}) collective-permute-start(bf16[1344,128]{1,0:T(8,128)(2,1)S(1)} %get-tuple-element.60.own), channel_id=1, source_target_pairs={{0,1},{1,2},{2,3},{3,0},{4,5},{5,6},{6,7},{7,4},{8,9},{9,10},{10,1... | collective-permute-start | bytes 1032200 | tf_op jit(solution)/shard_map/ppermute | solution.py:68
  160.7 3.0 %collective-permute-done.14.after = bf16[1344,128]{1,0:T(8,128)(2,1)S(1)} collective-permute-done((bf16[1344,128]{1,0:T(8,128)(2,1)S(1)}, bf16[1344,128]{1,0:T(8,128)(2,1)S(1)}, u32[]{:S(2)}, u32[]{:S(2)}) %collective-permute-start.14) | collective-permute-done | bytes 344096 | tf_op jit(solution)/shard_map/ppermute | solution.py:68
  163.7 5.0 %collective-permute-done.13.before = bf16[1344,128]{1,0:T(8,128)(2,1)S(1)} collective-permute-done((bf16[1344,128]{1,0:T(8,128)(2,1)S(1)}, bf16[1344,128]{1,0:T(8,128)(2,1)S(1)}, u32[]{:S(2)}, u32[]{:S(2)}) %collective-permute-start.13) | collective-permute-done | bytes 344096 | tf_op jit(solution)/shard_map/ppermute | solution.py:68
  168.8 1.9 %collective-permute-start.17 = (bf16[704,128]{1,0:T(8,128)(2,1)S(1)}, bf16[704,128]{1,0:T(8,128)(2,1)S(1)}, u32[]{:S(2)}, u32[]{:S(2)}) collective-permute-start(bf16[704,128]{1,0:T(8,128)(2,1)S(1)} %slice.95), channel_id=1, source_target_pairs={{0,3},{1,0},{2,1},{3,2},{4,7},{5,4},{6,5},{7,6},{8,11},{9,8},{10,9... | collective-permute-start | bytes 540680 | tf_op jit(solution)/shard_map/ppermute | solution.py:68
  170.8 3.4 %collective-permute-start.16 = (bf16[640,128]{1,0:T(8,128)(2,1)S(1)}, bf16[640,128]{1,0:T(8,128)(2,1)S(1)}, u32[]{:S(2)}, u32[]{:S(2)}) collective-permute-start(bf16[640,128]{1,0:T(8,128)(2,1)S(1)} %slice.94), channel_id=1, source_target_pairs={{0,1},{1,2},{2,3},{3,0},{4,5},{5,6},{6,7},{7,4},{8,9},{9,10},{10,1... | collective-permute-start | bytes 491528 | tf_op jit(solution)/shard_map/ppermute | solution.py:68
  174.2 2.3 %collective-permute-start.15 = (bf16[192,512]{1,0:T(8,128)(2,1)S(1)}, bf16[192,512]{1,0:T(8,128)(2,1)S(1)}, u32[]{:S(2)}, u32[]{:S(2)}) collective-permute-start(bf16[192,512]{1,0:T(8,128)(2,1)S(1)} %fusion.17), channel_id=1, source_target_pairs={{0,64},{64,128},{128,192},{192,256},{256,320},{320,384},{384,448},... | collective-permute-start | bytes 589832 | tf_op jit(solution)/shard_map/ppermute | solution.py:63
  178.1 2.0 %shard_map.175 = bf16[80,8192]{1,0:T(8,128)(2,1)} custom-call(s32[2]{0:T(128)S(1)} %pad_add_fusion.own_ref, bf16[1344,128]{1,0:T(8,128)(2,1)S(1)} %get-tuple-element.60.own, bf16[1344,128]{1,0:T(8,128)(2,1)S(1)} %collective-permute-done.13.before, bf16[640,128]{1,0:T(8,128)(2,1)S(1)} %collective-permute-done.16.upper, ...), custom_call_target="tpu_custom_call" | custom-call | tf_op jit(solution)/shard_map/pallas_call | solution.py:143
  (90 shorter events, 14.5 us)
Async XLA Ops:
  7.2 14.8 %copy-start = (bf16[1,1,80,16]{2,3,1,0:T(8,128)(2,1)S(1)}, bf16[1,1,80,16]{2,3,1,0:T(8,128)(2,1)}, u32[]{:S(2)}) copy-start(bf16[1,1,80,16]{2,3,1,0:T(8,128)(2,1)} %param.17) | copy-start | bytes 7684
  7.2 70.0 %all-gather.3.cloned.1.call-start = ((), (), s32[]{:S(2)}) async-start(), calls=%async_computation.2 | async-start | bytes 3342336 | tf_op jit(solution)/shard_map/all_gather | solution.py:255
  10.9 39.6 %collective-permute-start.2 = (bf16[16,80]{1,0:T(8,128)(2,1)S(1)}, bf16[16,80]{1,0:T(8,128)(2,1)S(1)}, u32[]{:S(2)}, u32[]{:S(2)}) collective-permute-start(bf16[16,80]{1,0:T(8,128)(2,1)S(1)} %convolution_convert_fusion.6), channel_id=1, source_target_pairs={{0,3},{1,0},{2,1},{3,2},{4,7},{5,4},{6,5},{7,6},{8,11},{9,8},{10,9... | collective-permute-start | bytes 7688 | tf_op jit(solution)/shard_map/ppermute | solution.py:68
  16.1 34.4 %collective-permute-start.1 = (bf16[16,80]{1,0:T(8,128)(2,1)S(1)}, bf16[16,80]{1,0:T(8,128)(2,1)S(1)}, u32[]{:S(2)}, u32[]{:S(2)}) collective-permute-start(bf16[16,80]{1,0:T(8,128)(2,1)S(1)} %convolution_convert_fusion.6), channel_id=1, source_target_pairs={{0,2},{1,3},{2,0},{3,1},{4,6},{5,7},{6,4},{7,5},{8,10},{9,11},{10,... | collective-permute-start | bytes 7688 | tf_op jit(solution)/shard_map/ppermute | solution.py:68
  18.5 31.9 %collective-permute-start = (bf16[16,80]{1,0:T(8,128)(2,1)S(1)}, bf16[16,80]{1,0:T(8,128)(2,1)S(1)}, u32[]{:S(2)}, u32[]{:S(2)}) collective-permute-start(bf16[16,80]{1,0:T(8,128)(2,1)S(1)} %convolution_convert_fusion.6), channel_id=1, source_target_pairs={{0,1},{1,2},{2,3},{3,0},{4,5},{5,6},{6,7},{7,4},{8,9},{9,10},{10,1... | collective-permute-start | bytes 7688 | tf_op jit(solution)/shard_map/ppermute | solution.py:68
  22.0 14.0 %copy-start.4 = (s32[1,192]{1,0:T(1,128)S(1)}, s32[1,192]{1,0:T(1,128)}, u32[]{:S(2)}) copy-start(s32[1,192]{1,0:T(1,128)} %param.23) | copy-start | bytes 2308
  22.0 14.2 %copy-start.3 = (s32[1,192]{1,0:T(1,128)S(1)}, s32[1,192]{1,0:T(1,128)}, u32[]{:S(2)}) copy-start(s32[1,192]{1,0:T(1,128)} %param.24) | copy-start | bytes 2308
  23.8 52.5 %copy-start.5 = (bf16[1,512,192]{1,2,0:T(8,128)(2,1)S(1)}, bf16[1,512,192]{1,2,0:T(8,128)(2,1)}, u32[]{:S(2)}) copy-start(bf16[1,512,192]{1,2,0:T(8,128)(2,1)} %param.27) | copy-start | bytes 589828
  24.5 25.9 %all-to-all-start = ((bf16[16,16,512]{2,0,1:T(8,128)(2,1)}), bf16[16,16,512]{2,0,1:T(8,128)(2,1)S(1)}, u32[]{:S(2)}, u32[]{:S(2)}) async-start(bf16[16,16,512]{2,0,1:T(8,128)(2,1)} %bitcast.116), calls=%async_computation | async-start | bytes 524288 | tf_op jit(solution)/shard_map/all_to_all | solution.py:270
  36.0 123.7 %reduce-scatter.2.cloned.1.call-start = ((), (), s32[]{:S(2)}) async-start(), calls=%async_computation.3 | async-start | bytes 3342336 | tf_op jit(solution)/shard_map/reduce_scatter | solution.py:295
  86.5 0.9 copy-start.2
  86.5 15.1 %copy-start.6 = (bf16[192,512]{1,0:T(8,128)(2,1)S(1)}, bf16[192,512]{1,0:T(8,128)(2,1)}, u32[]{:S(2)}) copy-start(bf16[192,512]{1,0:T(8,128)(2,1)} %get-tuple-element.13) | copy-start | bytes 589828
  87.4 6.9 %collective-permute-start.4 = (bf16[192,512]{1,0:T(8,128)(2,1)S(1)}, bf16[192,512]{1,0:T(8,128)(2,1)S(1)}, u32[]{:S(2)}, u32[]{:S(2)}) collective-permute-start(bf16[192,512]{1,0:T(8,128)(2,1)S(1)} %copy-done.2), channel_id=1, source_target_pairs={{0,512},{1,513},{2,514},{3,515},{4,516},{5,517},{6,518},{7,519},{8... | collective-permute-start | bytes 589832 | tf_op jit(solution)/shard_map/ppermute | solution.py:78
  91.7 3.9 %collective-permute-start.3 = (bf16[192,512]{1,0:T(8,128)(2,1)S(1)}, bf16[192,512]{1,0:T(8,128)(2,1)S(1)}, u32[]{:S(2)}, u32[]{:S(2)}) collective-permute-start(bf16[192,512]{1,0:T(8,128)(2,1)S(1)} %copy-done.2), channel_id=1, source_target_pairs={{0,256},{1,257},{2,258},{3,259},{4,260},{5,261},{6,262},{7,263},{8... | collective-permute-start | bytes 589832 | tf_op jit(solution)/shard_map/ppermute | solution.py:78
  95.7 11.5 %collective-permute-start.6 = (bf16[192,128]{1,0:T(8,128)(2,1)S(1)}, bf16[192,128]{1,0:T(8,128)(2,1)S(1)}, u32[]{:S(2)}, u32[]{:S(2)}) collective-permute-start(bf16[192,128]{1,0:T(8,128)(2,1)S(1)} %get-tuple-element.44), channel_id=1, source_target_pairs={{0,709},{1,710},{2,711},{3,708},{4,725},{5,726},{6,727},{7,724},{8... | collective-permute-start | bytes 147464 | tf_op jit(solution)/shard_map/ppermute | solution.py:116
  97.7 9.6 %collective-permute-start.8 = (bf16[192,128]{1,0:T(8,128)(2,1)S(1)}, bf16[192,128]{1,0:T(8,128)(2,1)S(1)}, u32[]{:S(2)}, u32[]{:S(2)}) collective-permute-start(bf16[192,128]{1,0:T(8,128)(2,1)S(1)} %get-tuple-element.45), channel_id=1, source_target_pairs={{0,719},{1,716},{2,717},{3,718},{4,735},{5,732},{6,733},{7,734},{8... | collective-permute-start | bytes 147464 | tf_op jit(solution)/shard_map/ppermute | solution.py:116
  99.0 8.3 %collective-permute-start.7 = (bf16[192,128]{1,0:T(8,128)(2,1)S(1)}, bf16[192,128]{1,0:T(8,128)(2,1)S(1)}, u32[]{:S(2)}, u32[]{:S(2)}) collective-permute-start(bf16[192,128]{1,0:T(8,128)(2,1)S(1)} %get-tuple-element.46), channel_id=1, source_target_pairs={{0,714},{1,715},{2,712},{3,713},{4,730},{5,731},{6,728},{7,729},{8... | collective-permute-start | bytes 147464 | tf_op jit(solution)/shard_map/ppermute | solution.py:116
  100.3 7.0 %collective-permute-start.5 = (bf16[192,128]{1,0:T(8,128)(2,1)S(1)}, bf16[192,128]{1,0:T(8,128)(2,1)S(1)}, u32[]{:S(2)}, u32[]{:S(2)}) collective-permute-start(bf16[192,128]{1,0:T(8,128)(2,1)S(1)} %get-tuple-element.47), channel_id=1, source_target_pairs={{0,704},{1,705},{2,706},{3,707},{4,720},{5,721},{6,722},{7,723},{8... | collective-permute-start | bytes 147464 | tf_op jit(solution)/shard_map/ppermute | solution.py:116
  101.7 6.8 %collective-permute-start.9 = (bf16[192,512]{1,0:T(8,128)(2,1)S(1)}, bf16[192,512]{1,0:T(8,128)(2,1)S(1)}, u32[]{:S(2)}, u32[]{:S(2)}) collective-permute-start(bf16[192,512]{1,0:T(8,128)(2,1)S(1)} %copy-done.6), channel_id=1, source_target_pairs={{64,0},{128,64},{192,128},{256,192},{320,256},{384,320},{448,384},... | collective-permute-start | bytes 589832 | tf_op jit(solution)/shard_map/ppermute | solution.py:63
  137.6 22.1 %copy-start.1 = (bf16[192,512]{1,0:T(8,128)(2,1)S(1)}, bf16[192,512]{1,0:T(8,128)(2,1)}, u32[]{:S(2)}) copy-start(bf16[192,512]{1,0:T(8,128)(2,1)} %fusion.1.inputs_ref) | copy-start | bytes 589828
  137.8 38.8 %copy-start.7 = (bf16[1,1,80,16]{2,3,1,0:T(8,128)(2,1)S(1)}, bf16[1,1,80,16]{2,3,1,0:T(8,128)(2,1)}, u32[]{:S(2)}) copy-start(bf16[1,1,80,16]{2,3,1,0:T(8,128)(2,1)} %param.21) | copy-start | bytes 7684
  138.0 38.7 %copy-start.8 = (bf16[1,1,80,16]{2,3,1,0:T(8,128)(2,1)S(1)}, bf16[1,1,80,16]{2,3,1,0:T(8,128)(2,1)}, u32[]{:S(2)}) copy-start(bf16[1,1,80,16]{2,3,1,0:T(8,128)(2,1)} %param.19) | copy-start | bytes 7684
  138.0 38.9 %copy-start.9 = (bf16[1,1,80,16]{2,3,1,0:T(8,128)(2,1)S(1)}, bf16[1,1,80,16]{2,3,1,0:T(8,128)(2,1)}, u32[]{:S(2)}) copy-start(bf16[1,1,80,16]{2,3,1,0:T(8,128)(2,1)} %param.20) | copy-start | bytes 7684
  138.0 11.7 %collective-permute-start.11 = (bf16[384,128]{1,0:T(8,128)(2,1)S(1)}, bf16[384,128]{1,0:T(8,128)(2,1)S(1)}, u32[]{:S(2)}, u32[]{:S(2)}) collective-permute-start(bf16[384,128]{1,0:T(8,128)(2,1)S(1)} %constant_dynamic-update-slice_fusion.5), channel_id=1, source_target_pairs={{0,128},{64,192},{128,256},{192,320},{256,384},{320,448},{384,512}... | collective-permute-start | bytes 294920 | tf_op jit(solution)/shard_map/ppermute | solution.py:68
  140.0 9.8 %collective-permute-start.10 = (bf16[384,128]{1,0:T(8,128)(2,1)S(1)}, bf16[384,128]{1,0:T(8,128)(2,1)S(1)}, u32[]{:S(2)}, u32[]{:S(2)}) collective-permute-start(bf16[384,128]{1,0:T(8,128)(2,1)S(1)} %constant_dynamic-update-slice_fusion), channel_id=1, source_target_pairs={{0,64},{64,128},{128,192},{192,256},{256,320},{320,384},{384,448},... | collective-permute-start | bytes 294920 | tf_op jit(solution)/shard_map/ppermute | solution.py:68
  147.8 5.4 %collective-permute-start.12 = (bf16[384,128]{1,0:T(8,128)(2,1)S(1)}, bf16[384,128]{1,0:T(8,128)(2,1)S(1)}, u32[]{:S(2)}, u32[]{:S(2)}) collective-permute-start(bf16[384,128]{1,0:T(8,128)(2,1)S(1)} %constant_dynamic-update-slice_fusion.10), channel_id=1, source_target_pairs={{0,704},{64,0},{128,64},{192,128},{256,192},{320,256},{384,320},{4... | collective-permute-start | bytes 294920 | tf_op jit(solution)/shard_map/ppermute | solution.py:68
  153.2 10.5 %collective-permute-start.14 = (bf16[1344,128]{1,0:T(8,128)(2,1)S(1)}, bf16[1344,128]{1,0:T(8,128)(2,1)S(1)}, u32[]{:S(2)}, u32[]{:S(2)}) collective-permute-start(bf16[1344,128]{1,0:T(8,128)(2,1)S(1)} %get-tuple-element.60.own), channel_id=1, source_target_pairs={{0,3},{1,0},{2,1},{3,2},{4,7},{5,4},{6,5},{7,6},{8,11},{9,8},{10,9... | collective-permute-start | bytes 1032200 | tf_op jit(solution)/shard_map/ppermute | solution.py:68
  157.7 11.1 %collective-permute-start.13 = (bf16[1344,128]{1,0:T(8,128)(2,1)S(1)}, bf16[1344,128]{1,0:T(8,128)(2,1)S(1)}, u32[]{:S(2)}, u32[]{:S(2)}) collective-permute-start(bf16[1344,128]{1,0:T(8,128)(2,1)S(1)} %get-tuple-element.60.own), channel_id=1, source_target_pairs={{0,1},{1,2},{2,3},{3,0},{4,5},{5,6},{6,7},{7,4},{8,9},{9,10},{10,1... | collective-permute-start | bytes 1032200 | tf_op jit(solution)/shard_map/ppermute | solution.py:68
  168.8 7.7 %collective-permute-start.17 = (bf16[704,128]{1,0:T(8,128)(2,1)S(1)}, bf16[704,128]{1,0:T(8,128)(2,1)S(1)}, u32[]{:S(2)}, u32[]{:S(2)}) collective-permute-start(bf16[704,128]{1,0:T(8,128)(2,1)S(1)} %slice.95), channel_id=1, source_target_pairs={{0,3},{1,0},{2,1},{3,2},{4,7},{5,4},{6,5},{7,6},{8,11},{9,8},{10,9... | collective-permute-start | bytes 540680 | tf_op jit(solution)/shard_map/ppermute | solution.py:68
  170.8 7.3 %collective-permute-start.16 = (bf16[640,128]{1,0:T(8,128)(2,1)S(1)}, bf16[640,128]{1,0:T(8,128)(2,1)S(1)}, u32[]{:S(2)}, u32[]{:S(2)}) collective-permute-start(bf16[640,128]{1,0:T(8,128)(2,1)S(1)} %slice.94), channel_id=1, source_target_pairs={{0,1},{1,2},{2,3},{3,0},{4,5},{5,6},{6,7},{7,4},{8,9},{9,10},{10,1... | collective-permute-start | bytes 491528 | tf_op jit(solution)/shard_map/ppermute | solution.py:68
  174.2 6.6 %collective-permute-start.15 = (bf16[192,512]{1,0:T(8,128)(2,1)S(1)}, bf16[192,512]{1,0:T(8,128)(2,1)S(1)}, u32[]{:S(2)}, u32[]{:S(2)}) collective-permute-start(bf16[192,512]{1,0:T(8,128)(2,1)S(1)} %fusion.17), channel_id=1, source_target_pairs={{0,64},{64,128},{128,192},{192,256},{256,320},{320,384},{384,448},... | collective-permute-start | bytes 589832 | tf_op jit(solution)/shard_map/ppermute | solution.py:63
Sparse Core Ops, SparseCore 0:
  11.0 58.4 all-gather.2
  86.7 59.9 reduce-scatter.1

commit v4 on v3

--- a/solution.py
+++ b/solution.py
@@ -118,22 +118,19 @@
     return total
 
 
-def place_kernel(shape, own_ref, own, before, upper, lower, after, out_ref):
+def place_kernel(shape, own_ref, *refs):
     per_block, rows, width = shape
+    pieces, out_ref = refs[:-1], refs[-1]
     position, replica = own_ref[0], own_ref[1]
-    cut = upper.shape[0]
-    for step in range(4):
-        source = lax.rem(replica + 4 - step, 4)
+    replicas = len(pieces)
+    for step in range(replicas):
+        source = lax.rem(replica - step + replicas, replicas)
         for back in range(BLOCK):
             place = lax.rem(position - back + BLOCK, BLOCK)
             for j in range(per_block):
                 first = (back * per_block + j) * rows
-                if step == 2:
-                    piece, first = (upper, first) if first < cut else (lower, first - cut)
-                else:
-                    piece = {0: own, 1: before, 3: after}[step]
-                column = ((place * per_block + j) * 4 + source) * width
-                out_ref[:, pl.ds(pl.multiple_of(column, width), width)] = piece[
+                column = ((place * per_block + j) * replicas + source) * width
+                out_ref[:, pl.ds(pl.multiple_of(column, width), width)] = pieces[step][
                     first : first + rows, :
                 ]
 
@@ -142,7 +139,9 @@
     per_block, rows, width = shape
     return pl.pallas_call(
         functools.partial(place_kernel, shape),
-        out_shape=jax.ShapeDtypeStruct((rows, 4 * BLOCK * per_block * width), jnp.bfloat16),
+        out_shape=jax.ShapeDtypeStruct(
+            (rows, len(pieces) * BLOCK * per_block * width), jnp.bfloat16
+        ),
         in_specs=[pl.BlockSpec(memory_space=pltpu.SMEM)]
         + [pl.BlockSpec(memory_space=pltpu.VMEM)] * len(pieces),
         out_specs=pl.BlockSpec(memory_space=pltpu.VMEM),
@@ -155,7 +154,7 @@
     inputs_ref,
     weight_ref,
     upstream_ref,
-    table_ref,
+    slot_ref,
     product_ref,
     grad_ref,
     picked_ref,
@@ -181,12 +180,17 @@
     def _():
         grad = total[...].astype(jnp.bfloat16)
         grad_ref[...] = grad
-        picked_ref[...] = jnp.dot(
-            table_ref[...], grad, preferred_element_type=jnp.float32
+        tokens, count = grad.shape[0], slot_ref.shape[1]
+        table = lax.broadcasted_iota(jnp.int32, (tokens, count), 0) == slot_ref[...]
+        picked_ref[...] = lax.dot_general(
+            table.astype(jnp.float32).astype(jnp.bfloat16),
+            grad,
+            (((0,), (0,)), ((), ())),
+            preferred_element_type=jnp.float32,
         ).astype(jnp.bfloat16)
 
 
-def section_products(cotangent, inputs, weight, upstream, table):
+def section_products(cotangent, inputs, weight, upstream, slot):
     tokens, rows = inputs.shape
     width = weight.shape[1]
     tile = 2048
@@ -199,17 +203,17 @@
             whole,
             pl.BlockSpec((rows, tile), lambda n: (0, n)),
             whole,
-            pl.BlockSpec(table.shape, lambda n: (0, 0)),
+            pl.BlockSpec(slot.shape, lambda n: (0, 0)),
         ],
         out_specs=[
             pl.BlockSpec((tokens, tile), lambda n: (0, n)),
             whole,
-            pl.BlockSpec((table.shape[0], rows), lambda n: (0, 0)),
+            pl.BlockSpec((slot.shape[1], rows), lambda n: (0, 0)),
         ],
         out_shape=[
             jax.ShapeDtypeStruct((tokens, width), jnp.bfloat16),
             jax.ShapeDtypeStruct((tokens, rows), jnp.bfloat16),
-            jax.ShapeDtypeStruct((table.shape[0], rows), jnp.bfloat16),
+            jax.ShapeDtypeStruct((slot.shape[1], rows), jnp.bfloat16),
         ],
         scratch_shapes=[pltpu.VMEM((tokens, rows), jnp.float32)],
         compiler_params=pltpu.CompilerParams(vmem_limit_bytes=56 * 1024 * 1024),
@@ -218,7 +222,7 @@
             bytes_accessed=2 * (rows * width + 2 * tokens * width),
             transcendentals=0,
         ),
-    )(cotangent, inputs, weight, upstream, table)
+    )(cotangent, inputs, weight, upstream, slot)
 
 
 def local(
@@ -257,20 +261,20 @@
     current, _ = attend_parts(
         frame_query[0, 0], frame_key[0, 0], frame_value[0, 0], frame_segment[0, 0]
     )
+    columns = jnp.arange(token_count, dtype=jnp.int32)
+    slot_table = (visual_slot[0][:, None] == columns[None, :]).astype(jnp.bfloat16)
+
+    terms = jnp.dot(current, visual_proj, preferred_element_type=jnp.float32).astype(jnp.bfloat16)
+    terms = jnp.transpose(terms.reshape(group_rows, tensor_count, model_rows), (1, 0, 2))
+    terms, past_query, past_key = lax.optimization_barrier((terms, past_query, past_key))
     past_heads, past_saved = attend_parts(
         past_query[0, 0], past_key[0, 0], past_value[0, 0], past_segment[0, 0]
     )
-    columns = jnp.arange(token_count, dtype=jnp.int32)
-    slot_table = (visual_slot[0][:, None] == columns[None, :]).astype(jnp.bfloat16)
-    past_table = (past_slot[0][:, None] == columns[None, :]).astype(jnp.bfloat16)
 
     past_all = [past_heads] + [rotate(past_heads, "dp", step) for step in range(1, replica_count)]
 
-    terms = jnp.dot(current, visual_proj, preferred_element_type=jnp.float32).astype(jnp.bfloat16)
-    terms = lax.all_to_all(
-        terms.reshape(group_rows, tensor_count, model_rows), "tensor", 1, 1, tiled=True
-    )
-    embedded = jnp.sum(terms.astype(jnp.float32), axis=1).astype(jnp.bfloat16)
+    terms = lax.all_to_all(terms, "tensor", 0, 0, tiled=True)
+    embedded = jnp.sum(terms.astype(jnp.float32), axis=0).astype(jnp.bfloat16)
     spare = jnp.zeros((group_rows, -(head_rows * replica_count) % 128), jnp.bfloat16)
     parcel = lax.all_gather(
         jnp.concatenate([embedded, *past_all, spare], axis=1), "section", axis=0, tiled=True
@@ -290,7 +294,7 @@
     inputs = jnp.where(first_flag & (covered[:, None] > 0.5), placed, layer_input[0].T)
 
     products, input_grad, visual_grad = section_products(
-        pre_full, inputs, weight, layer_cotangent[0].T, past_table
+        pre_full, inputs, weight, layer_cotangent[0].T, past_slot
     )
     preact = lax.psum_scatter(products, "tensor", scatter_dimension=1, tiled=True).astype(
         jnp.float32
@@ -344,22 +348,17 @@
         head_sum = head_sum + arrived[column_rows:].astype(jnp.float32)
 
     bundle = jnp.concatenate(in_block + [head_sum.astype(jnp.bfloat16)], axis=0)
-    before, after, hidden = lax.optimization_barrier(
-        (rotate(bundle, "dp", 1), rotate(bundle, "dp", -1), hidden)
-    )
+    arrived = [rotate(bundle, "dp", step) for step in range(1, replica_count)]
     forward_out = shift(hidden, "section", 1)
-    cut = BLOCK * column_rows // 2
-    upper, lower = rotate(before[:cut], "dp", 1), rotate(after[cut:], "dp", -1)
-    halves = [(bundle[:cut], bundle[cut:]), (before[:cut], before[cut:]), (upper, lower)]
-    halves.append((after[:cut], after[cut:]))
+    *arrived, _ = lax.optimization_barrier((*arrived, hidden))
     head_grad = head_sum[:group_rows]
     for step in range(1, replica_count):
-        first = BLOCK * column_rows + (replica_count - step) * group_rows - cut
-        head_grad = head_grad + halves[step][1][first : first + group_rows].astype(jnp.float32)
+        first = BLOCK * column_rows + (replica_count - step) * group_rows
+        head_grad = head_grad + arrived[step - 1][first : first + group_rows].astype(jnp.float32)
     head_grad = head_grad[:, :head_rows].astype(jnp.bfloat16)
     grad_proj = place_columns(
         jnp.stack([position, replica]).astype(jnp.int32),
-        (bundle, before, upper, lower, after),
+        (bundle, *arrived),
         (per_block, head_rows, part_width),
     )
     frame_grads = attend_grad(past_saved, head_grad)

time: 191 us -> 180 us (0.942)
  waiting for transfers between devices: 33.3 us -> 27.8 us
    all_to_all x1, waiting for transfers between devices: 13.5 us -> 4.07 us  [local(): terms = lax.all_to_all(terms, 'tensor', 0, 0, tiled=True)]
    ppermute x10 -> x9, starting transfers between devices: 33.5 us -> 25.3 us  [rotate(): lax.ppermute(value, axis, [(i, (i + steps) % count) for i in range(count)])]
    ppermute x2, starting transfers between devices: 5.6 us -> 9.76 us  [to_relays(): lax.ppermute(value, 'section', [(0, relay)])]
    ppermute x10 -> x9, waiting for transfers between devices: 12.5 us -> 15.6 us  [rotate(): lax.ppermute(value, axis, [(i, (i + steps) % count) for i in range(count)])]
    ppermute x4, waiting for transfers between devices: 4.24 us -> 1.28 us  [spread_columns(): piece = lax.ppermute(part, ('section', 'tensor', 'dp'), pairs)]
    ppermute x2, waiting for transfers between devices: 1.25 us -> 3.81 us  [shift(): lax.ppermute(value, axis, [(source, source + steps) for source in range(f...]
    all_to_all x1, starting transfers between devices: 11.4 us -> 13.8 us  [local(): terms = lax.all_to_all(terms, 'tensor', 0, 0, tiled=True)]
  transfers between devices with their start and end apart: 21 -> 20, of which waited for: 9 -> 10; matrix products, arithmetic and copies ran while one was open for 7% -> 6% of each run, Pallas kernels for 1% -> 1%
where the time goes in v4:
time: 180 us; the launch traced here: 179 us
  starting transfers between devices  58.8 us (33%)
  blocking collectives  52.3 us (29%)
  waiting for transfers between devices  27.8 us (15%)
  between operations  14.6 us (8%)
  Pallas kernels  11.3 us (6%)
  matrix products  6.26 us (3%)
  local copies, waits for them, and re-layouts  4.21 us (2%)
  other arithmetic  3.91 us (2%)
    all_gather x1, blocking collectives, local(): gathered = lax.all_gather(piece, 'tensor', axis=0)  27.1 us
    ppermute x9, starting transfers between devices, rotate(): lax.ppermute(value, axis, [(i, (i + steps) % count) for i in range(count)])  25.3 us
    all_gather x1, blocking collectives, local(): lax.all_gather(jnp.concatenate([embedded, *past_all, spare], axis=1), 'se...  25.2 us
    ppermute x9, waiting for transfers between devices, rotate(): lax.ppermute(value, axis, [(i, (i + steps) % count) for i in range(count)])  15.6 us
    all_to_all x1, starting transfers between devices, local(): terms = lax.all_to_all(terms, 'tensor', 0, 0, tiled=True)  13.8 us
    ppermute x2, starting transfers between devices, to_relays(): lax.ppermute(value, 'section', [(0, relay)])  9.76 us
    pallas_call x1, Pallas kernels, section_products(): pl.pallas_call(section_kernel, grid=(width // tile,), in_specs=[pl.BlockS...  9.29 us
    ppermute x4, starting transfers between devices, spread_columns(): piece = lax.ppermute(part, ('section', 'tensor', 'dp'), pairs)  5.8 us
  transfers between devices with their start and end apart: 20, of which 10 were waited for; matrix products, arithmetic and copies ran while one was open for 6% of the time, Pallas kernels for 1%

profile of v4, /device:TPU:1, one launch (start us, length us, event | category | flops | bytes accessed | tf_op | source)
XLA Modules:
  0.0 179.2 jit_solution(5107846859938125591)
XLA Ops:
  7.2 1.9 %fusion.16 = bf16[192,512]{1,0:T(8,128)(2,1)} fusion(bf16[1,512,192]{1,2,0:T(8,128)(2,1)} %param.28, bf16[1,512,192]{1,2,0:T(8,128)(2,1)} %param.29), kind=kLoop, calls=%fused_computation.35 | loop fusion | flops 1081344 | bytes 589824 | tf_op jit(solution)/shard_map/convert_element_type | solution.py:258
  10.1 1.8 convolution_convert_fusion
  12.6 13.8 %all-to-all-start = ((bf16[16,16,512]{2,1,0:T(8,128)(2,1)}), bf16[16,16,512]{2,1,0:T(8,128)(2,1)S(1)}, u32[]{:S(2)}, u32[]{:S(2)}) async-start(bf16[16,16,512]{2,1,0:T(8,128)(2,1)} %bitcast.114), calls=%async_computation | async-start | bytes 524288 | tf_op jit(solution)/shard_map/all_to_all | solution.py:276
  26.9 1.9 %collective-permute-start.2 = (bf16[16,80]{1,0:T(8,128)(2,1)S(1)}, bf16[16,80]{1,0:T(8,128)(2,1)S(1)}, u32[]{:S(2)}, u32[]{:S(2)}) collective-permute-start(bf16[16,80]{1,0:T(8,128)(2,1)S(1)} %convolution_convert_fusion.6), channel_id=1, source_target_pairs={{0,3},{1,0},{2,1},{3,2},{4,7},{5,4},{6,5},{7,6},{8,11},{9,8},{10,9... | collective-permute-start | bytes 7688 | tf_op jit(solution)/shard_map/ppermute | solution.py:68
  28.8 1.9 %collective-permute-start.1 = (bf16[16,80]{1,0:T(8,128)(2,1)S(1)}, bf16[16,80]{1,0:T(8,128)(2,1)S(1)}, u32[]{:S(2)}, u32[]{:S(2)}) collective-permute-start(bf16[16,80]{1,0:T(8,128)(2,1)S(1)} %convolution_convert_fusion.6), channel_id=1, source_target_pairs={{0,2},{1,3},{2,0},{3,1},{4,6},{5,7},{6,4},{7,5},{8,10},{9,11},{10,... | collective-permute-start | bytes 7688 | tf_op jit(solution)/shard_map/ppermute | solution.py:68
  30.7 3.4 %collective-permute-start = (bf16[16,80]{1,0:T(8,128)(2,1)S(1)}, bf16[16,80]{1,0:T(8,128)(2,1)S(1)}, u32[]{:S(2)}, u32[]{:S(2)}) collective-permute-start(bf16[16,80]{1,0:T(8,128)(2,1)S(1)} %convolution_convert_fusion.6), channel_id=1, source_target_pairs={{0,1},{1,2},{2,3},{3,0},{4,5},{5,6},{6,7},{7,4},{8,9},{9,10},{10,1... | collective-permute-start | bytes 7688 | tf_op jit(solution)/shard_map/ppermute | solution.py:68
  34.2 4.1 %all-to-all-done = bf16[16,16,512]{2,1,0:T(8,128)(2,1)S(1)} async-done(((bf16[16,16,512]{2,1,0:T(8,128)(2,1)}), bf16[16,16,512]{2,1,0:T(8,128)(2,1)S(1)}, u32[]{:S(2)}, u32[]{:S(2)}) %all-to-all-start) | async-done | bytes 262176 | tf_op jit(solution)/shard_map/all_to_all | solution.py:276
  38.5 25.2 %all_gather.12 = bf16[192,896]{1,0:T(8,128)(2,1)S(1)} all-gather(bf16[16,896]{1,0:T(8,128)(2,1)S(1)} %concatenate.23), channel_id=1, replica_groups=mesh['section'=12,'tensor'=16,'dp'=4] {'section'}, dimensions={0}, use_global_device_ids=true | all-gather | bytes 372736 | tf_op jit(solution)/shard_map/all_gather | solution.py:279
  65.3 9.3 %shard_map.174 = (bf16[192,8192]{1,0:T(8,128)(2,1)}, bf16[192,512]{1,0:T(8,128)(2,1)}, bf16[192,512]{1,0:T(8,128)(2,1)}) custom-call(bf16[192,8192]{1,0:T(8,128)(2,1)} %all-gather.3.cloned.1.call-done.cotangent_ref, bf16[192,512]{1,0:T(8,128)(2,1)} %fusion.1.inputs_ref, bf16[512,8192]{1,0:T(8,128)(2,1)} %bitcast.115, bf16[192,512]{1,0:T(8,128)(2,1)} %bitcast.117, ...), custom_call_target="tpu_custom_call" | custom-call | flops 3221225472 | bytes 14680064 | tf_op jit(solution)/shard_map/pallas_call | solution.py:198
  75.5 8.5 %collective-permute-start.5 = (bf16[192,512]{1,0:T(8,128)(2,1)S(1)}, bf16[192,512]{1,0:T(8,128)(2,1)S(1)}, u32[]{:S(2)}, u32[]{:S(2)}) collective-permute-start(bf16[192,512]{1,0:T(8,128)(2,1)S(1)} %copy-done.2), channel_id=1, source_target_pairs={{0,512},{1,513},{2,514},{3,515},{4,516},{5,517},{6,518},{7,519},{8... | collective-permute-start | bytes 589832 | tf_op jit(solution)/shard_map/ppermute | solution.py:78
  84.0 1.3 collective-permute-start.4
  87.3 1.3 collective-permute-done.4
  88.7 1.9 %collective-permute-start.7 = (bf16[192,128]{1,0:T(8,128)(2,1)S(1)}, bf16[192,128]{1,0:T(8,128)(2,1)S(1)}, u32[]{:S(2)}, u32[]{:S(2)}) collective-permute-start(bf16[192,128]{1,0:T(8,128)(2,1)S(1)} %get-tuple-element.50), channel_id=1, source_target_pairs={{0,709},{1,710},{2,711},{3,708},{4,725},{5,726},{6,727},{7,724},{8... | collective-permute-start | bytes 147464 | tf_op jit(solution)/shard_map/ppermute | solution.py:116
  90.6 1.3 collective-permute-start.9
  91.9 1.3 collective-permute-start.8
  93.2 1.3 collective-permute-start.6
  94.7 1.3 collective-permute-start.10
  96.0 1.3 collective-permute-done.7
  97.3 3.8 %collective-permute-done.10 = bf16[192,512]{1,0:T(8,128)(2,1)S(1)} collective-permute-done((bf16[192,512]{1,0:T(8,128)(2,1)S(1)}, bf16[192,512]{1,0:T(8,128)(2,1)S(1)}, u32[]{:S(2)}, u32[]{:S(2)}) %collective-permute-start.10) | collective-permute-done | bytes 196640 | tf_op jit(solution)/shard_map/ppermute | solution.py:63
  101.1 27.1 %all-gather = bf16[3072,128]{1,0:T(8,128)(2,1)S(1)} all-gather(bf16[192,128]{1,0:T(8,128)(2,1)S(1)} %add_add_fusion.1), channel_id=2, replica_groups=mesh['section'=12,'tensor'=16,'dp'=4] {'tensor'}, dimensions={0}, use_global_device_ids=true | all-gather | bytes 835584 | tf_op jit(solution)/shard_map/all_gather | solution.py:307
  130.0 1.9 %collective-permute-start.12 = (bf16[384,128]{1,0:T(8,128)(2,1)S(1)}, bf16[384,128]{1,0:T(8,128)(2,1)S(1)}, u32[]{:S(2)}, u32[]{:S(2)}) collective-permute-start(bf16[384,128]{1,0:T(8,128)(2,1)S(1)} %constant_dynamic-update-slice_fusion.5), channel_id=1, source_target_pairs={{0,128},{64,192},{128,256},{192,320},{256,384},{320,448},{384,512}... | collective-permute-start | bytes 294920 | tf_op jit(solution)/shard_map/ppermute | solution.py:68
  132.0 6.6 %collective-permute-start.11 = (bf16[384,128]{1,0:T(8,128)(2,1)S(1)}, bf16[384,128]{1,0:T(8,128)(2,1)S(1)}, u32[]{:S(2)}, u32[]{:S(2)}) collective-permute-start(bf16[384,128]{1,0:T(8,128)(2,1)S(1)} %constant_dynamic-update-slice_fusion), channel_id=1, source_target_pairs={{0,64},{64,128},{128,192},{192,256},{256,320},{320,384},{384,448},... | collective-permute-start | bytes 294920 | tf_op jit(solution)/shard_map/ppermute | solution.py:68
  138.6 1.9 %collective-permute-start.13 = (bf16[384,128]{1,0:T(8,128)(2,1)S(1)}, bf16[384,128]{1,0:T(8,128)(2,1)S(1)}, u32[]{:S(2)}, u32[]{:S(2)}) collective-permute-start(bf16[384,128]{1,0:T(8,128)(2,1)S(1)} %constant_dynamic-update-slice_fusion.10), channel_id=1, source_target_pairs={{0,704},{64,0},{128,64},{192,128},{256,192},{320,256},{384,320},{4... | collective-permute-start | bytes 294920 | tf_op jit(solution)/shard_map/ppermute | solution.py:68
  140.5 1.2 collective-permute-done.11
  141.7 3.5 %collective-permute-done.13 = bf16[384,128]{1,0:T(8,128)(2,1)S(1)} collective-permute-done((bf16[384,128]{1,0:T(8,128)(2,1)S(1)}, bf16[384,128]{1,0:T(8,128)(2,1)S(1)}, u32[]{:S(2)}, u32[]{:S(2)}) %collective-permute-start.13) | collective-permute-done | bytes 98336 | tf_op jit(solution)/shard_map/ppermute | solution.py:68
  145.2 1.9 %collective-permute-start.16 = (bf16[1344,128]{1,0:T(8,128)(2,1)S(1)}, bf16[1344,128]{1,0:T(8,128)(2,1)S(1)}, u32[]{:S(2)}, u32[]{:S(2)}) collective-permute-start(bf16[1344,128]{1,0:T(8,128)(2,1)S(1)} %get-tuple-element.66.refs_0_), channel_id=1, source_target_pairs={{0,3},{1,0},{2,1},{3,2},{4,7},{5,4},{6,5},{7,6},{8,11},{9,8},{10,9... | collective-permute-start | bytes 1032200 | tf_op jit(solution)/shard_map/ppermute | solution.py:68
  147.1 3.3 %collective-permute-start.15 = (bf16[1344,128]{1,0:T(8,128)(2,1)S(1)}, bf16[1344,128]{1,0:T(8,128)(2,1)S(1)}, u32[]{:S(2)}, u32[]{:S(2)}) collective-permute-start(bf16[1344,128]{1,0:T(8,128)(2,1)S(1)} %get-tuple-element.66.refs_0_), channel_id=1, source_target_pairs={{0,2},{1,3},{2,0},{3,1},{4,6},{5,7},{6,4},{7,5},{8,10},{9,11},{10,... | collective-permute-start | bytes 1032200 | tf_op jit(solution)/shard_map/ppermute | solution.py:68
  150.5 2.5 %collective-permute-start.14 = (bf16[1344,128]{1,0:T(8,128)(2,1)S(1)}, bf16[1344,128]{1,0:T(8,128)(2,1)S(1)}, u32[]{:S(2)}, u32[]{:S(2)}) collective-permute-start(bf16[1344,128]{1,0:T(8,128)(2,1)S(1)} %get-tuple-element.66.refs_0_), channel_id=1, source_target_pairs={{0,1},{1,2},{2,3},{3,0},{4,5},{5,6},{6,7},{7,4},{8,9},{9,10},{10,1... | collective-permute-start | bytes 1032200 | tf_op jit(solution)/shard_map/ppermute | solution.py:68
  154.1 2.7 %collective-permute-start.3 = (bf16[192,512]{1,0:T(8,128)(2,1)S(1)}, bf16[192,512]{1,0:T(8,128)(2,1)S(1)}, u32[]{:S(2)}, u32[]{:S(2)}) collective-permute-start(bf16[192,512]{1,0:T(8,128)(2,1)S(1)} %fusion.17), channel_id=1, source_target_pairs={{0,64},{64,128},{128,192},{192,256},{256,320},{320,384},{384,448},... | collective-permute-start | bytes 589832 | tf_op jit(solution)/shard_map/ppermute | solution.py:63
  156.8 2.0 %collective-permute-done.15.refs_2_ = bf16[1344,128]{1,0:T(8,128)(2,1)S(1)} collective-permute-done((bf16[1344,128]{1,0:T(8,128)(2,1)S(1)}, bf16[1344,128]{1,0:T(8,128)(2,1)S(1)}, u32[]{:S(2)}, u32[]{:S(2)}) %collective-permute-start.15) | collective-permute-done | bytes 344096 | tf_op jit(solution)/shard_map/ppermute | solution.py:68
  158.8 9.0 %collective-permute-done.14.refs_1_ = bf16[1344,128]{1,0:T(8,128)(2,1)S(1)} collective-permute-done((bf16[1344,128]{1,0:T(8,128)(2,1)S(1)}, bf16[1344,128]{1,0:T(8,128)(2,1)S(1)}, u32[]{:S(2)}, u32[]{:S(2)}) %collective-permute-start.14) | collective-permute-done | bytes 344096 | tf_op jit(solution)/shard_map/ppermute | solution.py:68
  168.3 2.0 %shard_map.175 = bf16[80,8192]{1,0:T(8,128)(2,1)} custom-call(s32[2]{0:T(128)S(1)} %pad_add_fusion.own_ref, bf16[1344,128]{1,0:T(8,128)(2,1)S(1)} %get-tuple-element.66.refs_0_, bf16[1344,128]{1,0:T(8,128)(2,1)S(1)} %collective-permute-done.14.refs_1_, bf16[1344,128]{1,0:T(8,128)(2,1)S(1)} %collective-permute-done.15.refs_2_, ...), custom_call_target="tpu_custom_call" | custom-call | tf_op jit(solution)/shard_map/pallas_call | solution.py:140
  (85 shorter events, 12.6 us)
Async XLA Ops:
  7.2 2.9 %copy-start = (bf16[1,1,80,16]{2,3,1,0:T(8,128)(2,1)S(1)}, bf16[1,1,80,16]{2,3,1,0:T(8,128)(2,1)}, u32[]{:S(2)}) copy-start(bf16[1,1,80,16]{2,3,1,0:T(8,128)(2,1)} %param.17) | copy-start | bytes 7684
  7.2 58.1 %all-gather.3.cloned.1.call-start = ((), (), s32[]{:S(2)}) async-start(), calls=%async_computation.2 | async-start | bytes 3342336 | tf_op jit(solution)/shard_map/all_gather | solution.py:259
  10.0 16.5 %copy-start.7 = (bf16[1,1,80,16]{2,3,1,0:T(8,128)(2,1)S(1)}, bf16[1,1,80,16]{2,3,1,0:T(8,128)(2,1)}, u32[]{:S(2)}) copy-start(bf16[1,1,80,16]{2,3,1,0:T(8,128)(2,1)} %param.19) | copy-start | bytes 7684
  10.0 16.5 %copy-start.8 = (bf16[1,1,80,16]{2,3,1,0:T(8,128)(2,1)S(1)}, bf16[1,1,80,16]{2,3,1,0:T(8,128)(2,1)}, u32[]{:S(2)}) copy-start(bf16[1,1,80,16]{2,3,1,0:T(8,128)(2,1)} %param.20) | copy-start | bytes 7684
  10.0 16.5 %copy-start.9 = (s32[1,1,16]{2,1,0:T(1,128)S(1)}, s32[1,1,16]{2,1,0:T(1,128)}, u32[]{:S(2)}) copy-start(s32[1,1,16]{2,1,0:T(1,128)} %param.22) | copy-start | bytes 196
  10.1 16.6 %copy-start.6 = (bf16[1,1,80,16]{2,3,1,0:T(8,128)(2,1)S(1)}, bf16[1,1,80,16]{2,3,1,0:T(8,128)(2,1)}, u32[]{:S(2)}) copy-start(bf16[1,1,80,16]{2,3,1,0:T(8,128)(2,1)} %param.21) | copy-start | bytes 7684
  10.1 24.0 %copy-start.3 = (s32[1,192]{1,0:T(1,128)S(1)}, s32[1,192]{1,0:T(1,128)}, u32[]{:S(2)}) copy-start(s32[1,192]{1,0:T(1,128)} %param.23) | copy-start | bytes 2308
  11.9 51.9 %copy-start.4 = (bf16[1,512,192]{1,2,0:T(8,128)(2,1)S(1)}, bf16[1,512,192]{1,2,0:T(8,128)(2,1)}, u32[]{:S(2)}) copy-start(bf16[1,512,192]{1,2,0:T(8,128)(2,1)} %param.27) | copy-start | bytes 589828
  12.6 25.7 %all-to-all-start = ((bf16[16,16,512]{2,1,0:T(8,128)(2,1)}), bf16[16,16,512]{2,1,0:T(8,128)(2,1)S(1)}, u32[]{:S(2)}, u32[]{:S(2)}) async-start(bf16[16,16,512]{2,1,0:T(8,128)(2,1)} %bitcast.114), calls=%async_computation | async-start | bytes 524288 | tf_op jit(solution)/shard_map/all_to_all | solution.py:276
  26.5 126.6 %reduce-scatter.2.cloned.1.call-start = ((), (), s32[]{:S(2)}) async-start(), calls=%async_computation.3 | async-start | bytes 3342336 | tf_op jit(solution)/shard_map/reduce_scatter | solution.py:299
  26.9 11.5 %collective-permute-start.2 = (bf16[16,80]{1,0:T(8,128)(2,1)S(1)}, bf16[16,80]{1,0:T(8,128)(2,1)S(1)}, u32[]{:S(2)}, u32[]{:S(2)}) collective-permute-start(bf16[16,80]{1,0:T(8,128)(2,1)S(1)} %convolution_convert_fusion.6), channel_id=1, source_target_pairs={{0,3},{1,0},{2,1},{3,2},{4,7},{5,4},{6,5},{7,6},{8,11},{9,8},{10,9... | collective-permute-start | bytes 7688 | tf_op jit(solution)/shard_map/ppermute | solution.py:68
  28.8 9.6 %collective-permute-start.1 = (bf16[16,80]{1,0:T(8,128)(2,1)S(1)}, bf16[16,80]{1,0:T(8,128)(2,1)S(1)}, u32[]{:S(2)}, u32[]{:S(2)}) collective-permute-start(bf16[16,80]{1,0:T(8,128)(2,1)S(1)} %convolution_convert_fusion.6), channel_id=1, source_target_pairs={{0,2},{1,3},{2,0},{3,1},{4,6},{5,7},{6,4},{7,5},{8,10},{9,11},{10,... | collective-permute-start | bytes 7688 | tf_op jit(solution)/shard_map/ppermute | solution.py:68
  30.7 7.6 %collective-permute-start = (bf16[16,80]{1,0:T(8,128)(2,1)S(1)}, bf16[16,80]{1,0:T(8,128)(2,1)S(1)}, u32[]{:S(2)}, u32[]{:S(2)}) collective-permute-start(bf16[16,80]{1,0:T(8,128)(2,1)S(1)} %convolution_convert_fusion.6), channel_id=1, source_target_pairs={{0,1},{1,2},{2,3},{3,0},{4,5},{5,6},{6,7},{7,4},{8,9},{9,10},{10,1... | collective-permute-start | bytes 7688 | tf_op jit(solution)/shard_map/ppermute | solution.py:68
  74.6 0.9 copy-start.2
  74.6 20.1 %copy-start.5 = (bf16[192,512]{1,0:T(8,128)(2,1)S(1)}, bf16[192,512]{1,0:T(8,128)(2,1)}, u32[]{:S(2)}) copy-start(bf16[192,512]{1,0:T(8,128)(2,1)} %get-tuple-element.20) | copy-start | bytes 589828
  75.5 11.8 %collective-permute-start.5 = (bf16[192,512]{1,0:T(8,128)(2,1)S(1)}, bf16[192,512]{1,0:T(8,128)(2,1)S(1)}, u32[]{:S(2)}, u32[]{:S(2)}) collective-permute-start(bf16[192,512]{1,0:T(8,128)(2,1)S(1)} %copy-done.2), channel_id=1, source_target_pairs={{0,512},{1,513},{2,514},{3,515},{4,516},{5,517},{6,518},{7,519},{8... | collective-permute-start | bytes 589832 | tf_op jit(solution)/shard_map/ppermute | solution.py:78
  84.0 4.7 %collective-permute-start.4 = (bf16[192,512]{1,0:T(8,128)(2,1)S(1)}, bf16[192,512]{1,0:T(8,128)(2,1)S(1)}, u32[]{:S(2)}, u32[]{:S(2)}) collective-permute-start(bf16[192,512]{1,0:T(8,128)(2,1)S(1)} %copy-done.2), channel_id=1, source_target_pairs={{0,256},{1,257},{2,258},{3,259},{4,260},{5,261},{6,262},{7,263},{8... | collective-permute-start | bytes 589832 | tf_op jit(solution)/shard_map/ppermute | solution.py:78
  88.7 8.5 %collective-permute-start.7 = (bf16[192,128]{1,0:T(8,128)(2,1)S(1)}, bf16[192,128]{1,0:T(8,128)(2,1)S(1)}, u32[]{:S(2)}, u32[]{:S(2)}) collective-permute-start(bf16[192,128]{1,0:T(8,128)(2,1)S(1)} %get-tuple-element.50), channel_id=1, source_target_pairs={{0,709},{1,710},{2,711},{3,708},{4,725},{5,726},{6,727},{7,724},{8... | collective-permute-start | bytes 147464 | tf_op jit(solution)/shard_map/ppermute | solution.py:116
  90.6 6.6 %collective-permute-start.9 = (bf16[192,128]{1,0:T(8,128)(2,1)S(1)}, bf16[192,128]{1,0:T(8,128)(2,1)S(1)}, u32[]{:S(2)}, u32[]{:S(2)}) collective-permute-start(bf16[192,128]{1,0:T(8,128)(2,1)S(1)} %get-tuple-element.51), channel_id=1, source_target_pairs={{0,719},{1,716},{2,717},{3,718},{4,735},{5,732},{6,733},{7,734},{8... | collective-permute-start | bytes 147464 | tf_op jit(solution)/shard_map/ppermute | solution.py:116
  91.9 5.3 %collective-permute-start.8 = (bf16[192,128]{1,0:T(8,128)(2,1)S(1)}, bf16[192,128]{1,0:T(8,128)(2,1)S(1)}, u32[]{:S(2)}, u32[]{:S(2)}) collective-permute-start(bf16[192,128]{1,0:T(8,128)(2,1)S(1)} %get-tuple-element.52), channel_id=1, source_target_pairs={{0,714},{1,715},{2,712},{3,713},{4,730},{5,731},{6,728},{7,729},{8... | collective-permute-start | bytes 147464 | tf_op jit(solution)/shard_map/ppermute | solution.py:116
  93.2 4.0 %collective-permute-start.6 = (bf16[192,128]{1,0:T(8,128)(2,1)S(1)}, bf16[192,128]{1,0:T(8,128)(2,1)S(1)}, u32[]{:S(2)}, u32[]{:S(2)}) collective-permute-start(bf16[192,128]{1,0:T(8,128)(2,1)S(1)} %get-tuple-element.53), channel_id=1, source_target_pairs={{0,704},{1,705},{2,706},{3,707},{4,720},{5,721},{6,722},{7,723},{8... | collective-permute-start | bytes 147464 | tf_op jit(solution)/shard_map/ppermute | solution.py:116
  94.7 6.4 %collective-permute-start.10 = (bf16[192,512]{1,0:T(8,128)(2,1)S(1)}, bf16[192,512]{1,0:T(8,128)(2,1)S(1)}, u32[]{:S(2)}, u32[]{:S(2)}) collective-permute-start(bf16[192,512]{1,0:T(8,128)(2,1)S(1)} %copy-done.5), channel_id=1, source_target_pairs={{64,0},{128,64},{192,128},{256,192},{320,256},{384,320},{448,384},... | collective-permute-start | bytes 589832 | tf_op jit(solution)/shard_map/ppermute | solution.py:63
  129.6 23.5 %copy-start.1 = (bf16[192,512]{1,0:T(8,128)(2,1)S(1)}, bf16[192,512]{1,0:T(8,128)(2,1)}, u32[]{:S(2)}) copy-start(bf16[192,512]{1,0:T(8,128)(2,1)} %fusion.1.inputs_ref) | copy-start | bytes 589828
  130.0 11.6 %collective-permute-start.12 = (bf16[384,128]{1,0:T(8,128)(2,1)S(1)}, bf16[384,128]{1,0:T(8,128)(2,1)S(1)}, u32[]{:S(2)}, u32[]{:S(2)}) collective-permute-start(bf16[384,128]{1,0:T(8,128)(2,1)S(1)} %constant_dynamic-update-slice_fusion.5), channel_id=1, source_target_pairs={{0,128},{64,192},{128,256},{192,320},{256,384},{320,448},{384,512}... | collective-permute-start | bytes 294920 | tf_op jit(solution)/shard_map/ppermute | solution.py:68
  132.0 9.7 %collective-permute-start.11 = (bf16[384,128]{1,0:T(8,128)(2,1)S(1)}, bf16[384,128]{1,0:T(8,128)(2,1)S(1)}, u32[]{:S(2)}, u32[]{:S(2)}) collective-permute-start(bf16[384,128]{1,0:T(8,128)(2,1)S(1)} %constant_dynamic-update-slice_fusion), channel_id=1, source_target_pairs={{0,64},{64,128},{128,192},{192,256},{256,320},{320,384},{384,448},... | collective-permute-start | bytes 294920 | tf_op jit(solution)/shard_map/ppermute | solution.py:68
  138.6 6.6 %collective-permute-start.13 = (bf16[384,128]{1,0:T(8,128)(2,1)S(1)}, bf16[384,128]{1,0:T(8,128)(2,1)S(1)}, u32[]{:S(2)}, u32[]{:S(2)}) collective-permute-start(bf16[384,128]{1,0:T(8,128)(2,1)S(1)} %constant_dynamic-update-slice_fusion.10), channel_id=1, source_target_pairs={{0,704},{64,0},{128,64},{192,128},{256,192},{320,256},{384,320},{4... | collective-permute-start | bytes 294920 | tf_op jit(solution)/shard_map/ppermute | solution.py:68
  145.2 11.6 %collective-permute-start.16 = (bf16[1344,128]{1,0:T(8,128)(2,1)S(1)}, bf16[1344,128]{1,0:T(8,128)(2,1)S(1)}, u32[]{:S(2)}, u32[]{:S(2)}) collective-permute-start(bf16[1344,128]{1,0:T(8,128)(2,1)S(1)} %get-tuple-element.66.refs_0_), channel_id=1, source_target_pairs={{0,3},{1,0},{2,1},{3,2},{4,7},{5,4},{6,5},{7,6},{8,11},{9,8},{10,9... | collective-permute-start | bytes 1032200 | tf_op jit(solution)/shard_map/ppermute | solution.py:68
  147.1 11.7 %collective-permute-start.15 = (bf16[1344,128]{1,0:T(8,128)(2,1)S(1)}, bf16[1344,128]{1,0:T(8,128)(2,1)S(1)}, u32[]{:S(2)}, u32[]{:S(2)}) collective-permute-start(bf16[1344,128]{1,0:T(8,128)(2,1)S(1)} %get-tuple-element.66.refs_0_), channel_id=1, source_target_pairs={{0,2},{1,3},{2,0},{3,1},{4,6},{5,7},{6,4},{7,5},{8,10},{9,11},{10,... | collective-permute-start | bytes 1032200 | tf_op jit(solution)/shard_map/ppermute | solution.py:68
  150.5 17.3 %collective-permute-start.14 = (bf16[1344,128]{1,0:T(8,128)(2,1)S(1)}, bf16[1344,128]{1,0:T(8,128)(2,1)S(1)}, u32[]{:S(2)}, u32[]{:S(2)}) collective-permute-start(bf16[1344,128]{1,0:T(8,128)(2,1)S(1)} %get-tuple-element.66.refs_0_), channel_id=1, source_target_pairs={{0,1},{1,2},{2,3},{3,0},{4,5},{5,6},{6,7},{7,4},{8,9},{9,10},{10,1... | collective-permute-start | bytes 1032200 | tf_op jit(solution)/shard_map/ppermute | solution.py:68
  154.1 16.9 %collective-permute-start.3 = (bf16[192,512]{1,0:T(8,128)(2,1)S(1)}, bf16[192,512]{1,0:T(8,128)(2,1)S(1)}, u32[]{:S(2)}, u32[]{:S(2)}) collective-permute-start(bf16[192,512]{1,0:T(8,128)(2,1)S(1)} %fusion.17), channel_id=1, source_target_pairs={{0,64},{64,128},{128,192},{192,256},{256,320},{320,384},{384,448},... | collective-permute-start | bytes 589832 | tf_op jit(solution)/shard_map/ppermute | solution.py:63
Sparse Core Ops, SparseCore 0:
  11.0 54.2 all-gather.2
  74.7 64.3 reduce-scatter.1

commit v5 on v4

--- a/solution.py
+++ b/solution.py
@@ -150,21 +150,40 @@
 
 
 def section_kernel(
+    flag_ref,
     cotangent_ref,
-    inputs_ref,
+    parcel_ref,
+    visual_slot_ref,
+    text_ref,
     weight_ref,
     upstream_ref,
-    slot_ref,
+    past_slot_ref,
     product_ref,
     grad_ref,
     picked_ref,
+    inputs_ref,
     total,
 ):
     step = pl.program_id(0)
+    tokens, rows = text_ref.shape
+
+    def table(slot_ref):
+        positions = lax.broadcasted_iota(jnp.int32, (tokens, slot_ref.shape[1]), 0)
+        return (positions == slot_ref[...]).astype(jnp.float32)
 
     @pl.when(step == 0)
     def _():
         total[...] = upstream_ref[...].astype(jnp.float32)
+        slots = table(visual_slot_ref)
+        placed = jnp.dot(
+            slots.astype(jnp.bfloat16), parcel_ref[...], preferred_element_type=jnp.float32
+        )
+        covered = jnp.sum(slots, axis=1, keepdims=True) * flag_ref[0].astype(jnp.float32)
+        inputs_ref[...] = jnp.where(
+            jnp.broadcast_to(covered, (tokens, rows)) > 0.5,
+            placed,
+            text_ref[...].astype(jnp.float32),
+        ).astype(jnp.bfloat16)
 
     total[...] += lax.dot_general(
         cotangent_ref[...],
@@ -180,40 +199,46 @@
     def _():
         grad = total[...].astype(jnp.bfloat16)
         grad_ref[...] = grad
-        tokens, count = grad.shape[0], slot_ref.shape[1]
-        table = lax.broadcasted_iota(jnp.int32, (tokens, count), 0) == slot_ref[...]
         picked_ref[...] = lax.dot_general(
-            table.astype(jnp.float32).astype(jnp.bfloat16),
+            table(past_slot_ref).astype(jnp.bfloat16),
             grad,
             (((0,), (0,)), ((), ())),
             preferred_element_type=jnp.float32,
         ).astype(jnp.bfloat16)
 
 
-def section_products(cotangent, inputs, weight, upstream, slot):
-    tokens, rows = inputs.shape
+def section_products(flag, cotangent, parcel, visual_slot, text, weight, upstream, past_slot):
+    tokens, rows = text.shape
     width = weight.shape[1]
     tile = 2048
     whole = pl.BlockSpec((tokens, rows), lambda n: (0, 0))
+    slots = pl.BlockSpec(past_slot.shape, lambda n: (0, 0))
+    rows_shape = jax.ShapeDtypeStruct((tokens, rows), jnp.bfloat16)
+    count = past_slot.shape[1]
     return pl.pallas_call(
         section_kernel,
         grid=(width // tile,),
         in_specs=[
+            pl.BlockSpec(memory_space=pltpu.SMEM),
             pl.BlockSpec((tokens, tile), lambda n: (0, n)),
+            pl.BlockSpec((parcel.shape[0], rows), lambda n: (0, 0)),
+            slots,
             whole,
             pl.BlockSpec((rows, tile), lambda n: (0, n)),
             whole,
-            pl.BlockSpec(slot.shape, lambda n: (0, 0)),
+            slots,
         ],
         out_specs=[
             pl.BlockSpec((tokens, tile), lambda n: (0, n)),
             whole,
-            pl.BlockSpec((slot.shape[1], rows), lambda n: (0, 0)),
+            pl.BlockSpec((count, rows), lambda n: (0, 0)),
+            whole,
         ],
         out_shape=[
             jax.ShapeDtypeStruct((tokens, width), jnp.bfloat16),
-            jax.ShapeDtypeStruct((tokens, rows), jnp.bfloat16),
-            jax.ShapeDtypeStruct((slot.shape[1], rows), jnp.bfloat16),
+            rows_shape,
+            jax.ShapeDtypeStruct((count, rows), jnp.bfloat16),
+            rows_shape,
         ],
         scratch_shapes=[pltpu.VMEM((tokens, rows), jnp.float32)],
         compiler_params=pltpu.CompilerParams(vmem_limit_bytes=56 * 1024 * 1024),
@@ -222,7 +247,7 @@
             bytes_accessed=2 * (rows * width + 2 * tokens * width),
             transcendentals=0,
         ),
-    )(cotangent, inputs, weight, upstream, slot)
+    )(flag, cotangent, parcel, visual_slot, text, weight, upstream, past_slot)
 
 
 def local(
@@ -261,9 +286,6 @@
     current, _ = attend_parts(
         frame_query[0, 0], frame_key[0, 0], frame_value[0, 0], frame_segment[0, 0]
     )
-    columns = jnp.arange(token_count, dtype=jnp.int32)
-    slot_table = (visual_slot[0][:, None] == columns[None, :]).astype(jnp.bfloat16)
-
     terms = jnp.dot(current, visual_proj, preferred_element_type=jnp.float32).astype(jnp.bfloat16)
     terms = jnp.transpose(terms.reshape(group_rows, tensor_count, model_rows), (1, 0, 2))
     terms, past_query, past_key = lax.optimization_barrier((terms, past_query, past_key))
@@ -279,7 +301,6 @@
     parcel = lax.all_gather(
         jnp.concatenate([embedded, *past_all, spare], axis=1), "section", axis=0, tiled=True
     )
-    visual_rows = parcel[:, :model_rows]
     past_rows = jnp.concatenate(
         [
             parcel[:, model_rows + step * head_rows : model_rows + (step + 1) * head_rows]
@@ -287,14 +308,15 @@
         ],
         axis=0,
     )
-    placed = lax.dot_general(
-        slot_table, visual_rows, (((0,), (0,)), ((), ())), preferred_element_type=jnp.float32
-    ).astype(jnp.bfloat16)
-    covered = jnp.sum(slot_table, axis=0, dtype=jnp.float32)
-    inputs = jnp.where(first_flag & (covered[:, None] > 0.5), placed, layer_input[0].T)
-
-    products, input_grad, visual_grad = section_products(
-        pre_full, inputs, weight, layer_cotangent[0].T, past_slot
+    products, input_grad, visual_grad, inputs = section_products(
+        first_flag.astype(jnp.int32)[None],
+        pre_full,
+        parcel,
+        visual_slot,
+        layer_input[0].T,
+        weight,
+        layer_cotangent[0].T,
+        past_slot,
     )
     preact = lax.psum_scatter(products, "tensor", scatter_dimension=1, tiled=True).astype(
         jnp.float32
@@ -336,16 +358,29 @@
             replica_count * group_rows, part_width
         )
 
-    column_rows = own_columns.shape[0]
-    in_block, head_sum = [own_columns], head_of(own_section).astype(jnp.float32)
-    for step in range(1, BLOCK):
-        hops = step if step <= BLOCK // 2 else step - BLOCK
-        target = lax.rem(own_section + hops + section_count, section_count)
-        arrived = rotate(
-            jnp.concatenate([own_columns, head_of(target)], axis=0), "section", hops
-        )
-        in_block.append(arrived[:column_rows])
-        head_sum = head_sum + arrived[column_rows:].astype(jnp.float32)
+    column_rows, group_total = own_columns.shape[0], replica_count * group_rows
+
+    def section_at(hops):
+        return lax.rem(own_section + hops + section_count, section_count)
+
+    before = rotate(
+        jnp.concatenate([head_of(section_at(1)), own_columns, head_of(section_at(2))], axis=0),
+        "section",
+        1,
+    )
+    after = rotate(
+        jnp.concatenate([head_of(section_at(-1)), own_columns], axis=0), "section", -1
+    )
+    second = rotate(before[group_total:], "section", 1)
+    in_block = [
+        own_columns,
+        before[group_total : group_total + column_rows],
+        second[:column_rows],
+        after[group_total:],
+    ]
+    head_sum = head_of(own_section).astype(jnp.float32)
+    for terms in (before[:group_total], second[column_rows:], after[:group_total]):
+        head_sum = head_sum + terms.astype(jnp.float32)
 
     bundle = jnp.concatenate(in_block + [head_sum.astype(jnp.bfloat16)], axis=0)
     arrived = [rotate(bundle, "dp", step) for step in range(1, replica_count)]
@@ -361,6 +396,7 @@
         (bundle, *arrived),
         (per_block, head_rows, part_width),
     )
+    head_grad, forward_out = lax.optimization_barrier((head_grad, forward_out))
     frame_grads = attend_grad(past_saved, head_grad)
     return (forward_out.T[None], backward_out.T[None], grad_proj, frame_grads[:, None, None])
 

time: 180 us -> 178 us (0.989)
  waiting for transfers between devices: 27.8 us -> 25.8 us
    ppermute x4, waiting for transfers between devices: 1.28 us -> 4.77 us  [spread_columns(): piece = lax.ppermute(part, ('section', 'tensor', 'dp'), pairs)]
    ppermute x2, waiting for transfers between devices: 3.81 us -> 0.72 us  [shift(): lax.ppermute(value, axis, [(source, source + steps) for source in range(f...]
  transfers between devices with their start and end apart: 20 -> 20, of which waited for: 10 -> 9; matrix products, arithmetic and copies ran while one was open for 6% -> 4% of each run, Pallas kernels for 1% -> 1%
where the time goes in v5:
time: 178 us; the launch traced here: 177 us
  starting transfers between devices  57.9 us (33%)
  blocking collectives  53.4 us (30%)
  waiting for transfers between devices  25.8 us (14%)
  between operations  14.6 us (8%)
  Pallas kernels  11.6 us (7%)
  matrix products  5.32 us (3%)
  local copies, waits for them, and re-layouts  4.17 us (2%)
  other arithmetic  3.8 us (2%)
    all_gather x1, blocking collectives, local(): lax.all_gather(jnp.concatenate([embedded, *past_all, spare], axis=1), 'se...  26.8 us
    all_gather x1, blocking collectives, local(): gathered = lax.all_gather(piece, 'tensor', axis=0)  26.6 us
    ppermute x9, starting transfers between devices, rotate(): lax.ppermute(value, axis, [(i, (i + steps) % count) for i in range(count)])  26.5 us
    ppermute x9, waiting for transfers between devices, rotate(): lax.ppermute(value, axis, [(i, (i + steps) % count) for i in range(count)])  15.1 us
    all_to_all x1, starting transfers between devices, local(): terms = lax.all_to_all(terms, 'tensor', 0, 0, tiled=True)  13.8 us
    pallas_call x1, Pallas kernels, section_products(): pl.pallas_call(section_kernel, grid=(width // tile,), in_specs=[pl.BlockS...  9.62 us
    ppermute x2, starting transfers between devices, to_relays(): lax.ppermute(value, 'section', [(0, relay)])  9.11 us
    ppermute x4, starting transfers between devices, spread_columns(): piece = lax.ppermute(part, ('section', 'tensor', 'dp'), pairs)  5.8 us
  transfers between devices with their start and end apart: 20, of which 9 were waited for; matrix products, arithmetic and copies ran while one was open for 4% of the time, Pallas kernels for 1%

profile of v5, /device:TPU:1, one launch (start us, length us, event | category | flops | bytes accessed | tf_op | source)
XLA Modules:
  0.0 176.6 jit_solution(17845710916036080780)
XLA Ops:
  7.2 1.9 %fusion.15 = bf16[192,512]{1,0:T(8,128)(2,1)} fusion(bf16[1,512,192]{1,2,0:T(8,128)(2,1)} %param.28, bf16[1,512,192]{1,2,0:T(8,128)(2,1)} %param.29), kind=kLoop, calls=%fused_computation.33 | loop fusion | flops 1081344 | bytes 589824 | tf_op jit(solution)/shard_map/convert_element_type | solution.py:283
  10.1 1.8 %convolution_convert_fusion = bf16[16,8192]{1,0:T(8,128)(2,1)S(1)} fusion(bf16[80,8192]{1,0:T(8,128)(2,1)} %param.25, f32[16,16]{0,1:T(8,128)S(1)} %get-tuple-element.69, bf16[1,1,80,16]{2,3,1,0:T(8,128)(2,1)S(1)} %copy-done, f32[16]{0:T(128)S(1)} %fusion.35, f32[16]{0:T(128)S(1)} %get-tuple-element.68), kind=kOutput, calls=%fused_computation | convolution fusion | flops 21145600 | bytes 1576576 | tf_op jit(solution)/shard_map/dot_general | solution.py:289
  12.6 13.8 %all-to-all-start = ((bf16[16,16,512]{2,1,0:T(8,128)(2,1)}), bf16[16,16,512]{2,1,0:T(8,128)(2,1)S(1)}, u32[]{:S(2)}, u32[]{:S(2)}) async-start(bf16[16,16,512]{2,1,0:T(8,128)(2,1)} %bitcast.113), calls=%async_computation | async-start | bytes 524288 | tf_op jit(solution)/shard_map/all_to_all | solution.py:298
  26.9 1.9 %collective-permute-start = (bf16[16,80]{1,0:T(8,128)(2,1)S(1)}, bf16[16,80]{1,0:T(8,128)(2,1)S(1)}, u32[]{:S(2)}, u32[]{:S(2)}) collective-permute-start(bf16[16,80]{1,0:T(8,128)(2,1)S(1)} %convolution_convert_fusion.5), channel_id=1, source_target_pairs={{0,1},{1,2},{2,3},{3,0},{4,5},{5,6},{6,7},{7,4},{8,9},{9,10},{10,1... | collective-permute-start | bytes 7688 | tf_op jit(solution)/shard_map/ppermute | solution.py:68
  28.8 1.9 %collective-permute-start.1 = (bf16[16,80]{1,0:T(8,128)(2,1)S(1)}, bf16[16,80]{1,0:T(8,128)(2,1)S(1)}, u32[]{:S(2)}, u32[]{:S(2)}) collective-permute-start(bf16[16,80]{1,0:T(8,128)(2,1)S(1)} %convolution_convert_fusion.5), channel_id=1, source_target_pairs={{0,2},{1,3},{2,0},{3,1},{4,6},{5,7},{6,4},{7,5},{8,10},{9,11},{10,... | collective-permute-start | bytes 7688 | tf_op jit(solution)/shard_map/ppermute | solution.py:68
  30.7 4.6 %collective-permute-start.2 = (bf16[16,80]{1,0:T(8,128)(2,1)S(1)}, bf16[16,80]{1,0:T(8,128)(2,1)S(1)}, u32[]{:S(2)}, u32[]{:S(2)}) collective-permute-start(bf16[16,80]{1,0:T(8,128)(2,1)S(1)} %convolution_convert_fusion.5), channel_id=1, source_target_pairs={{0,3},{1,0},{2,1},{3,2},{4,7},{5,4},{6,5},{7,6},{8,11},{9,8},{10,9... | collective-permute-start | bytes 7688 | tf_op jit(solution)/shard_map/ppermute | solution.py:68
  35.3 3.0 %all-to-all-done = bf16[16,16,512]{2,1,0:T(8,128)(2,1)S(1)} async-done(((bf16[16,16,512]{2,1,0:T(8,128)(2,1)}), bf16[16,16,512]{2,1,0:T(8,128)(2,1)S(1)}, u32[]{:S(2)}, u32[]{:S(2)}) %all-to-all-start) | async-done | bytes 262176 | tf_op jit(solution)/shard_map/all_to_all | solution.py:298
  38.5 26.8 %all_gather.13.parcel_ref = bf16[192,896]{1,0:T(8,128)(2,1)} all-gather(bf16[16,896]{1,0:T(8,128)(2,1)S(1)} %concatenate.19), channel_id=1, replica_groups=mesh['section'=12,'tensor'=16,'dp'=4] {'section'}, dimensions={0}, use_global_device_ids=true | all-gather | bytes 372736 | tf_op jit(solution)/shard_map/all_gather | solution.py:301
  65.3 9.6 %shard_map.174 = (bf16[192,8192]{1,0:T(8,128)(2,1)}, bf16[192,512]{1,0:T(8,128)(2,1)}, bf16[192,512]{1,0:T(8,128)(2,1)}, bf16[192,512]{1,0:T(8,128)(2,1)}) custom-call(s32[1]{0:T(128)} %bitcast.flag_ref, bf16[192,8192]{1,0:T(8,128)(2,1)} %all-gather.3.cloned.1.call-done.cotangent_ref, bf16[192,896]{1,0:T(8,128)(2,1)} %all_gather.13.parcel_ref, ...), custom_call_target="tpu_custom_call" | custom-call | flops 3221225472 | bytes 14680064 | tf_op jit(solution)/shard_map/pallas_call | solution.py:218
  75.8 7.7 %collective-permute-start.3 = (bf16[192,512]{1,0:T(8,128)(2,1)S(1)}, bf16[192,512]{1,0:T(8,128)(2,1)S(1)}, u32[]{:S(2)}, u32[]{:S(2)}) collective-permute-start(bf16[192,512]{1,0:T(8,128)(2,1)S(1)} %copy-done.3), channel_id=1, source_target_pairs={{0,256},{1,257},{2,258},{3,259},{4,260},{5,261},{6,262},{7,263},{8... | collective-permute-start | bytes 589832 | tf_op jit(solution)/shard_map/ppermute | solution.py:78
  83.6 1.4 collective-permute-start.4
  86.6 1.4 collective-permute-done.4
  88.2 1.3 collective-permute-start.5
  89.5 1.9 %collective-permute-start.6 = (bf16[192,128]{1,0:T(8,128)(2,1)S(1)}, bf16[192,128]{1,0:T(8,128)(2,1)S(1)}, u32[]{:S(2)}, u32[]{:S(2)}) collective-permute-start(bf16[192,128]{1,0:T(8,128)(2,1)S(1)} %get-tuple-element.52), channel_id=1, source_target_pairs={{0,709},{1,710},{2,711},{3,708},{4,725},{5,726},{6,727},{7,724},{8... | collective-permute-start | bytes 147464 | tf_op jit(solution)/shard_map/ppermute | solution.py:116
  91.4 1.3 collective-permute-start.7
  92.7 1.3 collective-permute-start.8
  94.1 1.3 collective-permute-start.9
  95.4 4.8 %collective-permute-done.6 = bf16[192,128]{1,0:T(8,128)(2,1)S(1)} collective-permute-done((bf16[192,128]{1,0:T(8,128)(2,1)S(1)}, bf16[192,128]{1,0:T(8,128)(2,1)S(1)}, u32[]{:S(2)}, u32[]{:S(2)}) %collective-permute-start.6) | collective-permute-done | bytes 49184 | tf_op jit(solution)/shard_map/ppermute | solution.py:116
  100.9 26.6 %all-gather = bf16[3072,128]{1,0:T(8,128)(2,1)S(1)} all-gather(bf16[192,128]{1,0:T(8,128)(2,1)S(1)} %add_add_fusion.1), channel_id=2, replica_groups=mesh['section'=12,'tensor'=16,'dp'=4] {'tensor'}, dimensions={0}, use_global_device_ids=true | all-gather | bytes 835584 | tf_op jit(solution)/shard_map/all_gather | solution.py:329
  129.4 1.9 %collective-permute-start.10 = (bf16[448,128]{1,0:T(8,128)(2,1)S(1)}, bf16[448,128]{1,0:T(8,128)(2,1)S(1)}, u32[]{:S(2)}, u32[]{:S(2)}) collective-permute-start(bf16[448,128]{1,0:T(8,128)(2,1)S(1)} %constant_dynamic-update-slice_fusion), channel_id=1, source_target_pairs={{0,64},{64,128},{128,192},{192,256},{256,320},{320,384},{384,448},... | collective-permute-start | bytes 344072 | tf_op jit(solution)/shard_map/ppermute | solution.py:68
  131.3 4.6 %collective-permute-start.12 = (bf16[384,128]{1,0:T(8,128)(2,1)S(1)}, bf16[384,128]{1,0:T(8,128)(2,1)S(1)}, u32[]{:S(2)}, u32[]{:S(2)}) collective-permute-start(bf16[384,128]{1,0:T(8,128)(2,1)S(1)} %get-tuple-element.57), channel_id=1, source_target_pairs={{0,704},{64,0},{128,64},{192,128},{256,192},{320,256},{384,320},{4... | collective-permute-start | bytes 294920 | tf_op jit(solution)/shard_map/ppermute | solution.py:68
  135.9 1.3 collective-permute-done.10
  137.2 1.9 %collective-permute-start.11 = (bf16[384,128]{1,0:T(8,128)(2,1)S(1)}, bf16[384,128]{1,0:T(8,128)(2,1)S(1)}, u32[]{:S(2)}, u32[]{:S(2)}) collective-permute-start(bf16[384,128]{1,0:T(8,128)(2,1)S(1)} %slice.102), channel_id=1, source_target_pairs={{0,64},{64,128},{128,192},{192,256},{256,320},{320,384},{384,448},... | collective-permute-start | bytes 294920 | tf_op jit(solution)/shard_map/ppermute | solution.py:68
  139.2 4.6 %collective-permute-done.11 = bf16[384,128]{1,0:T(8,128)(2,1)S(1)} collective-permute-done((bf16[384,128]{1,0:T(8,128)(2,1)S(1)}, bf16[384,128]{1,0:T(8,128)(2,1)S(1)}, u32[]{:S(2)}, u32[]{:S(2)}) %collective-permute-start.11) | collective-permute-done | bytes 98336 | tf_op jit(solution)/shard_map/ppermute | solution.py:68
  143.9 2.9 %collective-permute-start.13 = (bf16[1344,128]{1,0:T(8,128)(2,1)S(1)}, bf16[1344,128]{1,0:T(8,128)(2,1)S(1)}, u32[]{:S(2)}, u32[]{:S(2)}) collective-permute-start(bf16[1344,128]{1,0:T(8,128)(2,1)S(1)} %get-tuple-element.72.refs_0_), channel_id=1, source_target_pairs={{0,1},{1,2},{2,3},{3,0},{4,5},{5,6},{6,7},{7,4},{8,9},{9,10},{10,1... | collective-permute-start | bytes 1032200 | tf_op jit(solution)/shard_map/ppermute | solution.py:68
  146.8 3.6 %collective-permute-start.14 = (bf16[1344,128]{1,0:T(8,128)(2,1)S(1)}, bf16[1344,128]{1,0:T(8,128)(2,1)S(1)}, u32[]{:S(2)}, u32[]{:S(2)}) collective-permute-start(bf16[1344,128]{1,0:T(8,128)(2,1)S(1)} %get-tuple-element.72.refs_0_), channel_id=1, source_target_pairs={{0,2},{1,3},{2,0},{3,1},{4,6},{5,7},{6,4},{7,5},{8,10},{9,11},{10,... | collective-permute-start | bytes 1032200 | tf_op jit(solution)/shard_map/ppermute | solution.py:68
  150.3 3.2 %collective-permute-start.15 = (bf16[1344,128]{1,0:T(8,128)(2,1)S(1)}, bf16[1344,128]{1,0:T(8,128)(2,1)S(1)}, u32[]{:S(2)}, u32[]{:S(2)}) collective-permute-start(bf16[1344,128]{1,0:T(8,128)(2,1)S(1)} %get-tuple-element.72.refs_0_), channel_id=1, source_target_pairs={{0,3},{1,0},{2,1},{3,2},{4,7},{5,4},{6,5},{7,6},{8,11},{9,8},{10,9... | collective-permute-start | bytes 1032200 | tf_op jit(solution)/shard_map/ppermute | solution.py:68
  153.7 1.1 fusion.16
  154.7 1.3 collective-permute-start.16
  156.0 5.7 %collective-permute-done.14.refs_2_ = bf16[1344,128]{1,0:T(8,128)(2,1)S(1)} collective-permute-done((bf16[1344,128]{1,0:T(8,128)(2,1)S(1)}, bf16[1344,128]{1,0:T(8,128)(2,1)S(1)}, u32[]{:S(2)}, u32[]{:S(2)}) %collective-permute-start.14) | collective-permute-done | bytes 344096 | tf_op jit(solution)/shard_map/ppermute | solution.py:68
  161.7 3.4 %collective-permute-done.15.refs_3_ = bf16[1344,128]{1,0:T(8,128)(2,1)S(1)} collective-permute-done((bf16[1344,128]{1,0:T(8,128)(2,1)S(1)}, bf16[1344,128]{1,0:T(8,128)(2,1)S(1)}, u32[]{:S(2)}, u32[]{:S(2)}) %collective-permute-start.15) | collective-permute-done | bytes 344096 | tf_op jit(solution)/shard_map/ppermute | solution.py:68
  165.2 2.0 %shard_map.175 = bf16[80,8192]{1,0:T(8,128)(2,1)} custom-call(s32[2]{0:T(128)S(1)} %pad_add_fusion.own_ref, bf16[1344,128]{1,0:T(8,128)(2,1)S(1)} %get-tuple-element.72.refs_0_, bf16[1344,128]{1,0:T(8,128)(2,1)S(1)} %collective-permute-done.13.refs_1_, bf16[1344,128]{1,0:T(8,128)(2,1)S(1)} %collective-permute-done.14.refs_2_, ...), custom_call_target="tpu_custom_call" | custom-call | tf_op jit(solution)/shard_map/pallas_call | solution.py:140
  (78 shorter events, 10.2 us)
Async XLA Ops:
  7.2 2.9 %copy-start = (bf16[1,1,80,16]{2,3,1,0:T(8,128)(2,1)S(1)}, bf16[1,1,80,16]{2,3,1,0:T(8,128)(2,1)}, u32[]{:S(2)}) copy-start(bf16[1,1,80,16]{2,3,1,0:T(8,128)(2,1)} %param.17) | copy-start | bytes 7684
  7.2 58.1 %all-gather.3.cloned.1.call-start = ((), (), s32[]{:S(2)}) async-start(), calls=%async_computation.2 | async-start | bytes 3342336 | tf_op jit(solution)/shard_map/all_gather | solution.py:284
  10.0 16.5 %copy-start.6 = (bf16[1,1,80,16]{2,3,1,0:T(8,128)(2,1)S(1)}, bf16[1,1,80,16]{2,3,1,0:T(8,128)(2,1)}, u32[]{:S(2)}) copy-start(bf16[1,1,80,16]{2,3,1,0:T(8,128)(2,1)} %param.20) | copy-start | bytes 7684
  10.0 16.5 %copy-start.7 = (bf16[1,1,80,16]{2,3,1,0:T(8,128)(2,1)S(1)}, bf16[1,1,80,16]{2,3,1,0:T(8,128)(2,1)}, u32[]{:S(2)}) copy-start(bf16[1,1,80,16]{2,3,1,0:T(8,128)(2,1)} %param.19) | copy-start | bytes 7684
  10.0 16.5 %copy-start.8 = (s32[1,1,16]{2,1,0:T(1,128)S(1)}, s32[1,1,16]{2,1,0:T(1,128)}, u32[]{:S(2)}) copy-start(s32[1,1,16]{2,1,0:T(1,128)} %param.22) | copy-start | bytes 196
  10.1 16.6 %copy-start.5 = (bf16[1,1,80,16]{2,3,1,0:T(8,128)(2,1)S(1)}, bf16[1,1,80,16]{2,3,1,0:T(8,128)(2,1)}, u32[]{:S(2)}) copy-start(bf16[1,1,80,16]{2,3,1,0:T(8,128)(2,1)} %param.21) | copy-start | bytes 7684
  12.6 25.7 %all-to-all-start = ((bf16[16,16,512]{2,1,0:T(8,128)(2,1)}), bf16[16,16,512]{2,1,0:T(8,128)(2,1)S(1)}, u32[]{:S(2)}, u32[]{:S(2)}) async-start(bf16[16,16,512]{2,1,0:T(8,128)(2,1)} %bitcast.113), calls=%async_computation | async-start | bytes 524288 | tf_op jit(solution)/shard_map/all_to_all | solution.py:298
  26.4 127.2 %reduce-scatter.2.cloned.1.call-start = ((), (), s32[]{:S(2)}) async-start(), calls=%async_computation.3 | async-start | bytes 3342336 | tf_op jit(solution)/shard_map/reduce_scatter | solution.py:321
  26.9 11.5 %collective-permute-start = (bf16[16,80]{1,0:T(8,128)(2,1)S(1)}, bf16[16,80]{1,0:T(8,128)(2,1)S(1)}, u32[]{:S(2)}, u32[]{:S(2)}) collective-permute-start(bf16[16,80]{1,0:T(8,128)(2,1)S(1)} %convolution_convert_fusion.5), channel_id=1, source_target_pairs={{0,1},{1,2},{2,3},{3,0},{4,5},{5,6},{6,7},{7,4},{8,9},{9,10},{10,1... | collective-permute-start | bytes 7688 | tf_op jit(solution)/shard_map/ppermute | solution.py:68
  28.8 9.6 %collective-permute-start.1 = (bf16[16,80]{1,0:T(8,128)(2,1)S(1)}, bf16[16,80]{1,0:T(8,128)(2,1)S(1)}, u32[]{:S(2)}, u32[]{:S(2)}) collective-permute-start(bf16[16,80]{1,0:T(8,128)(2,1)S(1)} %convolution_convert_fusion.5), channel_id=1, source_target_pairs={{0,2},{1,3},{2,0},{3,1},{4,6},{5,7},{6,4},{7,5},{8,10},{9,11},{10,... | collective-permute-start | bytes 7688 | tf_op jit(solution)/shard_map/ppermute | solution.py:68
  30.7 7.6 %collective-permute-start.2 = (bf16[16,80]{1,0:T(8,128)(2,1)S(1)}, bf16[16,80]{1,0:T(8,128)(2,1)S(1)}, u32[]{:S(2)}, u32[]{:S(2)}) collective-permute-start(bf16[16,80]{1,0:T(8,128)(2,1)S(1)} %convolution_convert_fusion.5), channel_id=1, source_target_pairs={{0,3},{1,0},{2,1},{3,2},{4,7},{5,4},{6,5},{7,6},{8,11},{9,8},{10,9... | collective-permute-start | bytes 7688 | tf_op jit(solution)/shard_map/ppermute | solution.py:68
  74.9 0.9 copy-start.3
  75.0 19.0 %copy-start.1 = (bf16[192,896]{1,0:T(8,128)(2,1)S(1)}, bf16[192,896]{1,0:T(8,128)(2,1)}, u32[]{:S(2)}) copy-start(bf16[192,896]{1,0:T(8,128)(2,1)} %all_gather.13.parcel_ref) | copy-start | bytes 1032196
  75.0 19.1 %copy-start.4 = (bf16[192,512]{1,0:T(8,128)(2,1)S(1)}, bf16[192,512]{1,0:T(8,128)(2,1)}, u32[]{:S(2)}) copy-start(bf16[192,512]{1,0:T(8,128)(2,1)} %get-tuple-element.22) | copy-start | bytes 589828
  75.8 10.8 %collective-permute-start.3 = (bf16[192,512]{1,0:T(8,128)(2,1)S(1)}, bf16[192,512]{1,0:T(8,128)(2,1)S(1)}, u32[]{:S(2)}, u32[]{:S(2)}) collective-permute-start(bf16[192,512]{1,0:T(8,128)(2,1)S(1)} %copy-done.3), channel_id=1, source_target_pairs={{0,256},{1,257},{2,258},{3,259},{4,260},{5,261},{6,262},{7,263},{8... | collective-permute-start | bytes 589832 | tf_op jit(solution)/shard_map/ppermute | solution.py:78
  83.6 4.5 %collective-permute-start.4 = (bf16[192,512]{1,0:T(8,128)(2,1)S(1)}, bf16[192,512]{1,0:T(8,128)(2,1)S(1)}, u32[]{:S(2)}, u32[]{:S(2)}) collective-permute-start(bf16[192,512]{1,0:T(8,128)(2,1)S(1)} %copy-done.3), channel_id=1, source_target_pairs={{0,512},{1,513},{2,514},{3,515},{4,516},{5,517},{6,518},{7,519},{8... | collective-permute-start | bytes 589832 | tf_op jit(solution)/shard_map/ppermute | solution.py:78
  88.2 7.3 %collective-permute-start.5 = (bf16[192,128]{1,0:T(8,128)(2,1)S(1)}, bf16[192,128]{1,0:T(8,128)(2,1)S(1)}, u32[]{:S(2)}, u32[]{:S(2)}) collective-permute-start(bf16[192,128]{1,0:T(8,128)(2,1)S(1)} %get-tuple-element.55), channel_id=1, source_target_pairs={{0,704},{1,705},{2,706},{3,707},{4,720},{5,721},{6,722},{7,723},{8... | collective-permute-start | bytes 147464 | tf_op jit(solution)/shard_map/ppermute | solution.py:116
  89.5 10.7 %collective-permute-start.6 = (bf16[192,128]{1,0:T(8,128)(2,1)S(1)}, bf16[192,128]{1,0:T(8,128)(2,1)S(1)}, u32[]{:S(2)}, u32[]{:S(2)}) collective-permute-start(bf16[192,128]{1,0:T(8,128)(2,1)S(1)} %get-tuple-element.52), channel_id=1, source_target_pairs={{0,709},{1,710},{2,711},{3,708},{4,725},{5,726},{6,727},{7,724},{8... | collective-permute-start | bytes 147464 | tf_op jit(solution)/shard_map/ppermute | solution.py:116
  91.4 8.8 %collective-permute-start.7 = (bf16[192,128]{1,0:T(8,128)(2,1)S(1)}, bf16[192,128]{1,0:T(8,128)(2,1)S(1)}, u32[]{:S(2)}, u32[]{:S(2)}) collective-permute-start(bf16[192,128]{1,0:T(8,128)(2,1)S(1)} %get-tuple-element.54), channel_id=1, source_target_pairs={{0,714},{1,715},{2,712},{3,713},{4,730},{5,731},{6,728},{7,729},{8... | collective-permute-start | bytes 147464 | tf_op jit(solution)/shard_map/ppermute | solution.py:116
  92.7 7.5 %collective-permute-start.8 = (bf16[192,128]{1,0:T(8,128)(2,1)S(1)}, bf16[192,128]{1,0:T(8,128)(2,1)S(1)}, u32[]{:S(2)}, u32[]{:S(2)}) collective-permute-start(bf16[192,128]{1,0:T(8,128)(2,1)S(1)} %get-tuple-element.53), channel_id=1, source_target_pairs={{0,719},{1,716},{2,717},{3,718},{4,735},{5,732},{6,733},{7,734},{8... | collective-permute-start | bytes 147464 | tf_op jit(solution)/shard_map/ppermute | solution.py:116
  94.1 6.8 %collective-permute-start.9 = (bf16[192,512]{1,0:T(8,128)(2,1)S(1)}, bf16[192,512]{1,0:T(8,128)(2,1)S(1)}, u32[]{:S(2)}, u32[]{:S(2)}) collective-permute-start(bf16[192,512]{1,0:T(8,128)(2,1)S(1)} %copy-done.4), channel_id=1, source_target_pairs={{64,0},{128,64},{192,128},{256,192},{320,256},{384,320},{448,384},... | collective-permute-start | bytes 589832 | tf_op jit(solution)/shard_map/ppermute | solution.py:63
  128.9 24.8 %copy-start.2 = (bf16[192,512]{1,0:T(8,128)(2,1)S(1)}, bf16[192,512]{1,0:T(8,128)(2,1)}, u32[]{:S(2)}) copy-start(bf16[192,512]{1,0:T(8,128)(2,1)} %get-tuple-element.24) | copy-start | bytes 589828
  129.4 7.8 %collective-permute-start.10 = (bf16[448,128]{1,0:T(8,128)(2,1)S(1)}, bf16[448,128]{1,0:T(8,128)(2,1)S(1)}, u32[]{:S(2)}, u32[]{:S(2)}) collective-permute-start(bf16[448,128]{1,0:T(8,128)(2,1)S(1)} %constant_dynamic-update-slice_fusion), channel_id=1, source_target_pairs={{0,64},{64,128},{128,192},{192,256},{256,320},{320,384},{384,448},... | collective-permute-start | bytes 344072 | tf_op jit(solution)/shard_map/ppermute | solution.py:68
  131.3 12.5 %collective-permute-start.12 = (bf16[384,128]{1,0:T(8,128)(2,1)S(1)}, bf16[384,128]{1,0:T(8,128)(2,1)S(1)}, u32[]{:S(2)}, u32[]{:S(2)}) collective-permute-start(bf16[384,128]{1,0:T(8,128)(2,1)S(1)} %get-tuple-element.57), channel_id=1, source_target_pairs={{0,704},{64,0},{128,64},{192,128},{256,192},{320,256},{384,320},{4... | collective-permute-start | bytes 294920 | tf_op jit(solution)/shard_map/ppermute | solution.py:68
  137.2 6.6 %collective-permute-start.11 = (bf16[384,128]{1,0:T(8,128)(2,1)S(1)}, bf16[384,128]{1,0:T(8,128)(2,1)S(1)}, u32[]{:S(2)}, u32[]{:S(2)}) collective-permute-start(bf16[384,128]{1,0:T(8,128)(2,1)S(1)} %slice.102), channel_id=1, source_target_pairs={{0,64},{64,128},{128,192},{192,256},{256,320},{320,384},{384,448},... | collective-permute-start | bytes 294920 | tf_op jit(solution)/shard_map/ppermute | solution.py:68
  143.9 12.1 %collective-permute-start.13 = (bf16[1344,128]{1,0:T(8,128)(2,1)S(1)}, bf16[1344,128]{1,0:T(8,128)(2,1)S(1)}, u32[]{:S(2)}, u32[]{:S(2)}) collective-permute-start(bf16[1344,128]{1,0:T(8,128)(2,1)S(1)} %get-tuple-element.72.refs_0_), channel_id=1, source_target_pairs={{0,1},{1,2},{2,3},{3,0},{4,5},{5,6},{6,7},{7,4},{8,9},{9,10},{10,1... | collective-permute-start | bytes 1032200 | tf_op jit(solution)/shard_map/ppermute | solution.py:68
  146.8 15.0 %collective-permute-start.14 = (bf16[1344,128]{1,0:T(8,128)(2,1)S(1)}, bf16[1344,128]{1,0:T(8,128)(2,1)S(1)}, u32[]{:S(2)}, u32[]{:S(2)}) collective-permute-start(bf16[1344,128]{1,0:T(8,128)(2,1)S(1)} %get-tuple-element.72.refs_0_), channel_id=1, source_target_pairs={{0,2},{1,3},{2,0},{3,1},{4,6},{5,7},{6,4},{7,5},{8,10},{9,11},{10,... | collective-permute-start | bytes 1032200 | tf_op jit(solution)/shard_map/ppermute | solution.py:68
  150.3 14.8 %collective-permute-start.15 = (bf16[1344,128]{1,0:T(8,128)(2,1)S(1)}, bf16[1344,128]{1,0:T(8,128)(2,1)S(1)}, u32[]{:S(2)}, u32[]{:S(2)}) collective-permute-start(bf16[1344,128]{1,0:T(8,128)(2,1)S(1)} %get-tuple-element.72.refs_0_), channel_id=1, source_target_pairs={{0,3},{1,0},{2,1},{3,2},{4,7},{5,4},{6,5},{7,6},{8,11},{9,8},{10,9... | collective-permute-start | bytes 1032200 | tf_op jit(solution)/shard_map/ppermute | solution.py:68
  154.7 12.4 %collective-permute-start.16 = (bf16[192,512]{1,0:T(8,128)(2,1)S(1)}, bf16[192,512]{1,0:T(8,128)(2,1)S(1)}, u32[]{:S(2)}, u32[]{:S(2)}) collective-permute-start(bf16[192,512]{1,0:T(8,128)(2,1)S(1)} %fusion.16), channel_id=1, source_target_pairs={{0,64},{64,128},{128,192},{192,256},{256,320},{320,384},{384,448},... | collective-permute-start | bytes 589832 | tf_op jit(solution)/shard_map/ppermute | solution.py:63
Sparse Core Ops, SparseCore 0:
  11.0 54.2 all-gather.2
  75.1 66.2 reduce-scatter.1

commit v6 on v5

--- a/solution.py
+++ b/solution.py
@@ -66,6 +66,16 @@
 def rotate(value, axis, steps):
     count = lax.axis_size(axis)
     return lax.ppermute(value, axis, [(i, (i + steps) % count) for i in range(count)])
+
+
+def rotate_apart(value, steps):
+    tensors, count = lax.axis_size("tensor"), lax.axis_size("dp")
+    pairs = [
+        (t * count + r, t * count + (r + (steps if t % 2 == 0 else -steps)) % count)
+        for t in range(tensors)
+        for r in range(count)
+    ]
+    return lax.ppermute(value, ("tensor", "dp"), pairs)
 
 
 BLOCK = 4
@@ -121,10 +131,10 @@
 def place_kernel(shape, own_ref, *refs):
     per_block, rows, width = shape
     pieces, out_ref = refs[:-1], refs[-1]
-    position, replica = own_ref[0], own_ref[1]
+    position, replica, odd = own_ref[0], own_ref[1], own_ref[2]
     replicas = len(pieces)
-    for step in range(replicas):
-        source = lax.rem(replica - step + replicas, replicas)
+    for step, back_by in enumerate((0, 1 + 2 * odd, 2, 3 - 2 * odd)):
+        source = lax.rem(replica - back_by + replicas, replicas)
         for back in range(BLOCK):
             place = lax.rem(position - back + BLOCK, BLOCK)
             for j in range(per_block):
@@ -210,7 +220,7 @@
 def section_products(flag, cotangent, parcel, visual_slot, text, weight, upstream, past_slot):
     tokens, rows = text.shape
     width = weight.shape[1]
-    tile = 2048
+    tile = 4096
     whole = pl.BlockSpec((tokens, rows), lambda n: (0, 0))
     slots = pl.BlockSpec(past_slot.shape, lambda n: (0, 0))
     rows_shape = jax.ShapeDtypeStruct((tokens, rows), jnp.bfloat16)
@@ -383,16 +393,20 @@
         head_sum = head_sum + terms.astype(jnp.float32)
 
     bundle = jnp.concatenate(in_block + [head_sum.astype(jnp.bfloat16)], axis=0)
-    arrived = [rotate(bundle, "dp", step) for step in range(1, replica_count)]
+    odd = lax.rem(lax.axis_index("tensor"), 2)
+    arrived = [rotate_apart(bundle, 1), rotate(bundle, "dp", 2), rotate_apart(bundle, -1)]
+    steps = [1 + 2 * odd, 2, 3 - 2 * odd]
     forward_out = shift(hidden, "section", 1)
     *arrived, _ = lax.optimization_barrier((*arrived, hidden))
     head_grad = head_sum[:group_rows]
-    for step in range(1, replica_count):
+    for step, bundle_there in zip(steps, arrived):
         first = BLOCK * column_rows + (replica_count - step) * group_rows
-        head_grad = head_grad + arrived[step - 1][first : first + group_rows].astype(jnp.float32)
+        head_grad = head_grad + lax.dynamic_slice_in_dim(
+            bundle_there, first, group_rows, axis=0
+        ).astype(jnp.float32)
     head_grad = head_grad[:, :head_rows].astype(jnp.bfloat16)
     grad_proj = place_columns(
-        jnp.stack([position, replica]).astype(jnp.int32),
+        jnp.stack([position, replica, odd]).astype(jnp.int32),
         (bundle, *arrived),
         (per_block, head_rows, part_width),
     )

time: 178 us -> 178 us (level)
  waiting for transfers between devices: 25.8 us -> 28.3 us
    ppermute x0 -> x2, waiting for transfers between devices: none -> 9.67 us  [rotate_apart(): return lax.ppermute(value, ('tensor', 'dp'), pairs)]
    ppermute x9 -> x7, waiting for transfers between devices: 15.1 us -> 7.91 us  [rotate(): lax.ppermute(value, axis, [(i, (i + steps) % count) for i in range(count)])]
    ppermute x9 -> x7, starting transfers between devices: 26.5 us -> 20.1 us  [rotate(): lax.ppermute(value, axis, [(i, (i + steps) % count) for i in range(count)])]
    ppermute x0 -> x2, starting transfers between devices: none -> 5.35 us  [rotate_apart(): return lax.ppermute(value, ('tensor', 'dp'), pairs)]
  transfers between devices with their start and end apart: 20 -> 20, of which waited for: 9 -> 10; matrix products, arithmetic and copies ran while one was open for 4% -> 4% of each run, Pallas kernels for 1% -> 1%
where the time goes in v6:
time: 178 us
  starting transfers between devices  56.8 us (32%)
  blocking collectives  53.3 us (30%)
  waiting for transfers between devices  28.3 us (16%)
  between operations  14.6 us (8%)
  Pallas kernels  11.3 us (6%)
  matrix products  5.31 us (3%)
  local copies, waits for them, and re-layouts  4.17 us (2%)
  other arithmetic  3.8 us (2%)
    all_gather x1, blocking collectives, local(): lax.all_gather(jnp.concatenate([embedded, *past_all, spare], axis=1), 'se...  26.8 us
    all_gather x1, blocking collectives, local(): gathered = lax.all_gather(piece, 'tensor', axis=0)  26.5 us
    ppermute x7, starting transfers between devices, rotate(): lax.ppermute(value, axis, [(i, (i + steps) % count) for i in range(count)])  20.1 us
    all_to_all x1, starting transfers between devices, local(): terms = lax.all_to_all(terms, 'tensor', 0, 0, tiled=True)  13.8 us
    ppermute x2, waiting for transfers between devices, rotate_apart(): return lax.ppermute(value, ('tensor', 'dp'), pairs)  9.67 us
    pallas_call x1, Pallas kernels, section_products(): pl.pallas_call(section_kernel, grid=(width // tile,), in_specs=[pl.BlockS...  9.32 us
    ppermute x2, starting transfers between devices, to_relays(): lax.ppermute(value, 'section', [(0, relay)])  9.1 us
    ppermute x7, waiting for transfers between devices, rotate(): lax.ppermute(value, axis, [(i, (i + steps) % count) for i in range(count)])  7.91 us
  transfers between devices with their start and end apart: 20, of which 10 were waited for; matrix products, arithmetic and copies ran while one was open for 4% of the time, Pallas kernels for 1%

profile of v6, /device:TPU:1, one launch (start us, length us, event | category | flops | bytes accessed | tf_op | source)
XLA Modules:
  0.0 177.6 jit_solution(4608922442726600295)
XLA Ops:
  7.2 1.9 %fusion.15 = bf16[192,512]{1,0:T(8,128)(2,1)} fusion(bf16[1,512,192]{1,2,0:T(8,128)(2,1)} %param.28, bf16[1,512,192]{1,2,0:T(8,128)(2,1)} %param.29), kind=kLoop, calls=%fused_computation.33 | loop fusion | flops 1081344 | bytes 589824 | tf_op jit(solution)/shard_map/convert_element_type | solution.py:293
  10.1 1.8 %convolution_convert_fusion = bf16[16,8192]{1,0:T(8,128)(2,1)S(1)} fusion(bf16[80,8192]{1,0:T(8,128)(2,1)} %param.25, f32[16,16]{0,1:T(8,128)S(1)} %get-tuple-element.69, bf16[1,1,80,16]{2,3,1,0:T(8,128)(2,1)S(1)} %copy-done, f32[16]{0:T(128)S(1)} %fusion.35, f32[16]{0:T(128)S(1)} %get-tuple-element.68), kind=kOutput, calls=%fused_computation | convolution fusion | flops 21145600 | bytes 1576576 | tf_op jit(solution)/shard_map/dot_general | solution.py:299
  12.6 13.8 %all-to-all-start = ((bf16[16,16,512]{2,1,0:T(8,128)(2,1)}), bf16[16,16,512]{2,1,0:T(8,128)(2,1)S(1)}, u32[]{:S(2)}, u32[]{:S(2)}) async-start(bf16[16,16,512]{2,1,0:T(8,128)(2,1)} %bitcast.114), calls=%async_computation | async-start | bytes 524288 | tf_op jit(solution)/shard_map/all_to_all | solution.py:308
  26.9 1.9 %collective-permute-start = (bf16[16,80]{1,0:T(8,128)(2,1)S(1)}, bf16[16,80]{1,0:T(8,128)(2,1)S(1)}, u32[]{:S(2)}, u32[]{:S(2)}) collective-permute-start(bf16[16,80]{1,0:T(8,128)(2,1)S(1)} %convolution_convert_fusion.5), channel_id=1, source_target_pairs={{0,1},{1,2},{2,3},{3,0},{4,5},{5,6},{6,7},{7,4},{8,9},{9,10},{10,1... | collective-permute-start | bytes 7688 | tf_op jit(solution)/shard_map/ppermute | solution.py:68
  28.8 1.9 %collective-permute-start.1 = (bf16[16,80]{1,0:T(8,128)(2,1)S(1)}, bf16[16,80]{1,0:T(8,128)(2,1)S(1)}, u32[]{:S(2)}, u32[]{:S(2)}) collective-permute-start(bf16[16,80]{1,0:T(8,128)(2,1)S(1)} %convolution_convert_fusion.5), channel_id=1, source_target_pairs={{0,2},{1,3},{2,0},{3,1},{4,6},{5,7},{6,4},{7,5},{8,10},{9,11},{10,... | collective-permute-start | bytes 7688 | tf_op jit(solution)/shard_map/ppermute | solution.py:68
  30.7 4.6 %collective-permute-start.2 = (bf16[16,80]{1,0:T(8,128)(2,1)S(1)}, bf16[16,80]{1,0:T(8,128)(2,1)S(1)}, u32[]{:S(2)}, u32[]{:S(2)}) collective-permute-start(bf16[16,80]{1,0:T(8,128)(2,1)S(1)} %convolution_convert_fusion.5), channel_id=1, source_target_pairs={{0,3},{1,0},{2,1},{3,2},{4,7},{5,4},{6,5},{7,6},{8,11},{9,8},{10,9... | collective-permute-start | bytes 7688 | tf_op jit(solution)/shard_map/ppermute | solution.py:68
  35.3 3.0 %all-to-all-done = bf16[16,16,512]{2,1,0:T(8,128)(2,1)S(1)} async-done(((bf16[16,16,512]{2,1,0:T(8,128)(2,1)}), bf16[16,16,512]{2,1,0:T(8,128)(2,1)S(1)}, u32[]{:S(2)}, u32[]{:S(2)}) %all-to-all-start) | async-done | bytes 262176 | tf_op jit(solution)/shard_map/all_to_all | solution.py:308
  38.5 26.8 %all_gather.13.parcel_ref = bf16[192,896]{1,0:T(8,128)(2,1)} all-gather(bf16[16,896]{1,0:T(8,128)(2,1)S(1)} %concatenate.19), channel_id=1, replica_groups=mesh['section'=12,'tensor'=16,'dp'=4] {'section'}, dimensions={0}, use_global_device_ids=true | all-gather | bytes 372736 | tf_op jit(solution)/shard_map/all_gather | solution.py:311
  65.3 9.3 %shard_map.174 = (bf16[192,8192]{1,0:T(8,128)(2,1)}, bf16[192,512]{1,0:T(8,128)(2,1)}, bf16[192,512]{1,0:T(8,128)(2,1)}, bf16[192,512]{1,0:T(8,128)(2,1)}) custom-call(s32[1]{0:T(128)} %bitcast.flag_ref, bf16[192,8192]{1,0:T(8,128)(2,1)} %all-gather.3.cloned.1.call-done.cotangent_ref, bf16[192,896]{1,0:T(8,128)(2,1)} %all_gather.13.parcel_ref, ...), custom_call_target="tpu_custom_call" | custom-call | flops 3221225472 | bytes 14680064 | tf_op jit(solution)/shard_map/pallas_call | solution.py:228
  75.5 7.7 %collective-permute-start.3 = (bf16[192,512]{1,0:T(8,128)(2,1)S(1)}, bf16[192,512]{1,0:T(8,128)(2,1)S(1)}, u32[]{:S(2)}, u32[]{:S(2)}) collective-permute-start(bf16[192,512]{1,0:T(8,128)(2,1)S(1)} %copy-done.3), channel_id=1, source_target_pairs={{0,256},{1,257},{2,258},{3,259},{4,260},{5,261},{6,262},{7,263},{8... | collective-permute-start | bytes 589832 | tf_op jit(solution)/shard_map/ppermute | solution.py:88
  83.3 1.4 collective-permute-start.4
  86.3 1.4 collective-permute-done.4
  87.8 1.3 collective-permute-start.5
  89.1 1.9 %collective-permute-start.6 = (bf16[192,128]{1,0:T(8,128)(2,1)S(1)}, bf16[192,128]{1,0:T(8,128)(2,1)S(1)}, u32[]{:S(2)}, u32[]{:S(2)}) collective-permute-start(bf16[192,128]{1,0:T(8,128)(2,1)S(1)} %get-tuple-element.52), channel_id=1, source_target_pairs={{0,709},{1,710},{2,711},{3,708},{4,725},{5,726},{6,727},{7,724},{8... | collective-permute-start | bytes 147464 | tf_op jit(solution)/shard_map/ppermute | solution.py:126
  91.1 1.3 collective-permute-start.7
  92.4 1.3 collective-permute-start.8
  93.8 1.3 collective-permute-start.9
  95.1 4.8 %collective-permute-done.6 = bf16[192,128]{1,0:T(8,128)(2,1)S(1)} collective-permute-done((bf16[192,128]{1,0:T(8,128)(2,1)S(1)}, bf16[192,128]{1,0:T(8,128)(2,1)S(1)}, u32[]{:S(2)}, u32[]{:S(2)}) %collective-permute-start.6) | collective-permute-done | bytes 49184 | tf_op jit(solution)/shard_map/ppermute | solution.py:126
  100.6 26.5 %all-gather = bf16[3072,128]{1,0:T(8,128)(2,1)S(1)} all-gather(bf16[192,128]{1,0:T(8,128)(2,1)S(1)} %add_add_fusion.1), channel_id=2, replica_groups=mesh['section'=12,'tensor'=16,'dp'=4] {'tensor'}, dimensions={0}, use_global_device_ids=true | all-gather | bytes 835584 | tf_op jit(solution)/shard_map/all_gather | solution.py:339
  129.0 1.9 %collective-permute-start.10 = (bf16[448,128]{1,0:T(8,128)(2,1)S(1)}, bf16[448,128]{1,0:T(8,128)(2,1)S(1)}, u32[]{:S(2)}, u32[]{:S(2)}) collective-permute-start(bf16[448,128]{1,0:T(8,128)(2,1)S(1)} %constant_dynamic-update-slice_fusion), channel_id=1, source_target_pairs={{0,64},{64,128},{128,192},{192,256},{256,320},{320,384},{384,448},... | collective-permute-start | bytes 344072 | tf_op jit(solution)/shard_map/ppermute | solution.py:68
  130.9 4.6 %collective-permute-start.12 = (bf16[384,128]{1,0:T(8,128)(2,1)S(1)}, bf16[384,128]{1,0:T(8,128)(2,1)S(1)}, u32[]{:S(2)}, u32[]{:S(2)}) collective-permute-start(bf16[384,128]{1,0:T(8,128)(2,1)S(1)} %get-tuple-element.57), channel_id=1, source_target_pairs={{0,704},{64,0},{128,64},{192,128},{256,192},{320,256},{384,320},{4... | collective-permute-start | bytes 294920 | tf_op jit(solution)/shard_map/ppermute | solution.py:68
  135.5 1.3 collective-permute-done.10
  136.8 1.9 %collective-permute-start.11 = (bf16[384,128]{1,0:T(8,128)(2,1)S(1)}, bf16[384,128]{1,0:T(8,128)(2,1)S(1)}, u32[]{:S(2)}, u32[]{:S(2)}) collective-permute-start(bf16[384,128]{1,0:T(8,128)(2,1)S(1)} %slice.90), channel_id=1, source_target_pairs={{0,64},{64,128},{128,192},{192,256},{256,320},{320,384},{384,448},... | collective-permute-start | bytes 294920 | tf_op jit(solution)/shard_map/ppermute | solution.py:68
  138.8 4.6 %collective-permute-done.11 = bf16[384,128]{1,0:T(8,128)(2,1)S(1)} collective-permute-done((bf16[384,128]{1,0:T(8,128)(2,1)S(1)}, bf16[384,128]{1,0:T(8,128)(2,1)S(1)}, u32[]{:S(2)}, u32[]{:S(2)}) %collective-permute-start.11) | collective-permute-done | bytes 98336 | tf_op jit(solution)/shard_map/ppermute | solution.py:68
  143.5 3.4 %collective-permute-start.13 = (bf16[1344,128]{1,0:T(8,128)(2,1)S(1)}, bf16[1344,128]{1,0:T(8,128)(2,1)S(1)}, u32[]{:S(2)}, u32[]{:S(2)}) collective-permute-start(bf16[1344,128]{1,0:T(8,128)(2,1)S(1)} %get-tuple-element.72.refs_0_), channel_id=1, source_target_pairs={{0,1},{1,2},{2,3},{3,0},{4,7},{5,4},{6,5},{7,6},{8,9},{9,10},{10,1... | collective-permute-start | bytes 1032200 | tf_op jit(solution)/shard_map/ppermute | solution.py:78
  146.9 3.2 %collective-permute-start.14 = (bf16[1344,128]{1,0:T(8,128)(2,1)S(1)}, bf16[1344,128]{1,0:T(8,128)(2,1)S(1)}, u32[]{:S(2)}, u32[]{:S(2)}) collective-permute-start(bf16[1344,128]{1,0:T(8,128)(2,1)S(1)} %get-tuple-element.72.refs_0_), channel_id=1, source_target_pairs={{0,2},{1,3},{2,0},{3,1},{4,6},{5,7},{6,4},{7,5},{8,10},{9,11},{10,... | collective-permute-start | bytes 1032200 | tf_op jit(solution)/shard_map/ppermute | solution.py:68
  150.2 1.9 %collective-permute-start.15 = (bf16[1344,128]{1,0:T(8,128)(2,1)S(1)}, bf16[1344,128]{1,0:T(8,128)(2,1)S(1)}, u32[]{:S(2)}, u32[]{:S(2)}) collective-permute-start(bf16[1344,128]{1,0:T(8,128)(2,1)S(1)} %get-tuple-element.72.refs_0_), channel_id=1, source_target_pairs={{0,3},{1,0},{2,1},{3,2},{4,5},{5,6},{6,7},{7,4},{8,11},{9,8},{10,9... | collective-permute-start | bytes 1032200 | tf_op jit(solution)/shard_map/ppermute | solution.py:78
  153.2 1.3 collective-permute-start.16
  154.5 3.9 %collective-permute-done.13.refs_1_ = bf16[1344,128]{1,0:T(8,128)(2,1)S(1)} collective-permute-done((bf16[1344,128]{1,0:T(8,128)(2,1)S(1)}, bf16[1344,128]{1,0:T(8,128)(2,1)S(1)}, u32[]{:S(2)}, u32[]{:S(2)}) %collective-permute-start.13) | collective-permute-done | bytes 344096 | tf_op jit(solution)/shard_map/ppermute | solution.py:78
  158.5 2.0 %collective-permute-done.14.refs_2_ = bf16[1344,128]{1,0:T(8,128)(2,1)S(1)} collective-permute-done((bf16[1344,128]{1,0:T(8,128)(2,1)S(1)}, bf16[1344,128]{1,0:T(8,128)(2,1)S(1)}, u32[]{:S(2)}, u32[]{:S(2)}) %collective-permute-start.14) | collective-permute-done | bytes 344096 | tf_op jit(solution)/shard_map/ppermute | solution.py:68
  160.4 5.8 %collective-permute-done.15.refs_3_ = bf16[1344,128]{1,0:T(8,128)(2,1)S(1)} collective-permute-done((bf16[1344,128]{1,0:T(8,128)(2,1)S(1)}, bf16[1344,128]{1,0:T(8,128)(2,1)S(1)}, u32[]{:S(2)}, u32[]{:S(2)}) %collective-permute-start.15) | collective-permute-done | bytes 344096 | tf_op jit(solution)/shard_map/ppermute | solution.py:78
  166.2 2.0 %shard_map.175 = bf16[80,8192]{1,0:T(8,128)(2,1)} custom-call(s32[3]{0:T(128)S(1)} %pad_add_fusion.own_ref, bf16[1344,128]{1,0:T(8,128)(2,1)S(1)} %get-tuple-element.72.refs_0_, bf16[1344,128]{1,0:T(8,128)(2,1)S(1)} %collective-permute-done.13.refs_1_, bf16[1344,128]{1,0:T(8,128)(2,1)S(1)} %collective-permute-done.14.refs_2_, ...), custom_call_target="tpu_custom_call" | custom-call | tf_op jit(solution)/shard_map/pallas_call | solution.py:150
  (76 shorter events, 11.3 us)
Async XLA Ops:
  7.2 2.9 %copy-start = (bf16[1,1,80,16]{2,3,1,0:T(8,128)(2,1)S(1)}, bf16[1,1,80,16]{2,3,1,0:T(8,128)(2,1)}, u32[]{:S(2)}) copy-start(bf16[1,1,80,16]{2,3,1,0:T(8,128)(2,1)} %param.17) | copy-start | bytes 7684
  7.2 58.1 %all-gather.3.cloned.1.call-start = ((), (), s32[]{:S(2)}) async-start(), calls=%async_computation.2 | async-start | bytes 3342336 | tf_op jit(solution)/shard_map/all_gather | solution.py:294
  10.0 16.5 %copy-start.6 = (bf16[1,1,80,16]{2,3,1,0:T(8,128)(2,1)S(1)}, bf16[1,1,80,16]{2,3,1,0:T(8,128)(2,1)}, u32[]{:S(2)}) copy-start(bf16[1,1,80,16]{2,3,1,0:T(8,128)(2,1)} %param.20) | copy-start | bytes 7684
  10.0 16.5 %copy-start.7 = (bf16[1,1,80,16]{2,3,1,0:T(8,128)(2,1)S(1)}, bf16[1,1,80,16]{2,3,1,0:T(8,128)(2,1)}, u32[]{:S(2)}) copy-start(bf16[1,1,80,16]{2,3,1,0:T(8,128)(2,1)} %param.19) | copy-start | bytes 7684
  10.0 16.5 %copy-start.8 = (s32[1,1,16]{2,1,0:T(1,128)S(1)}, s32[1,1,16]{2,1,0:T(1,128)}, u32[]{:S(2)}) copy-start(s32[1,1,16]{2,1,0:T(1,128)} %param.22) | copy-start | bytes 196
  10.1 16.6 %copy-start.5 = (bf16[1,1,80,16]{2,3,1,0:T(8,128)(2,1)S(1)}, bf16[1,1,80,16]{2,3,1,0:T(8,128)(2,1)}, u32[]{:S(2)}) copy-start(bf16[1,1,80,16]{2,3,1,0:T(8,128)(2,1)} %param.21) | copy-start | bytes 7684
  12.6 25.7 %all-to-all-start = ((bf16[16,16,512]{2,1,0:T(8,128)(2,1)}), bf16[16,16,512]{2,1,0:T(8,128)(2,1)S(1)}, u32[]{:S(2)}, u32[]{:S(2)}) async-start(bf16[16,16,512]{2,1,0:T(8,128)(2,1)} %bitcast.114), calls=%async_computation | async-start | bytes 524288 | tf_op jit(solution)/shard_map/all_to_all | solution.py:308
  26.4 125.7 %reduce-scatter.2.cloned.1.call-start = ((), (), s32[]{:S(2)}) async-start(), calls=%async_computation.3 | async-start | bytes 3342336 | tf_op jit(solution)/shard_map/reduce_scatter | solution.py:331
  26.9 11.5 %collective-permute-start = (bf16[16,80]{1,0:T(8,128)(2,1)S(1)}, bf16[16,80]{1,0:T(8,128)(2,1)S(1)}, u32[]{:S(2)}, u32[]{:S(2)}) collective-permute-start(bf16[16,80]{1,0:T(8,128)(2,1)S(1)} %convolution_convert_fusion.5), channel_id=1, source_target_pairs={{0,1},{1,2},{2,3},{3,0},{4,5},{5,6},{6,7},{7,4},{8,9},{9,10},{10,1... | collective-permute-start | bytes 7688 | tf_op jit(solution)/shard_map/ppermute | solution.py:68
  28.8 9.6 %collective-permute-start.1 = (bf16[16,80]{1,0:T(8,128)(2,1)S(1)}, bf16[16,80]{1,0:T(8,128)(2,1)S(1)}, u32[]{:S(2)}, u32[]{:S(2)}) collective-permute-start(bf16[16,80]{1,0:T(8,128)(2,1)S(1)} %convolution_convert_fusion.5), channel_id=1, source_target_pairs={{0,2},{1,3},{2,0},{3,1},{4,6},{5,7},{6,4},{7,5},{8,10},{9,11},{10,... | collective-permute-start | bytes 7688 | tf_op jit(solution)/shard_map/ppermute | solution.py:68
  30.7 7.6 %collective-permute-start.2 = (bf16[16,80]{1,0:T(8,128)(2,1)S(1)}, bf16[16,80]{1,0:T(8,128)(2,1)S(1)}, u32[]{:S(2)}, u32[]{:S(2)}) collective-permute-start(bf16[16,80]{1,0:T(8,128)(2,1)S(1)} %convolution_convert_fusion.5), channel_id=1, source_target_pairs={{0,3},{1,0},{2,1},{3,2},{4,7},{5,4},{6,5},{7,6},{8,11},{9,8},{10,9... | collective-permute-start | bytes 7688 | tf_op jit(solution)/shard_map/ppermute | solution.py:68
  74.6 0.9 copy-start.3
  74.6 19.0 %copy-start.1 = (bf16[192,896]{1,0:T(8,128)(2,1)S(1)}, bf16[192,896]{1,0:T(8,128)(2,1)}, u32[]{:S(2)}) copy-start(bf16[192,896]{1,0:T(8,128)(2,1)} %all_gather.13.parcel_ref) | copy-start | bytes 1032196
  74.7 19.1 %copy-start.4 = (bf16[192,512]{1,0:T(8,128)(2,1)S(1)}, bf16[192,512]{1,0:T(8,128)(2,1)}, u32[]{:S(2)}) copy-start(bf16[192,512]{1,0:T(8,128)(2,1)} %get-tuple-element.22) | copy-start | bytes 589828
  75.5 10.8 %collective-permute-start.3 = (bf16[192,512]{1,0:T(8,128)(2,1)S(1)}, bf16[192,512]{1,0:T(8,128)(2,1)S(1)}, u32[]{:S(2)}, u32[]{:S(2)}) collective-permute-start(bf16[192,512]{1,0:T(8,128)(2,1)S(1)} %copy-done.3), channel_id=1, source_target_pairs={{0,256},{1,257},{2,258},{3,259},{4,260},{5,261},{6,262},{7,263},{8... | collective-permute-start | bytes 589832 | tf_op jit(solution)/shard_map/ppermute | solution.py:88
  83.3 4.5 %collective-permute-start.4 = (bf16[192,512]{1,0:T(8,128)(2,1)S(1)}, bf16[192,512]{1,0:T(8,128)(2,1)S(1)}, u32[]{:S(2)}, u32[]{:S(2)}) collective-permute-start(bf16[192,512]{1,0:T(8,128)(2,1)S(1)} %copy-done.3), channel_id=1, source_target_pairs={{0,512},{1,513},{2,514},{3,515},{4,516},{5,517},{6,518},{7,519},{8... | collective-permute-start | bytes 589832 | tf_op jit(solution)/shard_map/ppermute | solution.py:88
  87.8 7.3 %collective-permute-start.5 = (bf16[192,128]{1,0:T(8,128)(2,1)S(1)}, bf16[192,128]{1,0:T(8,128)(2,1)S(1)}, u32[]{:S(2)}, u32[]{:S(2)}) collective-permute-start(bf16[192,128]{1,0:T(8,128)(2,1)S(1)} %get-tuple-element.55), channel_id=1, source_target_pairs={{0,704},{1,705},{2,706},{3,707},{4,720},{5,721},{6,722},{7,723},{8... | collective-permute-start | bytes 147464 | tf_op jit(solution)/shard_map/ppermute | solution.py:126
  89.1 10.8 %collective-permute-start.6 = (bf16[192,128]{1,0:T(8,128)(2,1)S(1)}, bf16[192,128]{1,0:T(8,128)(2,1)S(1)}, u32[]{:S(2)}, u32[]{:S(2)}) collective-permute-start(bf16[192,128]{1,0:T(8,128)(2,1)S(1)} %get-tuple-element.52), channel_id=1, source_target_pairs={{0,709},{1,710},{2,711},{3,708},{4,725},{5,726},{6,727},{7,724},{8... | collective-permute-start | bytes 147464 | tf_op jit(solution)/shard_map/ppermute | solution.py:126
  91.1 8.8 %collective-permute-start.7 = (bf16[192,128]{1,0:T(8,128)(2,1)S(1)}, bf16[192,128]{1,0:T(8,128)(2,1)S(1)}, u32[]{:S(2)}, u32[]{:S(2)}) collective-permute-start(bf16[192,128]{1,0:T(8,128)(2,1)S(1)} %get-tuple-element.54), channel_id=1, source_target_pairs={{0,714},{1,715},{2,712},{3,713},{4,730},{5,731},{6,728},{7,729},{8... | collective-permute-start | bytes 147464 | tf_op jit(solution)/shard_map/ppermute | solution.py:126
  92.4 7.5 %collective-permute-start.8 = (bf16[192,128]{1,0:T(8,128)(2,1)S(1)}, bf16[192,128]{1,0:T(8,128)(2,1)S(1)}, u32[]{:S(2)}, u32[]{:S(2)}) collective-permute-start(bf16[192,128]{1,0:T(8,128)(2,1)S(1)} %get-tuple-element.53), channel_id=1, source_target_pairs={{0,719},{1,716},{2,717},{3,718},{4,735},{5,732},{6,733},{7,734},{8... | collective-permute-start | bytes 147464 | tf_op jit(solution)/shard_map/ppermute | solution.py:126
  93.8 6.8 %collective-permute-start.9 = (bf16[192,512]{1,0:T(8,128)(2,1)S(1)}, bf16[192,512]{1,0:T(8,128)(2,1)S(1)}, u32[]{:S(2)}, u32[]{:S(2)}) collective-permute-start(bf16[192,512]{1,0:T(8,128)(2,1)S(1)} %copy-done.4), channel_id=1, source_target_pairs={{64,0},{128,64},{192,128},{256,192},{320,256},{384,320},{448,384},... | collective-permute-start | bytes 589832 | tf_op jit(solution)/shard_map/ppermute | solution.py:63
  128.5 23.7 %copy-start.2 = (bf16[192,512]{1,0:T(8,128)(2,1)S(1)}, bf16[192,512]{1,0:T(8,128)(2,1)}, u32[]{:S(2)}) copy-start(bf16[192,512]{1,0:T(8,128)(2,1)} %get-tuple-element.24) | copy-start | bytes 589828
  129.0 7.8 %collective-permute-start.10 = (bf16[448,128]{1,0:T(8,128)(2,1)S(1)}, bf16[448,128]{1,0:T(8,128)(2,1)S(1)}, u32[]{:S(2)}, u32[]{:S(2)}) collective-permute-start(bf16[448,128]{1,0:T(8,128)(2,1)S(1)} %constant_dynamic-update-slice_fusion), channel_id=1, source_target_pairs={{0,64},{64,128},{128,192},{192,256},{256,320},{320,384},{384,448},... | collective-permute-start | bytes 344072 | tf_op jit(solution)/shard_map/ppermute | solution.py:68
  130.9 12.5 %collective-permute-start.12 = (bf16[384,128]{1,0:T(8,128)(2,1)S(1)}, bf16[384,128]{1,0:T(8,128)(2,1)S(1)}, u32[]{:S(2)}, u32[]{:S(2)}) collective-permute-start(bf16[384,128]{1,0:T(8,128)(2,1)S(1)} %get-tuple-element.57), channel_id=1, source_target_pairs={{0,704},{64,0},{128,64},{192,128},{256,192},{320,256},{384,320},{4... | collective-permute-start | bytes 294920 | tf_op jit(solution)/shard_map/ppermute | solution.py:68
  136.8 6.6 %collective-permute-start.11 = (bf16[384,128]{1,0:T(8,128)(2,1)S(1)}, bf16[384,128]{1,0:T(8,128)(2,1)S(1)}, u32[]{:S(2)}, u32[]{:S(2)}) collective-permute-start(bf16[384,128]{1,0:T(8,128)(2,1)S(1)} %slice.90), channel_id=1, source_target_pairs={{0,64},{64,128},{128,192},{192,256},{256,320},{320,384},{384,448},... | collective-permute-start | bytes 294920 | tf_op jit(solution)/shard_map/ppermute | solution.py:68
  143.5 15.0 %collective-permute-start.13 = (bf16[1344,128]{1,0:T(8,128)(2,1)S(1)}, bf16[1344,128]{1,0:T(8,128)(2,1)S(1)}, u32[]{:S(2)}, u32[]{:S(2)}) collective-permute-start(bf16[1344,128]{1,0:T(8,128)(2,1)S(1)} %get-tuple-element.72.refs_0_), channel_id=1, source_target_pairs={{0,1},{1,2},{2,3},{3,0},{4,7},{5,4},{6,5},{7,6},{8,9},{9,10},{10,1... | collective-permute-start | bytes 1032200 | tf_op jit(solution)/shard_map/ppermute | solution.py:78
  146.9 13.5 %collective-permute-start.14 = (bf16[1344,128]{1,0:T(8,128)(2,1)S(1)}, bf16[1344,128]{1,0:T(8,128)(2,1)S(1)}, u32[]{:S(2)}, u32[]{:S(2)}) collective-permute-start(bf16[1344,128]{1,0:T(8,128)(2,1)S(1)} %get-tuple-element.72.refs_0_), channel_id=1, source_target_pairs={{0,2},{1,3},{2,0},{3,1},{4,6},{5,7},{6,4},{7,5},{8,10},{9,11},{10,... | collective-permute-start | bytes 1032200 | tf_op jit(solution)/shard_map/ppermute | solution.py:68
  150.2 16.0 %collective-permute-start.15 = (bf16[1344,128]{1,0:T(8,128)(2,1)S(1)}, bf16[1344,128]{1,0:T(8,128)(2,1)S(1)}, u32[]{:S(2)}, u32[]{:S(2)}) collective-permute-start(bf16[1344,128]{1,0:T(8,128)(2,1)S(1)} %get-tuple-element.72.refs_0_), channel_id=1, source_target_pairs={{0,3},{1,0},{2,1},{3,2},{4,5},{5,6},{6,7},{7,4},{8,11},{9,8},{10,9... | collective-permute-start | bytes 1032200 | tf_op jit(solution)/shard_map/ppermute | solution.py:78
  153.2 15.0 %collective-permute-start.16 = (bf16[192,512]{1,0:T(8,128)(2,1)S(1)}, bf16[192,512]{1,0:T(8,128)(2,1)S(1)}, u32[]{:S(2)}, u32[]{:S(2)}) collective-permute-start(bf16[192,512]{1,0:T(8,128)(2,1)S(1)} %fusion.16), channel_id=1, source_target_pairs={{0,64},{64,128},{128,192},{192,256},{256,320},{320,384},{384,448},... | collective-permute-start | bytes 589832 | tf_op jit(solution)/shard_map/ppermute | solution.py:63
Sparse Core Ops, SparseCore 0:
  11.0 54.2 all-gather.2
  74.8 66.2 reduce-scatter.1
